TPU v7x, 256 devices: a whole 4x4x8 slice. The times are simulated.
256 devices in a mesh: dp: 64 (over y, z, core), tensor: 4 (over x).
Axes of the slice: x: 4, y: 4, z: 8, core: 2. Of those that a mesh axis runs over, the one named last changes fastest.
Arguments:
- old_weight: float32 [64, 4, 2688, 128], P('dp', 'tensor'), may hold values from -6 to 6
- old_first: float32 [64, 4, 2688, 128], P('dp', 'tensor'), may hold values from -6 to 6
- old_second: float32 [64, 4, 2688, 128], P('dp', 'tensor'), may hold values from 0.01 to 1
- gradient: bfloat16 [64, 4, 2688, 128], P('dp', 'tensor'), may hold values from -6 to 6
- old_offsets: int32 [8, 32], replicated, may hold values from 0 to 42336, as said below
- new_offsets: int32 [4, 64], replicated, may hold values from 0 to 85344, as said below
- old_heads: int32 [112], replicated, may hold values from 0 to 111, as said below
- new_heads: int32 [112], replicated, may hold values from 0 to 111, as said below
- step_count: int32 [], replicated, may hold values from 1 to 19
Outputs:
- new_weight: float32 [64, 4, 2688, 128], P('dp', 'tensor')
- new_first: float32 [64, 4, 2688, 128], P('dp', 'tensor')
- new_second: float32 [64, 4, 2688, 128], P('dp', 'tensor')
Inputs may be any that keep to these rules, and one draw needn't show every extreme that they name: `old_offsets`: entry [s, 0] is 0, entries never fall along a row, entry [s, r] lies within 672 of r * 1344; a fragment holds at most 2688 units and in every row one holds exactly that many. `new_offsets`: entry [t, 0] is 0, entries never fall along a row, entry [t, i] lies within 672 of i * 1344; a fragment holds at most 2688 units and in every row one holds exactly that many. `old_heads`: each head once. Each head once; for every t and c, exactly 7 of new_heads[t * 28 : (t + 1) * 28] are among old_heads[c * 28 : (c + 1) * 28].
All inputs are finite; a program needn't handle non-finite values.
Results may differ from a plain program's by a relative error of at most 0.0003.
Values sent between devices are 32-bit elements; how exact they have to be, the bound alone decides.
No kernel may reach another device: no remote copies, remote signals or barrier semaphores. Data moves between devices by JAX's collectives and lax.ppermute only.
A program may use at most 64 MiB of HBM per device.

v0:
```python
import jax
import jax.numpy as jnp
from jax import lax
from jax.sharding import PartitionSpec as P

beta_one = 0.9
beta_two = 0.95
learn_rate = 0.1
weight_decay = 0.1
epsilon = 1e-08


def from_behind(x, axis, by):
    size = lax.axis_size(axis)
    pairs = [(i, i + by) for i in range(size) if 0 <= i + by < size]
    return lax.ppermute(x, axis, pairs)


def partner(block, axis, bit):
    count = lax.axis_size(axis)
    route = []
    for low in range(count):
        high = low | 1 << bit
        if high != low and high < count:
            route += [(low, high), (high, low)]
    return lax.ppermute(block, axis, route)


def neighbour_rims(pieces, shift_by):
    from_lower = from_behind((pieces[0], pieces[1], pieces[2]), "dp", shift_by)
    from_upper = from_behind((pieces[0], pieces[1], pieces[2]), "dp", -shift_by)
    trimmed = 0
    return (from_lower, from_upper, trimmed)


def rearrange(
    own_rows, below_rows, above_rows, first_unit, own_start, own_end, lower_base, out_rows
):
    below_count = below_rows[0].shape[0]
    own_count = own_rows[0].shape[0]
    above_count = above_rows[0].shape[0]
    global_ids = first_unit + jnp.arange(out_rows, dtype=jnp.int32)
    row_index = jnp.where(
        global_ids < own_start,
        jnp.clip(global_ids - lower_base, 0, below_count - 1),
        jnp.where(
            global_ids >= own_end,
            below_count + own_count + jnp.clip(global_ids - own_end, 0, above_count - 1),
            below_count + jnp.clip(global_ids - own_start, 0, own_count - 1),
        ),
    )
    return tuple(
        (
            jnp.take(jnp.concatenate([below_part, own_part, above_part], axis=0), row_index, axis=0)
            for below_part, own_part, above_part in zip(below_rows, own_rows, above_rows)
        )
    )


def shards(
    old_weight,
    old_first,
    old_second,
    gradient,
    old_offsets,
    new_offsets,
    old_heads,
    new_heads,
    step_count,
):
    capacity = old_weight.shape[2]
    block_units = capacity // 2
    half_block = block_units // 2
    head_count = old_heads.shape[0]
    column_count = lax.axis_size("tensor")
    new_count = head_count // column_count
    old_count = head_count // (2 * column_count)
    dp_count = lax.axis_size("dp")
    old_ranks = old_offsets.shape[1]
    dp_index = lax.axis_index("dp")
    column = lax.axis_index("tensor")
    parity = dp_index % 2
    old_rank = dp_index // 2
    old_shard = 2 * column + parity
    old_bounds = jnp.concatenate(
        [
            lax.dynamic_index_in_dim(old_offsets, old_shard, 0, keepdims=False),
            jnp.full((1,), old_ranks * block_units, jnp.int32),
        ]
    )
    own_start = old_bounds[old_rank]
    prev_start = old_bounds[jnp.maximum(old_rank - 1, 0)]
    next_start = old_bounds[old_rank + 1]
    pieces = (old_weight[0, 0], old_first[0, 0], old_second[0, 0])
    from_lower, from_upper, trimmed = neighbour_rims(pieces, 2)
    balanced = rearrange(
        pieces,
        from_lower,
        from_upper,
        old_rank * block_units,
        own_start,
        next_start,
        prev_start,
        block_units,
    )
    halves = tuple((member.reshape(2, block_units // 2, member.shape[1]) for member in balanced))
    kept_half = tuple(
        (lax.dynamic_index_in_dim(member, parity, 0, keepdims=False) for member in halves)
    )
    sent_half = tuple(
        (lax.dynamic_index_in_dim(member, 1 - parity, 0, keepdims=False) for member in halves)
    )
    received = partner((sent_half[0], sent_half[1], sent_half[2]), "dp", 0)
    rows_dev = block_units // (3 * new_count)
    column_block = []
    for own_part, theirs in zip(kept_half, received):
        lower_shard = jnp.where(parity == 0, own_part, theirs)
        upper_shard = jnp.where(parity == 0, theirs, own_part)
        column_block.append(
            jnp.concatenate(
                [
                    lower_shard.reshape(rows_dev, old_count, 3, own_part.shape[1]),
                    upper_shard.reshape(rows_dev, old_count, 3, own_part.shape[1]),
                ],
                axis=1,
            )
        )
    head_ids = jnp.arange(head_count, dtype=jnp.int32)
    gathered = (
        lax.all_gather(column_block[0], "tensor", axis=1, tiled=True),
        lax.all_gather(column_block[1], "tensor", axis=1, tiled=True),
        lax.all_gather(column_block[2], "tensor", axis=1, tiled=True),
    )
    wanted = lax.dynamic_slice_in_dim(new_heads, column * new_count, new_count)
    same_head = old_heads[None, :] == wanted[:, None]
    positions = jnp.sum(jnp.where(same_head, head_ids[None, :], 0), axis=1)
    new_block = tuple(
        (
            jnp.take(member, positions, axis=1).reshape(block_units, member.shape[3])
            for member in gathered
        )
    )
    new_bounds = jnp.concatenate(
        [
            lax.dynamic_index_in_dim(new_offsets, column, 0, keepdims=False),
            jnp.full((1,), dp_count * block_units, jnp.int32),
        ]
    )
    frag_start = new_bounds[dp_index]
    frag_end = new_bounds[dp_index + 1]
    from_lower, from_upper, trimmed = neighbour_rims(new_block, 1)
    block_start = dp_index * block_units
    placed = rearrange(
        new_block,
        from_lower,
        from_upper,
        frag_start,
        block_start,
        block_start + block_units,
        block_start - block_units + trimmed * half_block,
        capacity,
    )
    in_range = (frag_start + jnp.arange(capacity, dtype=jnp.int32) < frag_end)[:, None]
    master, first_slots, second_slots = placed
    grad_float = gradient[0, 0].astype(jnp.float32)
    step_float = step_count.astype(jnp.float32)
    new_first = beta_one * first_slots + (1.0 - beta_one) * grad_float
    new_second = beta_two * second_slots + (1.0 - beta_two) * grad_float * grad_float
    fix_one = 1.0 - jnp.power(jnp.float32(beta_one), step_float)
    fix_two = 1.0 - jnp.power(jnp.float32(beta_two), step_float)
    adam_ratio = new_first / fix_one / (jnp.sqrt(new_second / fix_two) + epsilon)
    new_weight = master - learn_rate * (adam_ratio + weight_decay * master)
    return (
        jnp.where(in_range, new_weight, 0.0)[None, None],
        jnp.where(in_range, new_first, 0.0)[None, None],
        jnp.where(in_range, new_second, 0.0)[None, None],
    )


def solution(mesh):
    return jax.shard_map(
        shards,
        mesh=mesh,
        in_specs=(
            P("dp", "tensor", None, None),
            P("dp", "tensor", None, None),
            P("dp", "tensor", None, None),
            P("dp", "tensor", None, None),
            P(),
            P(),
            P(),
            P(),
            P(),
        ),
        out_specs=(
            P("dp", "tensor", None, None),
            P("dp", "tensor", None, None),
            P("dp", "tensor", None, None),
        ),
        check_vma=False,
    )
```

profile of v0, /device:TPU:8, one launch (start us, length us, event | category | flops | bytes accessed | tf_op | source)
XLA Modules:
  0.0 310.0 jit_solution(632801212742260719)
XLA Ops:
  7.2 3.8 %collective-permute-start.5 = (f32[2688,128]{1,0:T(8,128)}, f32[2688,128]{1,0:T(8,128)S(1)}, u32[]{:S(2)}, u32[]{:S(2)}) collective-permute-start(f32[2688,128]{1,0:T(8,128)} %bitcast.57), channel_id=1, source_target_pairs={{0,8},{4,12},{8,16},{12,20},{16,24},{20,28},{24,32},{28,36},{32,40... | collective-permute-start | bytes 4128776 | tf_op jit(solution)/shard_map/ppermute | solution.py:16
  11.1 5.7 %collective-permute-start.6 = (f32[2688,128]{1,0:T(8,128)}, f32[2688,128]{1,0:T(8,128)}, u32[]{:S(2)}, u32[]{:S(2)}) collective-permute-start(f32[2688,128]{1,0:T(8,128)} %bitcast.58), channel_id=1, source_target_pairs={{8,0},{12,4},{16,8},{20,12},{24,16},{28,20},{32,24},{36,28},{40,32... | collective-permute-start | bytes 4128776 | tf_op jit(solution)/shard_map/ppermute | solution.py:16
  16.8 1.9 collective-permute-start
  18.7 6.0 %collective-permute-start.1 = (f32[2688,128]{1,0:T(8,128)}, f32[2688,128]{1,0:T(8,128)}, u32[]{:S(2)}, u32[]{:S(2)}) collective-permute-start(f32[2688,128]{1,0:T(8,128)} %bitcast.61), channel_id=1, source_target_pairs={{8,0},{12,4},{16,8},{20,12},{24,16},{28,20},{32,24},{36,28},{40,32... | collective-permute-start | bytes 4128776 | tf_op jit(solution)/shard_map/ppermute | solution.py:16
  24.8 1.9 collective-permute-start.10
  26.8 0.6 fusion.10
  27.4 2.0 compare_and_fusion.1
  29.4 2.0 compare_select_fusion.1
  31.4 14.7 %collective-permute-done.5 = f32[2688,128]{1,0:T(8,128)S(1)} collective-permute-done((f32[2688,128]{1,0:T(8,128)}, f32[2688,128]{1,0:T(8,128)S(1)}, u32[]{:S(2)}, u32[]{:S(2)}) %collective-permute-start.5) | collective-permute-done | bytes 1376288 | tf_op jit(solution)/shard_map/ppermute | solution.py:16
  46.1 4.0 %collective-permute-start.11 = (f32[2688,128]{1,0:T(8,128)}, f32[2688,128]{1,0:T(8,128)}, u32[]{:S(2)}, u32[]{:S(2)}) collective-permute-start(f32[2688,128]{1,0:T(8,128)} %bitcast.64), channel_id=1, source_target_pairs={{8,0},{12,4},{16,8},{20,12},{24,16},{28,20},{32,24},{36,28},{40,32... | collective-permute-start | bytes 4128776 | tf_op jit(solution)/shard_map/ppermute | solution.py:16
  50.1 4.0 %pad_maximum_fusion.1 = f32[8064,128]{1,0:T(8,128)} fusion(f32[2688,128]{1,0:T(8,128)} %collective-permute-done.6, f32[2688,128]{1,0:T(8,128)} %bitcast.59, f32[2688,128]{1,0:T(8,128)S(1)} %collective-permute-done.5), kind=kLoop, calls=%fused_computation.10 | loop fusion | flops 2064384 | bytes 8257536 | tf_op jit(solution)/shard_map/concatenate | solution.py:54
  54.0 4.9 %gather_fusion.3 = f32[1344,128]{1,0:T(8,128)S(1)} fusion(f32[8064,128]{1,0:T(8,128)} %pad_maximum_fusion.1, s32[2048]{0:T(1024)S(1)} %pad_clamp_fusion.1), kind=kCustom, calls=%fused_computation.3.clone | custom fusion | bytes 1381632 | tf_op jit(solution)/shard_map/jit(_take)/gather | solution.py:54
  59.0 16.6 %collective-permute-done = f32[2688,128]{1,0:T(8,128)S(1)} collective-permute-done((f32[2688,128]{1,0:T(8,128)}, f32[2688,128]{1,0:T(8,128)S(1)}, u32[]{:S(2)}, u32[]{:S(2)}) %collective-permute-start) | collective-permute-done | bytes 1376288 | tf_op jit(solution)/shard_map/ppermute | solution.py:16
  75.6 1.6 collective-permute-done.1
  77.2 3.5 %pad_maximum_fusion = f32[8064,128]{1,0:T(8,128)} fusion(f32[2688,128]{1,0:T(8,128)} %collective-permute-done.1, f32[2688,128]{1,0:T(8,128)S(1)} %bitcast.62, f32[2688,128]{1,0:T(8,128)S(1)} %collective-permute-done), kind=kLoop, calls=%fused_computation.9 | loop fusion | flops 2064384 | bytes 8257536 | tf_op jit(solution)/shard_map/concatenate | solution.py:54
  80.7 4.9 %gather_fusion = f32[1344,128]{1,0:T(8,128)S(1)} fusion(f32[8064,128]{1,0:T(8,128)} %pad_maximum_fusion, s32[2048]{0:T(1024)S(1)} %pad_clamp_fusion.1), kind=kCustom, calls=%fused_computation.clone | custom fusion | bytes 1381632 | tf_op jit(solution)/shard_map/jit(_take)/gather | solution.py:54
  85.7 18.7 %collective-permute-done.10 = f32[2688,128]{1,0:T(8,128)} collective-permute-done((f32[2688,128]{1,0:T(8,128)}, f32[2688,128]{1,0:T(8,128)}, u32[]{:S(2)}, u32[]{:S(2)}) %collective-permute-start.10) | collective-permute-done | bytes 1376288 | tf_op jit(solution)/shard_map/ppermute | solution.py:16
  104.4 1.2 collective-permute-done.11
  105.5 4.0 %pad_maximum_fusion.2 = f32[8064,128]{1,0:T(8,128)} fusion(f32[2688,128]{1,0:T(8,128)} %collective-permute-done.11, f32[2688,128]{1,0:T(8,128)S(1)} %bitcast.65, f32[2688,128]{1,0:T(8,128)} %collective-permute-done.10), kind=kLoop, calls=%fused_computation.11 | loop fusion | flops 2064384 | bytes 8257536 | tf_op jit(solution)/shard_map/concatenate | solution.py:54
  109.5 4.8 %gather_fusion.6 = f32[1344,128]{1,0:T(8,128)S(1)} fusion(f32[8064,128]{1,0:T(8,128)} %pad_maximum_fusion.2, s32[2048]{0:T(1024)S(1)} %pad_clamp_fusion.1), kind=kCustom, calls=%fused_computation.4.clone | custom fusion | bytes 1381632 | tf_op jit(solution)/shard_map/jit(_take)/gather | solution.py:54
  114.3 0.2 broadcast_select_fusion
  114.6 0.8 copy-done.2
  115.6 1.6 collective-permute-done.2
  117.2 1.0 bitcast_select_fusion.5
  118.5 0.2 pad_maximum_fusion.6
  118.7 1.1 copy.27
  119.9 0.2 collective-permute-start.7
  120.1 1.5 collective-permute-done.7
  122.0 0.2 pad_maximum_fusion.7
  122.2 1.1 copy.29
  123.4 0.2 collective-permute-start.12
  123.6 1.5 collective-permute-done.12
  125.5 0.2 pad_maximum_fusion.8
  125.7 1.1 copy.31
  127.1 32.8 %all-gather.4.cloned.1.call-done = f32[16,112,3,128]{3,0,2,1:T(8,128)} async-done(((f32[16,28,3,128]{3,0,2,1:T(8,128)}), f32[16,112,3,128]{3,0,2,1:T(8,128)}) %all-gather.4.cloned.1.call-update) | async-done | bytes 2752528 | tf_op jit(solution)/shard_map/all_gather | solution.py:130
  159.9 2.4 gather_fusion.1
  162.3 39.0 %all-gather.6.cloned.1.call-done = f32[16,112,3,128]{3,0,2,1:T(8,128)} async-done(((f32[16,28,3,128]{3,0,2,1:T(8,128)}), f32[16,112,3,128]{3,0,2,1:T(8,128)}) %all-gather.6.cloned.1.call-update) | async-done | bytes 2752528 | tf_op jit(solution)/shard_map/all_gather | solution.py:131
  201.3 2.4 gather_fusion.4
  203.6 39.0 %all-gather.8.cloned.1.call-done = f32[16,112,3,128]{3,0,2,1:T(8,128)} async-done(((f32[16,28,3,128]{3,0,2,1:T(8,128)}), f32[16,112,3,128]{3,0,2,1:T(8,128)}) %all-gather.8.cloned.1.call-update) | async-done | bytes 2752528 | tf_op jit(solution)/shard_map/all_gather | solution.py:132
  242.7 2.4 gather_fusion.7
  245.0 0.2 select_bitcast_fusion.3
  245.2 0.4 copy.28
  245.6 0.3 reshape.69
  245.9 1.9 collective-permute-start.3
  247.9 5.8 %collective-permute-start.4 = (f32[1344,128]{1,0:T(8,128)S(1)}, f32[1344,128]{1,0:T(8,128)}, u32[]{:S(2)}, u32[]{:S(2)}) collective-permute-start(f32[1344,128]{1,0:T(8,128)S(1)} %reshape.69), channel_id=1, source_target_pairs={{4,0},{8,4},{12,8},{16,12},{20,16},{24,20},{28,24},{32,28},{36,32}... | collective-permute-start | bytes 2064392 | tf_op jit(solution)/shard_map/ppermute | solution.py:16
  254.4 0.7 fusion.7
  255.1 0.6 fusion.9
  255.8 0.6 compare_select_fusion
  256.4 0.4 copy.30
  256.8 1.2 reshape.73
  258.0 1.9 collective-permute-start.8
  259.9 5.8 %collective-permute-start.9 = (f32[1344,128]{1,0:T(8,128)}, f32[1344,128]{1,0:T(8,128)}, u32[]{:S(2)}, u32[]{:S(2)}) collective-permute-start(f32[1344,128]{1,0:T(8,128)} %reshape.73), channel_id=1, source_target_pairs={{4,0},{8,4},{12,8},{16,12},{20,16},{24,20},{28,24},{32,28},{36,32}... | collective-permute-start | bytes 2064392 | tf_op jit(solution)/shard_map/ppermute | solution.py:16
  265.6 1.3 fusion.4
  266.9 0.4 copy.32
  267.3 1.2 reshape.77
  268.5 1.9 collective-permute-start.13
  270.4 5.8 %collective-permute-start.14 = (f32[1344,128]{1,0:T(8,128)}, f32[1344,128]{1,0:T(8,128)}, u32[]{:S(2)}, u32[]{:S(2)}) collective-permute-start(f32[1344,128]{1,0:T(8,128)} %reshape.77), channel_id=1, source_target_pairs={{4,0},{8,4},{12,8},{16,12},{20,16},{24,20},{28,24},{32,28},{36,32}... | collective-permute-start | bytes 2064392 | tf_op jit(solution)/shard_map/ppermute | solution.py:16
  276.2 1.6 pad_maximum_fusion.3
  277.8 4.8 %gather_fusion.2 = f32[2688,128]{1,0:T(8,128)S(1)} fusion(f32[4032,128]{1,0:T(8,128)S(1)} %pad_maximum_fusion.3, s32[3072]{0:T(1024)S(1)} %pad_clamp_fusion), kind=kCustom, calls=%fused_computation.2.clone | custom fusion | bytes 2763264 | tf_op jit(solution)/shard_map/jit(_take)/gather | solution.py:54
  282.7 1.6 pad_maximum_fusion.4
  284.3 5.9 %gather_fusion.5 = f32[2688,128]{1,0:T(8,128)} fusion(f32[4032,128]{1,0:T(8,128)S(1)} %pad_maximum_fusion.4, s32[3072]{0:T(1024)S(1)} %pad_clamp_fusion), kind=kCustom, calls=%fused_computation.7.clone | custom fusion | bytes 2763264 | tf_op jit(solution)/shard_map/jit(_take)/gather | solution.py:54
  290.3 1.6 pad_maximum_fusion.5
  291.9 5.9 %gather_fusion.8 = f32[2688,128]{1,0:T(8,128)} fusion(f32[4032,128]{1,0:T(8,128)S(1)} %pad_maximum_fusion.5, s32[3072]{0:T(1024)S(1)} %pad_clamp_fusion), kind=kCustom, calls=%fused_computation.8.clone | custom fusion | bytes 2763264 | tf_op jit(solution)/shard_map/jit(_take)/gather | solution.py:54
  297.9 5.6 %select_bitcast_fusion = (f32[1,1,2688,128]{3,2,1,0:T(8,128)}, f32[1,1,2688,128]{3,2,1,0:T(8,128)}, f32[1,1,2688,128]{3,2,1,0:T(8,128)}) fusion(bf16[1,1,2688,128]{3,2,1,0:T(8,128)(2,1)} %param.18, f32[2688,128]{1,0:T(8,128)} %gather_fusion.8, pred[2688]{0:T(1024)(128)(4,1)S(1)} %get-tuple-element.27, pred[2688]{0:T(1024)(128)(4,1)S(1)} %get-tuple-element.26, ...), kind=kLoop, calls=%fused_computation.22 | loop fusion | flops 7569408 | bytes 8951048 | tf_op jit(solution)/shard_map/broadcast_in_dim | solution.py:176
  (50 shorter events, 1.8 us)
Async XLA Ops:
  7.2 19.6 %copy-start = (s32[8,32]{1,0:T(8,128)S(1)}, s32[8,32]{1,0:T(8,128)}, u32[]{:S(2)}) copy-start(s32[8,32]{1,0:T(8,128)} %param.19) | copy-start | bytes 3076
  7.2 152.7 %all-gather.4.cloned.1.call-start = ((), (), s32[]{:S(2)}) async-start(), calls=%async_computation | async-start | bytes 3440640 | tf_op jit(solution)/shard_map/all_gather | solution.py:130
  7.2 38.9 %collective-permute-start.5 = (f32[2688,128]{1,0:T(8,128)}, f32[2688,128]{1,0:T(8,128)S(1)}, u32[]{:S(2)}, u32[]{:S(2)}) collective-permute-start(f32[2688,128]{1,0:T(8,128)} %bitcast.57), channel_id=1, source_target_pairs={{0,8},{4,12},{8,16},{12,20},{16,24},{20,28},{24,32},{28,36},{32,40... | collective-permute-start | bytes 4128776 | tf_op jit(solution)/shard_map/ppermute | solution.py:16
  11.1 39.0 %collective-permute-start.6 = (f32[2688,128]{1,0:T(8,128)}, f32[2688,128]{1,0:T(8,128)}, u32[]{:S(2)}, u32[]{:S(2)}) collective-permute-start(f32[2688,128]{1,0:T(8,128)} %bitcast.58), channel_id=1, source_target_pairs={{8,0},{12,4},{16,8},{20,12},{24,16},{28,20},{32,24},{36,28},{40,32... | collective-permute-start | bytes 4128776 | tf_op jit(solution)/shard_map/ppermute | solution.py:16
  16.8 58.8 %collective-permute-start = (f32[2688,128]{1,0:T(8,128)}, f32[2688,128]{1,0:T(8,128)S(1)}, u32[]{:S(2)}, u32[]{:S(2)}) collective-permute-start(f32[2688,128]{1,0:T(8,128)} %bitcast.60), channel_id=1, source_target_pairs={{0,8},{4,12},{8,16},{12,20},{16,24},{20,28},{24,32},{28,36},{32,40... | collective-permute-start | bytes 4128776 | tf_op jit(solution)/shard_map/ppermute | solution.py:16
  18.7 58.4 %collective-permute-start.1 = (f32[2688,128]{1,0:T(8,128)}, f32[2688,128]{1,0:T(8,128)}, u32[]{:S(2)}, u32[]{:S(2)}) collective-permute-start(f32[2688,128]{1,0:T(8,128)} %bitcast.61), channel_id=1, source_target_pairs={{8,0},{12,4},{16,8},{20,12},{24,16},{28,20},{32,24},{36,28},{40,32... | collective-permute-start | bytes 4128776 | tf_op jit(solution)/shard_map/ppermute | solution.py:16
  24.8 79.6 %collective-permute-start.10 = (f32[2688,128]{1,0:T(8,128)}, f32[2688,128]{1,0:T(8,128)}, u32[]{:S(2)}, u32[]{:S(2)}) collective-permute-start(f32[2688,128]{1,0:T(8,128)} %bitcast.63), channel_id=1, source_target_pairs={{0,8},{4,12},{8,16},{12,20},{16,24},{20,28},{24,32},{28,36},{32,40... | collective-permute-start | bytes 4128776 | tf_op jit(solution)/shard_map/ppermute | solution.py:16
  46.1 59.4 %collective-permute-start.11 = (f32[2688,128]{1,0:T(8,128)}, f32[2688,128]{1,0:T(8,128)}, u32[]{:S(2)}, u32[]{:S(2)}) collective-permute-start(f32[2688,128]{1,0:T(8,128)} %bitcast.64), channel_id=1, source_target_pairs={{8,0},{12,4},{16,8},{20,12},{24,16},{28,20},{32,24},{36,28},{40,32... | collective-permute-start | bytes 4128776 | tf_op jit(solution)/shard_map/ppermute | solution.py:16
  54.0 23.2 %copy-start.4 = (f32[1,1,2688,128]{3,2,1,0:T(8,128)S(1)}, f32[1,1,2688,128]{3,2,1,0:T(8,128)}, u32[]{:S(2)}) copy-start(f32[1,1,2688,128]{3,2,1,0:T(8,128)} %param.15) | copy-start | bytes 4128772
  80.7 24.8 %copy-start.5 = (f32[1,1,2688,128]{3,2,1,0:T(8,128)S(1)}, f32[1,1,2688,128]{3,2,1,0:T(8,128)}, u32[]{:S(2)}) copy-start(f32[1,1,2688,128]{3,2,1,0:T(8,128)} %param.17) | copy-start | bytes 4128772
  114.6 0.8 copy-start.2
  115.4 1.7 collective-permute-start.2
  119.8 81.5 %all-gather.6.cloned.1.call-start = ((), (), s32[]{:S(2)}) async-start(), calls=%async_computation.1 | async-start | bytes 3440640 | tf_op jit(solution)/shard_map/all_gather | solution.py:131
  119.9 1.7 collective-permute-start.7
  123.3 119.4 %all-gather.8.cloned.1.call-start = ((), (), s32[]{:S(2)}) async-start(), calls=%async_computation.2 | async-start | bytes 3440640 | tf_op jit(solution)/shard_map/all_gather | solution.py:132
  123.4 1.7 collective-permute-start.12
  125.7 1.1 copy-start.6
  125.7 1.2 copy-start.7
  245.9 12.0 %copy-start.3 = (f32[1344,128]{1,0:T(8,128)}, f32[1344,128]{1,0:T(8,128)S(1)}, u32[]{:S(2)}) copy-start(f32[1344,128]{1,0:T(8,128)S(1)} %reshape.69) | copy-start | bytes 2064388
  245.9 24.4 %collective-permute-start.3 = (f32[1344,128]{1,0:T(8,128)S(1)}, f32[1344,128]{1,0:T(8,128)}, u32[]{:S(2)}, u32[]{:S(2)}) collective-permute-start(f32[1344,128]{1,0:T(8,128)S(1)} %reshape.69), channel_id=1, source_target_pairs={{0,4},{4,8},{8,12},{12,16},{16,20},{20,24},{24,28},{28,32},{32,36}... | collective-permute-start | bytes 2064392 | tf_op jit(solution)/shard_map/ppermute | solution.py:16
  247.9 28.3 %collective-permute-start.4 = (f32[1344,128]{1,0:T(8,128)S(1)}, f32[1344,128]{1,0:T(8,128)}, u32[]{:S(2)}, u32[]{:S(2)}) collective-permute-start(f32[1344,128]{1,0:T(8,128)S(1)} %reshape.69), channel_id=1, source_target_pairs={{4,0},{8,4},{12,8},{16,12},{20,16},{24,20},{28,24},{32,28},{36,32}... | collective-permute-start | bytes 2064392 | tf_op jit(solution)/shard_map/ppermute | solution.py:16
  258.0 24.7 %collective-permute-start.8 = (f32[1344,128]{1,0:T(8,128)}, f32[1344,128]{1,0:T(8,128)}, u32[]{:S(2)}, u32[]{:S(2)}) collective-permute-start(f32[1344,128]{1,0:T(8,128)} %reshape.73), channel_id=1, source_target_pairs={{0,4},{4,8},{8,12},{12,16},{16,20},{20,24},{24,28},{28,32},{32,36}... | collective-permute-start | bytes 2064392 | tf_op jit(solution)/shard_map/ppermute | solution.py:16
  259.9 22.8 %collective-permute-start.9 = (f32[1344,128]{1,0:T(8,128)}, f32[1344,128]{1,0:T(8,128)}, u32[]{:S(2)}, u32[]{:S(2)}) collective-permute-start(f32[1344,128]{1,0:T(8,128)} %reshape.73), channel_id=1, source_target_pairs={{4,0},{8,4},{12,8},{16,12},{20,16},{24,20},{28,24},{32,28},{36,32}... | collective-permute-start | bytes 2064392 | tf_op jit(solution)/shard_map/ppermute | solution.py:16
  268.5 21.8 %collective-permute-start.13 = (f32[1344,128]{1,0:T(8,128)}, f32[1344,128]{1,0:T(8,128)}, u32[]{:S(2)}, u32[]{:S(2)}) collective-permute-start(f32[1344,128]{1,0:T(8,128)} %reshape.77), channel_id=1, source_target_pairs={{0,4},{4,8},{8,12},{12,16},{16,20},{20,24},{24,28},{28,32},{32,36}... | collective-permute-start | bytes 2064392 | tf_op jit(solution)/shard_map/ppermute | solution.py:16
  270.4 19.9 %collective-permute-start.14 = (f32[1344,128]{1,0:T(8,128)}, f32[1344,128]{1,0:T(8,128)}, u32[]{:S(2)}, u32[]{:S(2)}) collective-permute-start(f32[1344,128]{1,0:T(8,128)} %reshape.77), channel_id=1, source_target_pairs={{4,0},{8,4},{12,8},{16,12},{20,16},{24,20},{28,24},{32,28},{36,32}... | collective-permute-start | bytes 2064392 | tf_op jit(solution)/shard_map/ppermute | solution.py:16
  297.9 5.6 %copy-start.1 = (s32[8,32]{1,0:T(8,128)S(1)}, s32[8,32]{1,0:T(8,128)}, u32[]{:S(2)}) copy-start(s32[8,32]{1,0:T(8,128)} %param.19) | copy-start | bytes 3076
Sparse Core Ops, SparseCore 0:
  119.9 39.8 all-gather.3
  162.3 38.9 all-gather.5
  203.7 38.9 all-gather.7
where the time goes:
time: 311 us; the launch traced here: 310 us
  waiting for transfers between devices  168 us (54%)
  local copies, waits for them, and re-layouts  49.2 us (16%)
  starting transfers between devices  47.1 us (15%)
  other arithmetic  30.4 us (10%)
  between operations  15 us (5%)
    ppermute x12, waiting for transfers between devices, from_behind(): return lax.ppermute(x, axis, pairs)  52.8 us
    ppermute x12, starting transfers between devices, from_behind(): return lax.ppermute(x, axis, pairs)  46.4 us
    all_gather x1, waiting for transfers between devices, shards(): lax.all_gather(column_block[2], 'tensor', axis=1, tiled=True)  39 us
    all_gather x1, waiting for transfers between devices, shards(): lax.all_gather(column_block[1], 'tensor', axis=1, tiled=True)  39 us
    all_gather x1, waiting for transfers between devices, shards(): lax.all_gather(column_block[0], 'tensor', axis=1, tiled=True)  32.8 us
    gather x6, local copies, waits for them, and re-layouts, rearrange(): jnp.take(jnp.concatenate([below_part, own_part, above_part], axis=0), row...  31.3 us
    concatenate x6, other arithmetic, rearrange(): jnp.concatenate([below_part, own_part, above_part], axis=0)  16.4 us
    gather x3, local copies, waits for them, and re-layouts, shards(): jnp.take(member, positions, axis=1).reshape(block_units, member.shape[3])  7.1 us
  transfers between devices with their start and end apart: 18, of which 11 were waited for; matrix products, arithmetic and copies ran while one was open for 16% of the time, Pallas kernels for 0%

commit v1 on v0

v1 whole, which is shorter than its diff:
```python
import functools
import jax
import jax.numpy as jnp
from jax import lax
from jax.experimental import pallas as pl
from jax.experimental.pallas import tpu as pltpu
from jax.sharding import PartitionSpec as P

beta_one = 0.9
beta_two = 0.95
learn_rate = 0.1
weight_decay = 0.1
epsilon = 1e-08

CAP = 2688
BLOCK = 1344
HALF = 672
WIDE = 680
OLD_RANKS = 32
OLD_UNITS = OLD_RANKS * BLOCK
N_DP = 64
NEW_UNITS = N_DP * BLOCK
HEADS = 112
COLUMNS = 4
GROUP = HEADS // COLUMNS
OLD_HEADS = GROUP // 2
PEER = GROUP // COLUMNS
PART = 16 * PEER * 3
LANES = 128
GROUPS = ((0,), (1,), (2,))
E_ROWS = CAP + BLOCK
CHUNK = 336

ANY = pl.BlockSpec(memory_space=pl.ANY)
VMEM = pl.BlockSpec(memory_space=pltpu.VMEM)
SMEM = pl.BlockSpec(memory_space=pltpu.SMEM)


def place():
    dp = lax.axis_index("dp")
    return dp // 2, dp % 2, lax.axis_index("tensor")


def old_start(offsets, shard, rank):
    inside = offsets[shard, jnp.minimum(rank, OLD_RANKS - 1)]
    return jnp.where(rank >= OLD_RANKS, OLD_UNITS, inside)


def aligned(start):
    return pl.multiple_of(jnp.minimum(start // 8 * 8, CAP - WIDE), 8)


def own_half_slot(rank, core, start):
    return jnp.where(
        core == 0,
        jnp.maximum(rank * BLOCK - start, 0),
        rank * BLOCK + HALF - start,
    )


def pack_kernel(count, offsets, *refs):
    sources = refs[:count]
    outs = refs[count : count + 3]
    wide, sems = refs[count + 3 :]
    rank, core, column = place()
    start = offsets[2 * column + core, rank]
    up = (rank + 1) * BLOCK - start
    firsts = (
        jnp.where(core == 0, up, 0),
        jnp.where(core == 0, 0, up),
        jnp.where(
            core == 0,
            rank * BLOCK + HALF - start,
            jnp.maximum(rank * BLOCK - start, 0),
        ),
    )
    copies = []
    for j in range(count):
        for m in range(3):
            copy = pltpu.make_async_copy(
                sources[j].at[pl.ds(aligned(firsts[m]), WIDE)],
                wide.at[j, m],
                sems.at[j, m],
            )
            copy.start()
            copies.append(copy)
    for j in range(count):
        for m in range(3):
            copies[3 * j + m].wait()
            rest = firsts[m] - aligned(firsts[m])
            outs[m][j] = wide[j, m, pl.ds(rest, HALF), :]


def pack(offsets, sources):
    count = len(sources)
    out = jax.ShapeDtypeStruct((count, HALF, LANES), jnp.float32)
    return pl.pallas_call(
        functools.partial(pack_kernel, count),
        out_shape=(out, out, out),
        in_specs=[SMEM] + [ANY] * count,
        out_specs=(VMEM, VMEM, VMEM),
        scratch_shapes=[
            pltpu.VMEM((count, 3, WIDE, LANES), jnp.float32),
            pltpu.SemaphoreType.DMA((count, 3)),
        ],
        cost_estimate=pl.CostEstimate(
            flops=0, bytes_accessed=count * 6 * HALF * LANES * 4, transcendentals=0
        ),
        name="pack",
    )(offsets, *sources)


def tables_kernel(old_heads, new_heads, after, send, recv, where, used):
    column = lax.axis_index("tensor")

    def invert(i, carry):
        where[old_heads[i]] = i
        return carry

    lax.fori_loop(0, HEADS, invert, 0)
    for s in range(COLUMNS):
        target = (column + s) % COLUMNS

        def one(b, found):
            position = where[new_heads[target * GROUP + b]] - column * GROUP
            mine = (position >= 0) & (position < GROUP)
            send[s * 8 + found] = position
            return found + jnp.where(mine, 1, 0)

        lax.fori_loop(0, GROUP, one, jnp.int32(0))
        used[s] = 0

    def slot(b, carry):
        source = where[new_heads[column * GROUP + b]] // GROUP
        shift = (column - source + COLUMNS) % COLUMNS
        found = used[shift]
        recv[shift * 8 + found] = b
        used[shift] = found + 1
        return carry

    lax.fori_loop(0, GROUP, slot, 0)


def tables(old_heads, new_heads, after):
    out = jax.ShapeDtypeStruct((8 * COLUMNS,), jnp.int32)
    return pl.pallas_call(
        tables_kernel,
        out_shape=(out, out),
        in_specs=[SMEM, SMEM, ANY],
        out_specs=(SMEM, SMEM),
        scratch_shapes=[
            pltpu.SMEM((HEADS,), jnp.int32),
            pltpu.SMEM((COLUMNS,), jnp.int32),
        ],
        cost_estimate=pl.CostEstimate(flops=0, bytes_accessed=4_000_000, transcendentals=0),
        name="tables",
    )(old_heads, new_heads, after)


def spread_kernel(count, offsets, send, *refs):
    sources = refs[:count]
    halo, other_halo, swapped = refs[count : count + 3]
    outs = refs[count + 3 : count + 7]
    held, sems = refs[count + 7 :]
    rank, core, column = place()
    shard = 2 * column + core
    start = old_start(offsets, shard, rank)
    slot = own_half_slot(rank, core, start)
    rest = slot - aligned(slot)

    def split(which):
        begin = old_start(offsets, which, rank)
        end = old_start(offsets, which, rank + 1)
        cut = jnp.where(core == 0, begin - rank * BLOCK, end - rank * BLOCK - HALF)
        return jnp.clip(cut, 0, HALF)

    cuts = (split(shard), split(shard + 1 - 2 * core))
    near = pl.multiple_of(jnp.where(core == 0, WIDE, 0), 8)
    far = pl.multiple_of(jnp.where(core == 0, 0, WIDE), 8)
    copies = []
    for j in range(count):
        copies += [
            pltpu.make_async_copy(
                sources[j].at[pl.ds(aligned(slot), WIDE)],
                held.at[j, 0, pl.ds(near, WIDE)],
                sems.at[j, 0],
            ),
            pltpu.make_async_copy(
                halo.at[j], held.at[j, 0, pl.ds(far, HALF)], sems.at[j, 1]
            ),
            pltpu.make_async_copy(
                other_halo.at[j], held.at[j, 1, pl.ds(far, HALF)], sems.at[j, 2]
            ),
            pltpu.make_async_copy(
                swapped.at[j], held.at[j, 1, pl.ds(near, HALF)], sems.at[j, 3]
            ),
        ]
    for copy in copies:
        copy.start()
    for copy in copies:
        copy.wait()
    low_rest = jnp.where(core == 0, 0, rest)
    high_rest = jnp.where(core == 0, rest, 0)
    steps = 42 * lax.broadcasted_iota(jnp.int32, (8, LANES), 0)
    for s in range(COLUMNS):

        def one(q, carry):
            head = send[s * 8 + q]
            side = head // OLD_HEADS
            mine = side == core
            lane = jnp.where(mine, 0, 1)
            unit = 3 * (head - side * OLD_HEADS)
            cut = jnp.where(mine, cuts[0], cuts[1])
            low = unit + jnp.where(mine, low_rest, 0)
            high = WIDE + unit - cut + jnp.where(mine, high_rest, 0)
            for j in range(count):
                for c in range(3):
                    for half in range(2):
                        more = half * 8 * 42 + c
                        first = held[j, lane, pl.ds(low + more, 8, stride=42), :]
                        second = held[j, lane, pl.ds(high + more, 8, stride=42), :]
                        row = pl.multiple_of(q * 48 + c * 16 + half * 8, 8)
                        outs[s][j, pl.ds(row, 8), :] = jnp.where(
                            steps < cut - unit - more, first, second
                        )
            return carry

        lax.fori_loop(0, PEER, one, 0)


def spread(offsets, send, sources, halo, other_halo, swapped):
    count = len(sources)
    out = jax.ShapeDtypeStruct((count, PART, LANES), jnp.float32)
    return pl.pallas_call(
        functools.partial(spread_kernel, count),
        out_shape=(out,) * 4,
        in_specs=[SMEM, SMEM] + [ANY] * (count + 3),
        out_specs=(VMEM,) * 4,
        scratch_shapes=[
            pltpu.VMEM((count, 2, 2 * WIDE, LANES), jnp.float32),
            pltpu.SemaphoreType.DMA((count, 4)),
        ],
        cost_estimate=pl.CostEstimate(
            flops=0, bytes_accessed=count * 6 * HALF * LANES * 4, transcendentals=0
        ),
        name="spread",
    )(offsets, send, *sources, halo, other_halo, swapped)


def collect_kernel(count, recv, *refs):
    parts = refs[:4]
    low, high = refs[4:]
    for s in range(COLUMNS):
        for q in range(PEER):
            b = recv[s * 8 + q]
            for j in range(count):
                for c in range(3):
                    row = q * 48 + c * 16
                    low[j, pl.ds(3 * b + c, 8, stride=84), :] = parts[s][j, row : row + 8, :]
                    high[j, pl.ds(3 * b + c, 8, stride=84), :] = parts[s][j, row + 8 : row + 16, :]


def collect(recv, parts):
    count = parts[0].shape[0]
    out = jax.ShapeDtypeStruct((count, HALF, LANES), jnp.float32)
    return pl.pallas_call(
        functools.partial(collect_kernel, count),
        out_shape=(out, out),
        in_specs=[SMEM] + [VMEM] * 4,
        out_specs=(VMEM, VMEM),
        cost_estimate=pl.CostEstimate(
            flops=0, bytes_accessed=count * 4 * HALF * LANES * 4, transcendentals=0
        ),
        name="collect",
    )(recv, *parts)


def update_kernel(groups, offsets, fixes, *refs):
    pieces = refs[: 4 * len(groups)]
    gradient = refs[4 * len(groups)]
    weight_out, first_out, second_out = refs[4 * len(groups) + 1 : 4 * len(groups) + 4]
    held, sems = refs[4 * len(groups) + 4 :]
    dp = lax.axis_index("dp")
    column = lax.axis_index("tensor")
    start = offsets[column, dp]
    inside = offsets[column, jnp.minimum(dp + 1, N_DP - 1)]
    end = jnp.where(dp == N_DP - 1, NEW_UNITS, inside)
    step = pl.program_id(0)

    @pl.when(step == 0)
    def _():
        copies = []
        for g, members in enumerate(groups):
            for j, which in enumerate(members):
                for k in range(4):
                    copies.append(
                        pltpu.make_async_copy(
                            pieces[4 * g + k].at[j],
                            held.at[which, pl.ds(k * HALF, HALF)],
                            sems.at[which, k],
                        )
                    )
        for copy in copies:
            copy.start()
        for copy in copies:
            copy.wait()

    begin = start - (dp * BLOCK - HALF) + step * CHUNK
    left = end - start - step * CHUNK

    @pl.when(left > 0)
    def _():
        used = lax.broadcasted_iota(jnp.int32, (CHUNK, LANES), 0) < left
        master = held[0, pl.ds(begin, CHUNK), :]
        first_slots = held[1, pl.ds(begin, CHUNK), :]
        second_slots = held[2, pl.ds(begin, CHUNK), :]
        grad = gradient[...].astype(jnp.float32)
        new_first = beta_one * first_slots + (1.0 - beta_one) * grad
        new_second = beta_two * second_slots + (1.0 - beta_two) * grad * grad
        ratio = new_first / fixes[0] / (jnp.sqrt(new_second / fixes[1]) + epsilon)
        new_weight = master - learn_rate * (ratio + weight_decay * master)
        weight_out[...] = jnp.where(used, new_weight, 0.0)
        first_out[...] = jnp.where(used, new_first, 0.0)
        second_out[...] = jnp.where(used, new_second, 0.0)

    @pl.when(left <= 0)
    def _():
        nothing = jnp.zeros((CHUNK, LANES), jnp.float32)
        weight_out[...] = nothing
        first_out[...] = nothing
        second_out[...] = nothing


def update(groups, offsets, fixes, pieces, gradient):
    out = jax.ShapeDtypeStruct((CAP, LANES), jnp.float32)
    block = pl.BlockSpec((CHUNK, LANES), lambda i: (i, 0))
    return pl.pallas_call(
        functools.partial(update_kernel, groups),
        grid=(CAP // CHUNK,),
        out_shape=(out,) * 3,
        in_specs=[SMEM, SMEM] + [ANY] * len(pieces) + [block],
        out_specs=(block,) * 3,
        scratch_shapes=[
            pltpu.VMEM((3, E_ROWS, LANES), jnp.float32),
            pltpu.SemaphoreType.DMA((3, 4)),
        ],
        compiler_params=pltpu.CompilerParams(vmem_limit_bytes=16 * 1024 * 1024),
        cost_estimate=pl.CostEstimate(
            flops=30 * CAP * LANES, bytes_accessed=7 * CAP * LANES * 4, transcendentals=0
        ),
        name="update",
    )(offsets, fixes, *pieces, gradient)


def routes():
    ranks = range(OLD_RANKS)
    above = [r for r in ranks if r + 1 < OLD_RANKS]
    below = [r for r in ranks if r > 0]
    own = [(2 * r, 2 * r + 2) for r in above] + [(2 * r + 1, 2 * r - 1) for r in below]
    other = [(2 * r + 1, 2 * r + 2) for r in above] + [(2 * r, 2 * r - 1) for r in below]
    swap = [(i, i ^ 1) for i in range(N_DP)]
    return own, other, swap


def shards(
    old_weight,
    old_first,
    old_second,
    gradient,
    old_offsets,
    new_offsets,
    old_heads,
    new_heads,
    step_count,
):
    state = (old_weight[0, 0], old_first[0, 0], old_second[0, 0])
    own_route, other_route, swap_route = routes()
    shift = [[(i, (i + s) % COLUMNS) for i in range(COLUMNS)] for s in range(COLUMNS)]
    to_next = [(i, i + 1) for i in range(N_DP - 1)]
    to_last = [(i + 1, i) for i in range(N_DP - 1)]

    moved = []
    send = recv = None
    for members in GROUPS:
        sources = [state[m] for m in members]
        own_part, other_part, swap_part = pack(old_offsets, sources)
        if send is None:
            send, recv = tables(old_heads, new_heads, own_part)
        moved.append(
            (
                sources,
                lax.ppermute(own_part, "dp", own_route),
                lax.ppermute(other_part, "dp", other_route),
                lax.ppermute(swap_part, "dp", swap_route),
            )
        )
    exchanged = []
    for sources, halo, other_halo, swapped in moved:
        parts = spread(old_offsets, send, sources, halo, other_halo, swapped)
        exchanged.append(
            [parts[0]] + [lax.ppermute(parts[s], "tensor", shift[s]) for s in (1, 2, 3)]
        )
    pieces = []
    for parts in exchanged:
        low, high = collect(recv, parts)
        pieces += [
            lax.ppermute(high, "dp", to_next),
            low,
            high,
            lax.ppermute(low, "dp", to_last),
        ]
    step_float = step_count.astype(jnp.float32)
    fixes = jnp.stack(
        [
            1.0 - jnp.power(jnp.float32(beta_one), step_float),
            1.0 - jnp.power(jnp.float32(beta_two), step_float),
        ]
    )
    outs = update(GROUPS, new_offsets, fixes, pieces, gradient[0, 0])
    return tuple(out[None, None] for out in outs)


def solution(mesh):
    spread_out = P("dp", "tensor", None, None)
    return jax.shard_map(
        shards,
        mesh=mesh,
        in_specs=(spread_out,) * 4 + (P(),) * 5,
        out_specs=(spread_out,) * 3,
        check_vma=False,
    )
```

time: 311 us -> 113 us (0.36)
  waiting for transfers between devices: 168 us -> 6.57 us
  local copies, waits for them, and re-layouts: 49.2 us -> 5.55 us
  Pallas kernels: 0 us -> 36.8 us
  other arithmetic: 30.4 us -> 0.08 us
  starting transfers between devices: 47.1 us -> 61.5 us
  between operations: 15 us -> 1.78 us
    all_gather x3 -> x0, waiting for transfers between devices: 111 us -> none  [the longest x1 39 us: shards(): lax.all_gather(column_block[2], 'tensor', axis=1, tiled=True)]
    ppermute x15 -> x24, waiting for transfers between devices: 57.5 us -> 6.57 us  [the longest x3 2.38 us: shards(): lax.ppermute(high, 'dp', to_next)]
    gather x9 -> x0, local copies, waits for them, and re-layouts: 38.4 us -> none  [the longest x6 31.3 us: rearrange(): jnp.take(jnp.concatenate([below_part, own_part, above_part], axis=0), row...]
    pallas_call x0 -> x11, Pallas kernels: none -> 36.8 us  [the longest x3 11 us: spread(): pl.pallas_call(functools.partial(spread_kernel, count), out_shape=(out,)...]
    concatenate x11 -> x0, other arithmetic: 17.2 us -> none  [the longest x6 16.4 us: rearrange(): jnp.concatenate([below_part, own_part, above_part], axis=0)]
    ppermute x15 -> x24, starting transfers between devices: 46.9 us -> 61.5 us  [the longest x9 16.5 us: shards(): lax.ppermute(parts[s], 'tensor', shift[s])]
    broadcast_in_dim x1 -> x0, other arithmetic: 5.58 us -> none  [shards(): jnp.where(in_range, new_second, 0.0)[None, None]]
    unnamed x16 -> x52, local copies, waits for them, and re-layouts: 0.88 us -> 5.55 us
  transfers between devices with their start and end apart: 18 -> 24, of which waited for: 11 -> 5; matrix products, arithmetic and copies ran while one was open for 16% -> 0% of each run, Pallas kernels for 0% -> 25%
where the time goes in v1:
time: 113 us; the launch traced here: 112 us
  starting transfers between devices  61.5 us (54%)
  Pallas kernels  36.8 us (33%)
  waiting for transfers between devices  6.57 us (6%)
  local copies, waits for them, and re-layouts  5.55 us (5%)
  between operations  1.78 us (2%)
    ppermute x9, starting transfers between devices, shards(): lax.ppermute(parts[s], 'tensor', shift[s])  16.5 us
    ppermute x3, starting transfers between devices, shards(): lax.ppermute(low, 'dp', to_last)  16.1 us
    ppermute x3, starting transfers between devices, shards(): lax.ppermute(other_part, 'dp', other_route)  13.8 us
    pallas_call x3, Pallas kernels, spread(): pl.pallas_call(functools.partial(spread_kernel, count), out_shape=(out,)...  11 us
    pallas_call x3, Pallas kernels, pack(): pl.pallas_call(functools.partial(pack_kernel, count), out_shape=(out, out...  8.82 us
    ppermute x3, starting transfers between devices, shards(): lax.ppermute(own_part, 'dp', own_route)  7.36 us
    pallas_call x3, Pallas kernels, collect(): pl.pallas_call(functools.partial(collect_kernel, count), out_shape=(out,...  6.23 us
    pallas_call x1, Pallas kernels, update(): pl.pallas_call(functools.partial(update_kernel, groups), grid=(CAP // CHU...  6.16 us
  transfers between devices with their start and end apart: 24, of which 5 were waited for; matrix products, arithmetic and copies ran while one was open for 0% of the time, Pallas kernels for 25%

profile of v1, /device:TPU:8, one launch (start us, length us, event | category | flops | bytes accessed | tf_op | source)
XLA Modules:
  0.0 112.3 jit_solution(5671036935996304287)
XLA Ops:
  0.6 2.9 %pack.3 = (f32[1,672,128]{2,1,0:T(8,128)}, f32[1,672,128]{2,1,0:T(8,128)}, f32[1,672,128]{2,1,0:T(8,128)}) custom-call(s32[8,32]{1,0:T(8,128)} %offsets.12, f32[2688,128]{1,0:T(8,128)} %bitcast.10), custom_call_target="tpu_custom_call" | custom-call | bytes 2064384 | tf_op jit(solution)/shard_map/pack/pallas_call | solution.py:97
  3.6 7.2 %collective-permute-start.1 = (f32[1,672,128]{2,1,0:T(8,128)}, f32[1,672,128]{2,1,0:T(8,128)S(1)}, u32[]{:S(2)}, u32[]{:S(2)}) collective-permute-start(f32[1,672,128]{2,1,0:T(8,128)} %get-tuple-element.38), channel_id=1, source_target_pairs={{4,8},{12,16},{20,24},{28,32},{36,40},{44,48},{52,56},{60,64},{68,... | collective-permute-start | bytes 1032200 | tf_op jit(solution)/shard_map/ppermute | solution.py:393
  10.8 0.1 collective-permute-start.2
  10.9 1.9 %collective-permute-start = (f32[1,672,128]{2,1,0:T(8,128)}, f32[1,672,128]{2,1,0:T(8,128)S(1)}, u32[]{:S(2)}, u32[]{:S(2)}) collective-permute-start(f32[1,672,128]{2,1,0:T(8,128)} %get-tuple-element.35.after), channel_id=1, source_target_pairs={{0,8},{8,16},{16,24},{24,32},{32,40},{40,48},{48,56},{56,64},{64,7... | collective-permute-start | bytes 1032200 | tf_op jit(solution)/shard_map/ppermute | solution.py:392
  12.8 2.9 %pack.4 = (f32[1,672,128]{2,1,0:T(8,128)}, f32[1,672,128]{2,1,0:T(8,128)}, f32[1,672,128]{2,1,0:T(8,128)}) custom-call(s32[8,32]{1,0:T(8,128)} %offsets.12, f32[2688,128]{1,0:T(8,128)} %bitcast.12), custom_call_target="tpu_custom_call" | custom-call | bytes 2064384 | tf_op jit(solution)/shard_map/pack/pallas_call | solution.py:97
  15.8 2.4 %collective-permute-start.8 = (f32[1,672,128]{2,1,0:T(8,128)}, f32[1,672,128]{2,1,0:T(8,128)S(1)}, u32[]{:S(2)}, u32[]{:S(2)}) collective-permute-start(f32[1,672,128]{2,1,0:T(8,128)} %get-tuple-element.46), channel_id=1, source_target_pairs={{0,8},{8,16},{16,24},{24,32},{32,40},{40,48},{48,56},{56,64},{64,7... | collective-permute-start | bytes 1032200 | tf_op jit(solution)/shard_map/ppermute | solution.py:392
  18.2 4.0 %collective-permute-start.9 = (f32[1,672,128]{2,1,0:T(8,128)}, f32[1,672,128]{2,1,0:T(8,128)S(1)}, u32[]{:S(2)}, u32[]{:S(2)}) collective-permute-start(f32[1,672,128]{2,1,0:T(8,128)} %get-tuple-element.47), channel_id=1, source_target_pairs={{4,8},{12,16},{20,24},{28,32},{36,40},{44,48},{52,56},{60,64},{68,... | collective-permute-start | bytes 1032200 | tf_op jit(solution)/shard_map/ppermute | solution.py:393
  22.2 0.0 collective-permute-done.1.refs_2_
  22.2 0.0 copy-start.14
  22.2 1.3 %collective-permute-start.10 = (f32[1,672,128]{2,1,0:T(8,128)}, f32[1,672,128]{2,1,0:T(8,128)S(1)}, u32[]{:S(2)}, u32[]{:S(2)}) collective-permute-start(f32[1,672,128]{2,1,0:T(8,128)} %get-tuple-element.48), channel_id=1, source_target_pairs={{0,4},{4,0},{8,12},{12,8},{16,20},{20,16},{24,28},{28,24},{32,36},... | collective-permute-start | bytes 1032200 | tf_op jit(solution)/shard_map/ppermute | solution.py:394
  23.6 4.6 %tables.1 = (s32[32]{0:T(128)}, s32[32]{0:T(128)}) custom-call(s32[112]{0:T(128)} %old_heads.1, s32[112]{0:T(128)} %new_heads.1, f32[1,672,128]{2,1,0:T(8,128)} %get-tuple-element.35.after), custom_call_target="tpu_custom_call" | custom-call | bytes 4000000 | tf_op jit(solution)/shard_map/tables/pallas_call | solution.py:146
  28.2 0.0 copy-start.15
  28.2 0.0 collective-permute-done.refs_1_
  28.2 0.0 copy-start.16
  28.2 0.7 copy-done.15
  28.9 0.1 copy-done.16
  29.1 3.7 %spread.3 = (f32[1,336,128]{2,1,0:T(8,128)}, f32[1,336,128]{2,1,0:T(8,128)}, f32[1,336,128]{2,1,0:T(8,128)}, f32[1,336,128]{2,1,0:T(8,128)}) custom-call(s32[8,32]{1,0:T(8,128)} %offsets.12, s32[32]{0:T(128)} %get-tuple-element.37.send, f32[2688,128]{1,0:T(8,128)} %bitcast.11, f32[1,672,128]{2,1,0:T(8,128)} %copy-done.16, f32[1,672,128]{2,1,0:T(8,128)} %copy-done.14, ...), custom_call_target="tpu_custom_call" | custom-call | bytes 2064384 | tf_op jit(solution)/shard_map/spread/pallas_call | solution.py:234
  32.7 1.5 %collective-permute-start.3 = (f32[1,336,128]{2,1,0:T(8,128)}, f32[1,336,128]{2,1,0:T(8,128)S(1)}, u32[]{:S(2)}, u32[]{:S(2)}) collective-permute-start(f32[1,336,128]{2,1,0:T(8,128)} %get-tuple-element.41), channel_id=1, source_target_pairs={{0,1},{1,2},{2,3},{3,0},{4,5},{5,6},{6,7},{7,4},{8,9},{9,10},{10,1... | collective-permute-start | bytes 516104 | tf_op jit(solution)/shard_map/ppermute | solution.py:401
  34.2 3.0 %pack.5 = (f32[1,672,128]{2,1,0:T(8,128)}, f32[1,672,128]{2,1,0:T(8,128)}, f32[1,672,128]{2,1,0:T(8,128)}) custom-call(s32[8,32]{1,0:T(8,128)} %offsets.12, f32[2688,128]{1,0:T(8,128)} %bitcast.14), custom_call_target="tpu_custom_call" | custom-call | bytes 2064384 | tf_op jit(solution)/shard_map/pack/pallas_call | solution.py:97
  37.2 3.0 %collective-permute-start.16 = (f32[1,672,128]{2,1,0:T(8,128)}, f32[1,672,128]{2,1,0:T(8,128)S(1)}, u32[]{:S(2)}, u32[]{:S(2)}) collective-permute-start(f32[1,672,128]{2,1,0:T(8,128)} %get-tuple-element.55), channel_id=1, source_target_pairs={{0,8},{8,16},{16,24},{24,32},{32,40},{40,48},{48,56},{56,64},{64,7... | collective-permute-start | bytes 1032200 | tf_op jit(solution)/shard_map/ppermute | solution.py:392
  40.2 0.0 collective-permute-done.8.refs_1_
  40.2 0.0 copy-start.10
  40.2 2.6 %collective-permute-start.17 = (f32[1,672,128]{2,1,0:T(8,128)}, f32[1,672,128]{2,1,0:T(8,128)S(1)}, u32[]{:S(2)}, u32[]{:S(2)}) collective-permute-start(f32[1,672,128]{2,1,0:T(8,128)} %get-tuple-element.56), channel_id=1, source_target_pairs={{4,8},{12,16},{20,24},{28,32},{36,40},{44,48},{52,56},{60,64},{68,... | collective-permute-start | bytes 1032200 | tf_op jit(solution)/shard_map/ppermute | solution.py:393
  42.9 0.0 collective-permute-done.9.refs_2_
  42.9 0.0 copy-start.11
  42.9 0.4 collective-permute-start.18
  43.3 0.0 collective-permute-done.10.refs_3_
  43.3 2.9 %collective-permute-start.4 = (f32[1,336,128]{2,1,0:T(8,128)S(1)}, f32[1,336,128]{2,1,0:T(8,128)S(1)}, u32[]{:S(2)}, u32[]{:S(2)}) collective-permute-start(f32[1,336,128]{2,1,0:T(8,128)S(1)} %copy-done.25), channel_id=1, source_target_pairs={{0,2},{1,3},{2,0},{3,1},{4,6},{5,7},{6,4},{7,5},{8,10},{9,11},{10,... | collective-permute-start | bytes 516104 | tf_op jit(solution)/shard_map/ppermute | solution.py:401
  46.2 1.4 %collective-permute-start.5 = (f32[1,336,128]{2,1,0:T(8,128)S(1)}, f32[1,336,128]{2,1,0:T(8,128)S(1)}, u32[]{:S(2)}, u32[]{:S(2)}) collective-permute-start(f32[1,336,128]{2,1,0:T(8,128)S(1)} %copy-done.24), channel_id=1, source_target_pairs={{0,3},{1,0},{2,1},{3,2},{4,7},{5,4},{6,5},{7,6},{8,11},{9,8},{10,9... | collective-permute-start | bytes 516104 | tf_op jit(solution)/shard_map/ppermute | solution.py:401
  47.6 3.6 %spread.4 = (f32[1,336,128]{2,1,0:T(8,128)}, f32[1,336,128]{2,1,0:T(8,128)}, f32[1,336,128]{2,1,0:T(8,128)}, f32[1,336,128]{2,1,0:T(8,128)}) custom-call(s32[8,32]{1,0:T(8,128)} %offsets.12, s32[32]{0:T(128)} %get-tuple-element.37.send, f32[2688,128]{1,0:T(8,128)} %bitcast.13, f32[1,672,128]{2,1,0:T(8,128)} %copy-done.10, f32[1,672,128]{2,1,0:T(8,128)} %copy-done.11, ...), custom_call_target="tpu_custom_call" | custom-call | bytes 2064384 | tf_op jit(solution)/shard_map/spread/pallas_call | solution.py:234
  51.3 0.1 collective-permute-done.4.refs_2_
  51.4 2.3 %collective-permute-start.11 = (f32[1,336,128]{2,1,0:T(8,128)}, f32[1,336,128]{2,1,0:T(8,128)S(1)}, u32[]{:S(2)}, u32[]{:S(2)}) collective-permute-start(f32[1,336,128]{2,1,0:T(8,128)} %get-tuple-element.50), channel_id=1, source_target_pairs={{0,1},{1,2},{2,3},{3,0},{4,5},{5,6},{6,7},{7,4},{8,9},{9,10},{10,1... | collective-permute-start | bytes 516104 | tf_op jit(solution)/shard_map/ppermute | solution.py:401
  53.6 0.6 collective-permute-done.5.refs_3_
  54.2 3.0 %collective-permute-start.12 = (f32[1,336,128]{2,1,0:T(8,128)}, f32[1,336,128]{2,1,0:T(8,128)S(1)}, u32[]{:S(2)}, u32[]{:S(2)}) collective-permute-start(f32[1,336,128]{2,1,0:T(8,128)} %get-tuple-element.51), channel_id=1, source_target_pairs={{0,2},{1,3},{2,0},{3,1},{4,6},{5,7},{6,4},{7,5},{8,10},{9,11},{10,... | collective-permute-start | bytes 516104 | tf_op jit(solution)/shard_map/ppermute | solution.py:401
  57.2 2.1 %collect.3 = (f32[1,672,128]{2,1,0:T(8,128)}, f32[1,672,128]{2,1,0:T(8,128)}) custom-call(s32[32]{0:T(128)} %get-tuple-element.36.recv, f32[1,336,128]{2,1,0:T(8,128)} %get-tuple-element.40.refs_0_, f32[1,336,128]{2,1,0:T(8,128)} %copy-done.19, f32[1,336,128]{2,1,0:T(8,128)} %copy-done.22, f32[1,336,128]{2,1,0:T(8,128)} %copy-done.23), custom_call_target="tpu_custom_call" | custom-call | bytes 1376256 | tf_op jit(solution)/shard_map/collect/pallas_call | solution.py:266
  59.3 2.1 %collective-permute-start.6 = (f32[1,672,128]{2,1,0:T(8,128)}, f32[1,672,128]{2,1,0:T(8,128)S(1)}, u32[]{:S(2)}, u32[]{:S(2)}) collective-permute-start(f32[1,672,128]{2,1,0:T(8,128)} %get-tuple-element.44.refs_2_), channel_id=1, source_target_pairs={{0,4},{4,8},{8,12},{12,16},{16,20},{20,24},{24,28},{28,32},{32,36}... | collective-permute-start | bytes 1032200 | tf_op jit(solution)/shard_map/ppermute | solution.py:407
  61.4 0.0 copy-start
  61.4 0.0 copy-start.2
  61.4 0.0 copy-start.7
  61.4 1.6 %collective-permute-start.13 = (f32[1,336,128]{2,1,0:T(8,128)}, f32[1,336,128]{2,1,0:T(8,128)}, u32[]{:S(2)}, u32[]{:S(2)}) collective-permute-start(f32[1,336,128]{2,1,0:T(8,128)} %get-tuple-element.52), channel_id=1, source_target_pairs={{0,3},{1,0},{2,1},{3,2},{4,7},{5,4},{6,5},{7,6},{8,11},{9,8},{10,9... | collective-permute-start | bytes 516104 | tf_op jit(solution)/shard_map/ppermute | solution.py:401
  63.0 0.7 copy-done.12
  63.8 3.7 %spread.5 = (f32[1,336,128]{2,1,0:T(8,128)}, f32[1,336,128]{2,1,0:T(8,128)}, f32[1,336,128]{2,1,0:T(8,128)}, f32[1,336,128]{2,1,0:T(8,128)}) custom-call(s32[8,32]{1,0:T(8,128)} %offsets.12, s32[32]{0:T(128)} %get-tuple-element.37.send, f32[2688,128]{1,0:T(8,128)} %bitcast.15, f32[1,672,128]{2,1,0:T(8,128)} %copy-done.8, f32[1,672,128]{2,1,0:T(8,128)} %copy-done.9, ...), custom_call_target="tpu_custom_call" | custom-call | bytes 2064384 | tf_op jit(solution)/shard_map/spread/pallas_call | solution.py:234
  67.5 0.6 collective-permute-start.19
  68.1 1.5 %collective-permute-start.20 = (f32[1,336,128]{2,1,0:T(8,128)}, f32[1,336,128]{2,1,0:T(8,128)S(1)}, u32[]{:S(2)}, u32[]{:S(2)}) collective-permute-start(f32[1,336,128]{2,1,0:T(8,128)} %get-tuple-element.60), channel_id=1, source_target_pairs={{0,2},{1,3},{2,0},{3,1},{4,6},{5,7},{6,4},{7,5},{8,10},{9,11},{10,... | collective-permute-start | bytes 516104 | tf_op jit(solution)/shard_map/ppermute | solution.py:401
  69.6 0.0 collective-permute-done.12.refs_2_
  69.6 1.7 %collective-permute-start.21 = (f32[1,336,128]{2,1,0:T(8,128)}, f32[1,336,128]{2,1,0:T(8,128)}, u32[]{:S(2)}, u32[]{:S(2)}) collective-permute-start(f32[1,336,128]{2,1,0:T(8,128)} %get-tuple-element.61), channel_id=1, source_target_pairs={{0,3},{1,0},{2,1},{3,2},{4,7},{5,4},{6,5},{7,6},{8,11},{9,8},{10,9... | collective-permute-start | bytes 516104 | tf_op jit(solution)/shard_map/ppermute | solution.py:401
  71.3 0.0 collective-permute-done.13.refs_3_
  71.3 4.6 %collective-permute-start.7 = (f32[1,672,128]{2,1,0:T(8,128)S(1)}, f32[1,672,128]{2,1,0:T(8,128)S(1)}, u32[]{:S(2)}, u32[]{:S(2)}) collective-permute-start(f32[1,672,128]{2,1,0:T(8,128)S(1)} %copy-done.1), channel_id=1, source_target_pairs={{4,0},{8,4},{12,8},{16,12},{20,16},{24,20},{28,24},{32,28},{36,32}... | collective-permute-start | bytes 1032200 | tf_op jit(solution)/shard_map/ppermute | solution.py:410
  75.9 2.1 %collect.4 = (f32[1,672,128]{2,1,0:T(8,128)}, f32[1,672,128]{2,1,0:T(8,128)}) custom-call(s32[32]{0:T(128)} %get-tuple-element.36.recv, f32[1,336,128]{2,1,0:T(8,128)} %get-tuple-element.49.refs_0_, f32[1,336,128]{2,1,0:T(8,128)} %copy-done.17, f32[1,336,128]{2,1,0:T(8,128)} %copy-done.18, f32[1,336,128]{2,1,0:T(8,128)} %collective-permute-done.13.refs_3_), custom_call_target="tpu_custom_call" | custom-call | bytes 1376256 | tf_op jit(solution)/shard_map/collect/pallas_call | solution.py:266
  78.0 1.6 %collective-permute-done.19.refs_1_ = f32[1,336,128]{2,1,0:T(8,128)S(1)} collective-permute-done((f32[1,336,128]{2,1,0:T(8,128)}, f32[1,336,128]{2,1,0:T(8,128)S(1)}, u32[]{:S(2)}, u32[]{:S(2)}) %collective-permute-start.19) | collective-permute-done | bytes 172064 | tf_op jit(solution)/shard_map/ppermute | solution.py:401
  79.6 1.9 %collective-permute-start.14 = (f32[1,672,128]{2,1,0:T(8,128)}, f32[1,672,128]{2,1,0:T(8,128)S(1)}, u32[]{:S(2)}, u32[]{:S(2)}) collective-permute-start(f32[1,672,128]{2,1,0:T(8,128)} %get-tuple-element.53.refs_6_), channel_id=1, source_target_pairs={{0,4},{4,8},{8,12},{12,16},{16,20},{20,24},{24,28},{28,32},{32,36}... | collective-permute-start | bytes 1032200 | tf_op jit(solution)/shard_map/ppermute | solution.py:407
  81.5 0.0 collective-permute-done.20.refs_2_
  81.6 5.8 %collective-permute-start.15 = (f32[1,672,128]{2,1,0:T(8,128)}, f32[1,672,128]{2,1,0:T(8,128)S(1)}, u32[]{:S(2)}, u32[]{:S(2)}) collective-permute-start(f32[1,672,128]{2,1,0:T(8,128)} %get-tuple-element.54.refs_5_), channel_id=1, source_target_pairs={{4,0},{8,4},{12,8},{16,12},{20,16},{24,20},{28,24},{32,28},{36,32}... | collective-permute-start | bytes 1032200 | tf_op jit(solution)/shard_map/ppermute | solution.py:410
  87.4 2.1 %collect.5 = (f32[1,672,128]{2,1,0:T(8,128)}, f32[1,672,128]{2,1,0:T(8,128)}) custom-call(s32[32]{0:T(128)} %get-tuple-element.36.recv, f32[1,336,128]{2,1,0:T(8,128)} %get-tuple-element.58.refs_0_, f32[1,336,128]{2,1,0:T(8,128)} %copy-done.20, f32[1,336,128]{2,1,0:T(8,128)} %copy-done.21, f32[1,336,128]{2,1,0:T(8,128)} %collective-permute-done.21.refs_3_), custom_call_target="tpu_custom_call" | custom-call | bytes 1376256 | tf_op jit(solution)/shard_map/collect/pallas_call | solution.py:266
  89.4 1.9 %collective-permute-start.22 = (f32[1,672,128]{2,1,0:T(8,128)}, f32[1,672,128]{2,1,0:T(8,128)S(1)}, u32[]{:S(2)}, u32[]{:S(2)}) collective-permute-start(f32[1,672,128]{2,1,0:T(8,128)} %get-tuple-element.62.refs_10_), channel_id=1, source_target_pairs={{0,4},{4,8},{8,12},{12,16},{16,20},{20,24},{24,28},{28,32},{32,36}... | collective-permute-start | bytes 1032200 | tf_op jit(solution)/shard_map/ppermute | solution.py:407
  91.4 5.8 %collective-permute-start.23 = (f32[1,672,128]{2,1,0:T(8,128)}, f32[1,672,128]{2,1,0:T(8,128)S(1)}, u32[]{:S(2)}, u32[]{:S(2)}) collective-permute-start(f32[1,672,128]{2,1,0:T(8,128)} %get-tuple-element.63.refs_9_), channel_id=1, source_target_pairs={{4,0},{8,4},{12,8},{16,12},{20,16},{24,20},{28,24},{32,28},{36,32}... | collective-permute-start | bytes 1032200 | tf_op jit(solution)/shard_map/ppermute | solution.py:410
  97.9 0.1 pad_maximum_fusion.fixes
  97.9 2.4 %collective-permute-done.22.refs_8_ = f32[1,672,128]{2,1,0:T(8,128)S(1)} collective-permute-done((f32[1,672,128]{2,1,0:T(8,128)}, f32[1,672,128]{2,1,0:T(8,128)S(1)}, u32[]{:S(2)}, u32[]{:S(2)}) %collective-permute-start.22) | collective-permute-done | bytes 344096 | tf_op jit(solution)/shard_map/ppermute | solution.py:407
  100.3 1.9 %collective-permute-done.23.refs_11_ = f32[1,672,128]{2,1,0:T(8,128)S(1)} collective-permute-done((f32[1,672,128]{2,1,0:T(8,128)}, f32[1,672,128]{2,1,0:T(8,128)S(1)}, u32[]{:S(2)}, u32[]{:S(2)}) %collective-permute-start.23) | collective-permute-done | bytes 344096 | tf_op jit(solution)/shard_map/ppermute | solution.py:410
  102.2 1.0 copy-done.3
  103.2 1.0 copy-done.4
  104.2 1.0 copy-done.5
  105.1 1.0 copy-done.6
  106.1 6.2 %update.1 = (f32[2688,128]{1,0:T(8,128)}, f32[2688,128]{1,0:T(8,128)}, f32[2688,128]{1,0:T(8,128)}) custom-call(s32[4,64]{1,0:T(4,128)S(1)} %copy-done.7, f32[2]{0:T(128)S(1)} %pad_maximum_fusion.fixes, f32[1,672,128]{2,1,0:T(8,128)S(1)} %collective-permute-done.6.refs_0_, f32[1,672,128]{2,1,0:T(8,128)S(1)} %copy-done.1, f32[1,672,128]{2,1,0:T(8,128)S(1)} %copy-done.2, ...), custom_call_target="tpu_custom_call" | custom-call | flops 10321920 | bytes 9633792 | tf_op jit(solution)/shard_map/update/pallas_call | solution.py:337
  (48 shorter events, 0.1 us)
Async XLA Ops:
  3.6 18.6 %collective-permute-start.1 = (f32[1,672,128]{2,1,0:T(8,128)}, f32[1,672,128]{2,1,0:T(8,128)S(1)}, u32[]{:S(2)}, u32[]{:S(2)}) collective-permute-start(f32[1,672,128]{2,1,0:T(8,128)} %get-tuple-element.38), channel_id=1, source_target_pairs={{4,8},{12,16},{20,24},{28,32},{36,40},{44,48},{52,56},{60,64},{68,... | collective-permute-start | bytes 1032200 | tf_op jit(solution)/shard_map/ppermute | solution.py:393
  10.8 17.4 %collective-permute-start.2 = (f32[1,672,128]{2,1,0:T(8,128)}, f32[1,672,128]{2,1,0:T(8,128)S(1)}, u32[]{:S(2)}, u32[]{:S(2)}) collective-permute-start(f32[1,672,128]{2,1,0:T(8,128)} %get-tuple-element.39), channel_id=1, source_target_pairs={{0,4},{4,0},{8,12},{12,8},{16,20},{20,16},{24,28},{28,24},{32,36},... | collective-permute-start | bytes 1032200 | tf_op jit(solution)/shard_map/ppermute | solution.py:394
  10.9 17.3 %collective-permute-start = (f32[1,672,128]{2,1,0:T(8,128)}, f32[1,672,128]{2,1,0:T(8,128)S(1)}, u32[]{:S(2)}, u32[]{:S(2)}) collective-permute-start(f32[1,672,128]{2,1,0:T(8,128)} %get-tuple-element.35.after), channel_id=1, source_target_pairs={{0,8},{8,16},{16,24},{24,32},{32,40},{40,48},{48,56},{56,64},{64,7... | collective-permute-start | bytes 1032200 | tf_op jit(solution)/shard_map/ppermute | solution.py:392
  15.8 24.4 %collective-permute-start.8 = (f32[1,672,128]{2,1,0:T(8,128)}, f32[1,672,128]{2,1,0:T(8,128)S(1)}, u32[]{:S(2)}, u32[]{:S(2)}) collective-permute-start(f32[1,672,128]{2,1,0:T(8,128)} %get-tuple-element.46), channel_id=1, source_target_pairs={{0,8},{8,16},{16,24},{24,32},{32,40},{40,48},{48,56},{56,64},{64,7... | collective-permute-start | bytes 1032200 | tf_op jit(solution)/shard_map/ppermute | solution.py:392
  18.2 24.7 %collective-permute-start.9 = (f32[1,672,128]{2,1,0:T(8,128)}, f32[1,672,128]{2,1,0:T(8,128)S(1)}, u32[]{:S(2)}, u32[]{:S(2)}) collective-permute-start(f32[1,672,128]{2,1,0:T(8,128)} %get-tuple-element.47), channel_id=1, source_target_pairs={{4,8},{12,16},{20,24},{28,32},{36,40},{44,48},{52,56},{60,64},{68,... | collective-permute-start | bytes 1032200 | tf_op jit(solution)/shard_map/ppermute | solution.py:393
  22.2 6.0 %copy-start.14 = (f32[1,672,128]{2,1,0:T(8,128)}, f32[1,672,128]{2,1,0:T(8,128)S(1)}, u32[]{:S(2)}) copy-start(f32[1,672,128]{2,1,0:T(8,128)S(1)} %collective-permute-done.1.refs_2_) | copy-start | bytes 1032196
  22.2 21.1 %collective-permute-start.10 = (f32[1,672,128]{2,1,0:T(8,128)}, f32[1,672,128]{2,1,0:T(8,128)S(1)}, u32[]{:S(2)}, u32[]{:S(2)}) collective-permute-start(f32[1,672,128]{2,1,0:T(8,128)} %get-tuple-element.48), channel_id=1, source_target_pairs={{0,4},{4,0},{8,12},{12,8},{16,20},{20,16},{24,28},{28,24},{32,36},... | collective-permute-start | bytes 1032200 | tf_op jit(solution)/shard_map/ppermute | solution.py:394
  28.2 0.7 copy-start.15
  28.2 0.8 copy-start.16
  32.7 10.6 %copy-start.25 = (f32[1,336,128]{2,1,0:T(8,128)S(1)}, f32[1,336,128]{2,1,0:T(8,128)}, u32[]{:S(2)}) copy-start(f32[1,336,128]{2,1,0:T(8,128)} %get-tuple-element.42) | copy-start | bytes 516100
  32.7 13.5 %copy-start.24 = (f32[1,336,128]{2,1,0:T(8,128)S(1)}, f32[1,336,128]{2,1,0:T(8,128)}, u32[]{:S(2)}) copy-start(f32[1,336,128]{2,1,0:T(8,128)} %get-tuple-element.43) | copy-start | bytes 516100
  32.7 13.5 %collective-permute-start.3 = (f32[1,336,128]{2,1,0:T(8,128)}, f32[1,336,128]{2,1,0:T(8,128)S(1)}, u32[]{:S(2)}, u32[]{:S(2)}) collective-permute-start(f32[1,336,128]{2,1,0:T(8,128)} %get-tuple-element.41), channel_id=1, source_target_pairs={{0,1},{1,2},{2,3},{3,0},{4,5},{5,6},{6,7},{7,4},{8,9},{9,10},{10,1... | collective-permute-start | bytes 516104 | tf_op jit(solution)/shard_map/ppermute | solution.py:401
  37.2 22.1 %collective-permute-start.16 = (f32[1,672,128]{2,1,0:T(8,128)}, f32[1,672,128]{2,1,0:T(8,128)S(1)}, u32[]{:S(2)}, u32[]{:S(2)}) collective-permute-start(f32[1,672,128]{2,1,0:T(8,128)} %get-tuple-element.55), channel_id=1, source_target_pairs={{0,8},{8,16},{16,24},{24,32},{32,40},{40,48},{48,56},{56,64},{64,7... | collective-permute-start | bytes 1032200 | tf_op jit(solution)/shard_map/ppermute | solution.py:392
  40.2 7.4 %copy-start.10 = (f32[1,672,128]{2,1,0:T(8,128)}, f32[1,672,128]{2,1,0:T(8,128)S(1)}, u32[]{:S(2)}) copy-start(f32[1,672,128]{2,1,0:T(8,128)S(1)} %collective-permute-done.8.refs_1_) | copy-start | bytes 1032196
  40.2 21.2 %collective-permute-start.17 = (f32[1,672,128]{2,1,0:T(8,128)}, f32[1,672,128]{2,1,0:T(8,128)S(1)}, u32[]{:S(2)}, u32[]{:S(2)}) collective-permute-start(f32[1,672,128]{2,1,0:T(8,128)} %get-tuple-element.56), channel_id=1, source_target_pairs={{4,8},{12,16},{20,24},{28,32},{36,40},{44,48},{52,56},{60,64},{68,... | collective-permute-start | bytes 1032200 | tf_op jit(solution)/shard_map/ppermute | solution.py:393
  42.9 4.8 %copy-start.11 = (f32[1,672,128]{2,1,0:T(8,128)}, f32[1,672,128]{2,1,0:T(8,128)S(1)}, u32[]{:S(2)}) copy-start(f32[1,672,128]{2,1,0:T(8,128)S(1)} %collective-permute-done.9.refs_2_) | copy-start | bytes 1032196
  42.9 20.1 %collective-permute-start.18 = (f32[1,672,128]{2,1,0:T(8,128)}, f32[1,672,128]{2,1,0:T(8,128)S(1)}, u32[]{:S(2)}, u32[]{:S(2)}) collective-permute-start(f32[1,672,128]{2,1,0:T(8,128)} %get-tuple-element.57), channel_id=1, source_target_pairs={{0,4},{4,0},{8,12},{12,8},{16,20},{20,16},{24,28},{28,24},{32,36},... | collective-permute-start | bytes 1032200 | tf_op jit(solution)/shard_map/ppermute | solution.py:394
  43.3 4.3 %copy-start.13 = (f32[1,672,128]{2,1,0:T(8,128)}, f32[1,672,128]{2,1,0:T(8,128)S(1)}, u32[]{:S(2)}) copy-start(f32[1,672,128]{2,1,0:T(8,128)S(1)} %collective-permute-done.10.refs_3_) | copy-start | bytes 1032196
  43.3 8.0 %collective-permute-start.4 = (f32[1,336,128]{2,1,0:T(8,128)S(1)}, f32[1,336,128]{2,1,0:T(8,128)S(1)}, u32[]{:S(2)}, u32[]{:S(2)}) collective-permute-start(f32[1,336,128]{2,1,0:T(8,128)S(1)} %copy-done.25), channel_id=1, source_target_pairs={{0,2},{1,3},{2,0},{3,1},{4,6},{5,7},{6,4},{7,5},{8,10},{9,11},{10,... | collective-permute-start | bytes 516104 | tf_op jit(solution)/shard_map/ppermute | solution.py:401
  46.2 11.0 %copy-start.19 = (f32[1,336,128]{2,1,0:T(8,128)}, f32[1,336,128]{2,1,0:T(8,128)S(1)}, u32[]{:S(2)}) copy-start(f32[1,336,128]{2,1,0:T(8,128)S(1)} %collective-permute-done.3.refs_1_) | copy-start | bytes 516100
  46.2 8.0 %collective-permute-start.5 = (f32[1,336,128]{2,1,0:T(8,128)S(1)}, f32[1,336,128]{2,1,0:T(8,128)S(1)}, u32[]{:S(2)}, u32[]{:S(2)}) collective-permute-start(f32[1,336,128]{2,1,0:T(8,128)S(1)} %copy-done.24), channel_id=1, source_target_pairs={{0,3},{1,0},{2,1},{3,2},{4,7},{5,4},{6,5},{7,6},{8,11},{9,8},{10,9... | collective-permute-start | bytes 516104 | tf_op jit(solution)/shard_map/ppermute | solution.py:401
  51.4 5.9 %copy-start.22 = (f32[1,336,128]{2,1,0:T(8,128)}, f32[1,336,128]{2,1,0:T(8,128)S(1)}, u32[]{:S(2)}) copy-start(f32[1,336,128]{2,1,0:T(8,128)S(1)} %collective-permute-done.4.refs_2_) | copy-start | bytes 516100
  51.4 16.7 %collective-permute-start.11 = (f32[1,336,128]{2,1,0:T(8,128)}, f32[1,336,128]{2,1,0:T(8,128)S(1)}, u32[]{:S(2)}, u32[]{:S(2)}) collective-permute-start(f32[1,336,128]{2,1,0:T(8,128)} %get-tuple-element.50), channel_id=1, source_target_pairs={{0,1},{1,2},{2,3},{3,0},{4,5},{5,6},{6,7},{7,4},{8,9},{9,10},{10,1... | collective-permute-start | bytes 516104 | tf_op jit(solution)/shard_map/ppermute | solution.py:401
  54.2 3.0 %copy-start.23 = (f32[1,336,128]{2,1,0:T(8,128)}, f32[1,336,128]{2,1,0:T(8,128)S(1)}, u32[]{:S(2)}) copy-start(f32[1,336,128]{2,1,0:T(8,128)S(1)} %collective-permute-done.5.refs_3_) | copy-start | bytes 516100
  54.2 15.4 %collective-permute-start.12 = (f32[1,336,128]{2,1,0:T(8,128)}, f32[1,336,128]{2,1,0:T(8,128)S(1)}, u32[]{:S(2)}, u32[]{:S(2)}) collective-permute-start(f32[1,336,128]{2,1,0:T(8,128)} %get-tuple-element.51), channel_id=1, source_target_pairs={{0,2},{1,3},{2,0},{3,1},{4,6},{5,7},{6,4},{7,5},{8,10},{9,11},{10,... | collective-permute-start | bytes 516104 | tf_op jit(solution)/shard_map/ppermute | solution.py:401
  59.3 12.0 %copy-start.1 = (f32[1,672,128]{2,1,0:T(8,128)S(1)}, f32[1,672,128]{2,1,0:T(8,128)}, u32[]{:S(2)}) copy-start(f32[1,672,128]{2,1,0:T(8,128)} %get-tuple-element.45.refs_1_) | copy-start | bytes 1032196
  59.3 3.7 %copy-start.8 = (f32[1,672,128]{2,1,0:T(8,128)}, f32[1,672,128]{2,1,0:T(8,128)S(1)}, u32[]{:S(2)}) copy-start(f32[1,672,128]{2,1,0:T(8,128)S(1)} %collective-permute-done.16.refs_1_) | copy-start | bytes 1032196
  59.3 32.0 %collective-permute-start.6 = (f32[1,672,128]{2,1,0:T(8,128)}, f32[1,672,128]{2,1,0:T(8,128)S(1)}, u32[]{:S(2)}, u32[]{:S(2)}) collective-permute-start(f32[1,672,128]{2,1,0:T(8,128)} %get-tuple-element.44.refs_2_), channel_id=1, source_target_pairs={{0,4},{4,8},{8,12},{12,16},{16,20},{20,24},{24,28},{28,32},{32,36}... | collective-permute-start | bytes 1032200 | tf_op jit(solution)/shard_map/ppermute | solution.py:407
  61.4 1.6 %copy-start.9 = (f32[1,672,128]{2,1,0:T(8,128)}, f32[1,672,128]{2,1,0:T(8,128)S(1)}, u32[]{:S(2)}) copy-start(f32[1,672,128]{2,1,0:T(8,128)S(1)} %collective-permute-done.17.refs_2_) | copy-start | bytes 1032196
  61.4 40.8 %copy-start = (bf16[1,1,2688,128]{3,2,1,0:T(8,128)(2,1)S(1)}, bf16[1,1,2688,128]{3,2,1,0:T(8,128)(2,1)}, u32[]{:S(2)}) copy-start(bf16[1,1,2688,128]{3,2,1,0:T(8,128)(2,1)} %param.12) | copy-start | bytes 2064388
  61.4 40.8 %copy-start.2 = (f32[1,672,128]{2,1,0:T(8,128)S(1)}, f32[1,672,128]{2,1,0:T(8,128)}, u32[]{:S(2)}) copy-start(f32[1,672,128]{2,1,0:T(8,128)} %get-tuple-element.44.refs_2_) | copy-start | bytes 1032196
  61.4 40.8 %copy-start.7 = (s32[4,64]{1,0:T(4,128)S(1)}, s32[4,64]{1,0:T(4,128)}, u32[]{:S(2)}) copy-start(s32[4,64]{1,0:T(4,128)} %offsets.13) | copy-start | bytes 3076
  61.4 9.8 %collective-permute-start.13 = (f32[1,336,128]{2,1,0:T(8,128)}, f32[1,336,128]{2,1,0:T(8,128)}, u32[]{:S(2)}, u32[]{:S(2)}) collective-permute-start(f32[1,336,128]{2,1,0:T(8,128)} %get-tuple-element.52), channel_id=1, source_target_pairs={{0,3},{1,0},{2,1},{3,2},{4,7},{5,4},{6,5},{7,6},{8,11},{9,8},{10,9... | collective-permute-start | bytes 516104 | tf_op jit(solution)/shard_map/ppermute | solution.py:401
  63.0 0.8 copy-start.12
  67.5 12.2 %collective-permute-start.19 = (f32[1,336,128]{2,1,0:T(8,128)}, f32[1,336,128]{2,1,0:T(8,128)S(1)}, u32[]{:S(2)}, u32[]{:S(2)}) collective-permute-start(f32[1,336,128]{2,1,0:T(8,128)} %get-tuple-element.59), channel_id=1, source_target_pairs={{0,1},{1,2},{2,3},{3,0},{4,5},{5,6},{6,7},{7,4},{8,9},{9,10},{10,1... | collective-permute-start | bytes 516104 | tf_op jit(solution)/shard_map/ppermute | solution.py:401
  68.1 7.9 %copy-start.17 = (f32[1,336,128]{2,1,0:T(8,128)}, f32[1,336,128]{2,1,0:T(8,128)S(1)}, u32[]{:S(2)}) copy-start(f32[1,336,128]{2,1,0:T(8,128)S(1)} %collective-permute-done.11.refs_1_) | copy-start | bytes 516100
  68.1 13.5 %collective-permute-start.20 = (f32[1,336,128]{2,1,0:T(8,128)}, f32[1,336,128]{2,1,0:T(8,128)S(1)}, u32[]{:S(2)}, u32[]{:S(2)}) collective-permute-start(f32[1,336,128]{2,1,0:T(8,128)} %get-tuple-element.60), channel_id=1, source_target_pairs={{0,2},{1,3},{2,0},{3,1},{4,6},{5,7},{6,4},{7,5},{8,10},{9,11},{10,... | collective-permute-start | bytes 516104 | tf_op jit(solution)/shard_map/ppermute | solution.py:401
  69.6 6.3 %copy-start.18 = (f32[1,336,128]{2,1,0:T(8,128)}, f32[1,336,128]{2,1,0:T(8,128)S(1)}, u32[]{:S(2)}) copy-start(f32[1,336,128]{2,1,0:T(8,128)S(1)} %collective-permute-done.12.refs_2_) | copy-start | bytes 516100
  69.6 17.7 %collective-permute-start.21 = (f32[1,336,128]{2,1,0:T(8,128)}, f32[1,336,128]{2,1,0:T(8,128)}, u32[]{:S(2)}, u32[]{:S(2)}) collective-permute-start(f32[1,336,128]{2,1,0:T(8,128)} %get-tuple-element.61), channel_id=1, source_target_pairs={{0,3},{1,0},{2,1},{3,2},{4,7},{5,4},{6,5},{7,6},{8,11},{9,8},{10,9... | collective-permute-start | bytes 516104 | tf_op jit(solution)/shard_map/ppermute | solution.py:401
  71.3 26.7 %collective-permute-start.7 = (f32[1,672,128]{2,1,0:T(8,128)S(1)}, f32[1,672,128]{2,1,0:T(8,128)S(1)}, u32[]{:S(2)}, u32[]{:S(2)}) collective-permute-start(f32[1,672,128]{2,1,0:T(8,128)S(1)} %copy-done.1), channel_id=1, source_target_pairs={{4,0},{8,4},{12,8},{16,12},{20,16},{24,20},{28,24},{32,28},{36,32}... | collective-permute-start | bytes 1032200 | tf_op jit(solution)/shard_map/ppermute | solution.py:410
  79.6 7.7 %copy-start.20 = (f32[1,336,128]{2,1,0:T(8,128)}, f32[1,336,128]{2,1,0:T(8,128)S(1)}, u32[]{:S(2)}) copy-start(f32[1,336,128]{2,1,0:T(8,128)S(1)} %collective-permute-done.19.refs_1_) | copy-start | bytes 516100
  79.6 18.3 %collective-permute-start.14 = (f32[1,672,128]{2,1,0:T(8,128)}, f32[1,672,128]{2,1,0:T(8,128)S(1)}, u32[]{:S(2)}, u32[]{:S(2)}) collective-permute-start(f32[1,672,128]{2,1,0:T(8,128)} %get-tuple-element.53.refs_6_), channel_id=1, source_target_pairs={{0,4},{4,8},{8,12},{12,16},{16,20},{20,24},{24,28},{28,32},{32,36}... | collective-permute-start | bytes 1032200 | tf_op jit(solution)/shard_map/ppermute | solution.py:407
  81.6 5.8 %copy-start.21 = (f32[1,336,128]{2,1,0:T(8,128)}, f32[1,336,128]{2,1,0:T(8,128)S(1)}, u32[]{:S(2)}) copy-start(f32[1,336,128]{2,1,0:T(8,128)S(1)} %collective-permute-done.20.refs_2_) | copy-start | bytes 516100
  81.6 16.4 %collective-permute-start.15 = (f32[1,672,128]{2,1,0:T(8,128)}, f32[1,672,128]{2,1,0:T(8,128)S(1)}, u32[]{:S(2)}, u32[]{:S(2)}) collective-permute-start(f32[1,672,128]{2,1,0:T(8,128)} %get-tuple-element.54.refs_5_), channel_id=1, source_target_pairs={{4,0},{8,4},{12,8},{16,12},{20,16},{24,20},{28,24},{32,28},{36,32}... | collective-permute-start | bytes 1032200 | tf_op jit(solution)/shard_map/ppermute | solution.py:410
  89.4 10.9 %collective-permute-start.22 = (f32[1,672,128]{2,1,0:T(8,128)}, f32[1,672,128]{2,1,0:T(8,128)S(1)}, u32[]{:S(2)}, u32[]{:S(2)}) collective-permute-start(f32[1,672,128]{2,1,0:T(8,128)} %get-tuple-element.62.refs_10_), channel_id=1, source_target_pairs={{0,4},{4,8},{8,12},{12,16},{16,20},{20,24},{24,28},{28,32},{32,36}... | collective-permute-start | bytes 1032200 | tf_op jit(solution)/shard_map/ppermute | solution.py:407
  91.4 10.8 %collective-permute-start.23 = (f32[1,672,128]{2,1,0:T(8,128)}, f32[1,672,128]{2,1,0:T(8,128)S(1)}, u32[]{:S(2)}, u32[]{:S(2)}) collective-permute-start(f32[1,672,128]{2,1,0:T(8,128)} %get-tuple-element.63.refs_9_), channel_id=1, source_target_pairs={{4,0},{8,4},{12,8},{16,12},{20,16},{24,20},{28,24},{32,28},{36,32}... | collective-permute-start | bytes 1032200 | tf_op jit(solution)/shard_map/ppermute | solution.py:410
  102.2 1.0 copy-start.3
  103.2 1.0 copy-start.4
  104.2 1.0 copy-start.5
  105.1 1.0 copy-start.6

commit v2 on v1

v2 whole, which is shorter than its diff:
```python
import functools
import jax
import jax.numpy as jnp
from jax import lax
from jax.experimental import pallas as pl
from jax.experimental.pallas import tpu as pltpu
from jax.sharding import PartitionSpec as P

beta_one = 0.9
beta_two = 0.95
learn_rate = 0.1
weight_decay = 0.1
epsilon = 1e-08

CAP = 2688
BLOCK = 1344
HALF = 672
WIDE = 680
OLD_RANKS = 32
OLD_UNITS = OLD_RANKS * BLOCK
N_DP = 64
NEW_UNITS = N_DP * BLOCK
HEADS = 112
COLUMNS = 4
GROUP = HEADS // COLUMNS
OLD_HEADS = GROUP // 2
PEER = GROUP // COLUMNS
PART = 16 * PEER * 3
LANES = 128
ORDER = (1, 2, 0)
E_ROWS = CAP + BLOCK
CHUNK = 672
TILE = 48
LIMIT = 12 * 1024 * 1024
FIRST_LIMIT = 62 * 1024 * 1024

HBM = pl.BlockSpec(memory_space=pltpu.HBM)
ANY = pl.BlockSpec(memory_space=pl.ANY)
VMEM = pl.BlockSpec(memory_space=pltpu.VMEM)
SMEM = pl.BlockSpec(memory_space=pltpu.SMEM)


def params():
    return pltpu.CompilerParams(vmem_limit_bytes=LIMIT)


def cost(moved):
    return pl.CostEstimate(flops=0, bytes_accessed=moved, transcendentals=0)


def place():
    dp = lax.axis_index("dp")
    return dp // 2, dp % 2, lax.axis_index("tensor")


def old_start(offsets, shard, rank):
    inside = offsets[shard, jnp.minimum(rank, OLD_RANKS - 1)]
    return jnp.where(rank >= OLD_RANKS, OLD_UNITS, inside)


def first_slots_of(offsets):
    rank, core, column = place()
    base = rank * BLOCK - offsets[2 * column + core, rank]
    up = base + BLOCK
    down = jnp.maximum(base - HALF, -HALF)
    return {
        "own": jnp.where(core == 0, up, down),
        "other": jnp.where(core == 0, down, up),
        "swap": jnp.where(core == 0, base + HALF, base),
        "keep": jnp.where(core == 0, base, base + HALF),
    }


def cut_kernel(plan, offsets, *refs):
    outs = refs[3 : 3 + len(plan)]
    wide, sems = refs[3 + len(plan) :]
    firsts = first_slots_of(offsets)
    copies = []
    for out, pieces in zip(outs, plan):
        for spot, (which, kind) in enumerate(pieces):
            begin = jnp.minimum(jnp.maximum(firsts[kind], 0) // 8 * 8, CAP - WIDE)
            begin = pl.multiple_of(begin, 8)
            n = len(copies)
            copy = pltpu.make_async_copy(
                refs[which].at[pl.ds(begin, WIDE)],
                wide.at[n, pl.ds(HALF, WIDE)],
                sems.at[n],
            )
            copy.start()
            copies.append((copy, out, spot * HALF, HALF + firsts[kind] - begin))
    for n, (copy, out, to, rest) in enumerate(copies):
        copy.wait()
        out[to : to + HALF, :] = wide[n, pl.ds(rest, HALF), :]


def cut(offsets, state, plan, limit, name):
    total = sum(len(pieces) for pieces in plan)
    return pl.pallas_call(
        functools.partial(cut_kernel, plan),
        out_shape=tuple(
            jax.ShapeDtypeStruct((len(pieces) * HALF, LANES), jnp.float32) for pieces in plan
        ),
        in_specs=[SMEM] + [HBM] * 3,
        out_specs=(VMEM,) * len(plan),
        scratch_shapes=[
            pltpu.VMEM((total, HALF + WIDE, LANES), jnp.float32),
            pltpu.SemaphoreType.DMA((total,)),
        ],
        compiler_params=pltpu.CompilerParams(vmem_limit_bytes=limit),
        cost_estimate=cost(total * 2 * HALF * LANES * 4),
        name=name,
    )(offsets, *state)


def tables_kernel(old_heads, new_heads, after, send, recv, where, used):
    column = lax.axis_index("tensor")

    def invert(i, carry):
        where[old_heads[i]] = i
        return carry

    lax.fori_loop(0, HEADS, invert, 0, unroll=8)
    for s in range(COLUMNS):
        target = (column + s) % COLUMNS

        def one(b, found):
            position = where[new_heads[target * GROUP + b]] - column * GROUP
            mine = (position >= 0) & (position < GROUP)
            send[s * 8 + found] = position
            return found + jnp.where(mine, 1, 0)

        lax.fori_loop(0, GROUP, one, jnp.int32(0), unroll=4)
        used[s] = 0

    def slot(b, carry):
        source = where[new_heads[column * GROUP + b]] // GROUP
        shift = (column - source + COLUMNS) % COLUMNS
        found = used[shift]
        recv[shift * 8 + found] = b
        used[shift] = found + 1
        return carry

    lax.fori_loop(0, GROUP, slot, 0, unroll=4)


def tables(old_heads, new_heads, after):
    out = jax.ShapeDtypeStruct((8 * COLUMNS,), jnp.int32)
    return pl.pallas_call(
        tables_kernel,
        out_shape=(out, out),
        in_specs=[SMEM, SMEM, ANY],
        out_specs=(SMEM, SMEM),
        scratch_shapes=[
            pltpu.SMEM((HEADS,), jnp.int32),
            pltpu.SMEM((COLUMNS,), jnp.int32),
        ],
        compiler_params=params(),
        cost_estimate=cost(4_000_000),
        name="tables",
    )(old_heads, new_heads, after)


def spread_kernel(turn, offsets, send, keep, halo, swapped, other_halo, *outs):
    rank, core, column = place()
    shard = 2 * column + core

    def split(which):
        begin = old_start(offsets, which, rank)
        end = old_start(offsets, which, rank + 1)
        return jnp.where(core == 0, begin - rank * BLOCK, end - rank * BLOCK - HALF)

    mine_cut = split(shard)
    other_cut = split(shard + 1 - 2 * core)
    steps = 42 * lax.broadcasted_iota(jnp.int32, (8, LANES), 0)
    low = core == 0

    def choose(first, second, rows, edge):
        return jnp.where((rows < edge) == low, second, first)

    for s in range(COLUMNS):

        def one(q, carry):
            head = send[s * 8 + q]
            side = head // OLD_HEADS
            mine = side == core
            unit = 3 * (head - side * OLD_HEADS)
            for c in range(3):
                for half in range(2):
                    begin = unit + (half * 8 * 42 + c)
                    where = pl.ds(begin, 8, stride=42)
                    rows = steps + begin
                    a = choose(keep[where, :], halo[where, :], rows, mine_cut)
                    there = pl.ds(begin + turn * HALF, 8, stride=42)
                    b = choose(swapped[there, :], other_halo[where, :], rows, other_cut)
                    row = pl.multiple_of(q * 48 + c * 16 + half * 8, 8)
                    outs[s][pl.ds(row, 8), :] = jnp.where(mine, a, b)
            return carry

        lax.fori_loop(0, PEER, one, 0, unroll=True)


def spread(turn, offsets, send, keep, halo, swapped, other_halo):
    out = jax.ShapeDtypeStruct((PART, LANES), jnp.float32)
    return pl.pallas_call(
        functools.partial(spread_kernel, turn),
        out_shape=(out,) * 4,
        in_specs=[SMEM, SMEM] + [VMEM] * 4,
        out_specs=(VMEM,) * 4,
        compiler_params=params(),
        cost_estimate=cost(6 * HALF * LANES * 4),
        name="spread",
    )(offsets, send, keep, halo, swapped, other_halo)


def collect_kernel(recv, *refs):
    parts = refs[:4]
    outer, inner = refs[4:]
    lower = lax.axis_index("dp") % 2 == 0
    for s in range(COLUMNS):
        for q in range(PEER):
            b = recv[s * 8 + q]
            for c in range(3):
                row = q * 48 + c * 16
                to = pl.ds(3 * b + c, 8, stride=84)
                low = parts[s][row : row + 8, :]
                high = parts[s][row + 8 : row + 16, :]
                outer[to, :] = jnp.where(lower, low, high)
                inner[to, :] = jnp.where(lower, high, low)


def collect(recv, parts):
    out = jax.ShapeDtypeStruct((HALF, LANES), jnp.float32)
    return pl.pallas_call(
        collect_kernel,
        out_shape=(out, out),
        in_specs=[SMEM] + [VMEM] * 4,
        out_specs=(VMEM, VMEM),
        compiler_params=params(),
        cost_estimate=cost(4 * HALF * LANES * 4),
        name="collect",
    )(recv, *parts)


def window(offsets):
    dp = lax.axis_index("dp")
    column = lax.axis_index("tensor")
    start = offsets[column, dp]
    inside = offsets[column, jnp.minimum(dp + 1, N_DP - 1)]
    end = jnp.where(dp == N_DP - 1, NEW_UNITS, inside)
    return start - (dp * BLOCK - HALF), end - start


def load_pieces(pieces, held):
    core = lax.axis_index("dp") % 2
    for k, piece in enumerate(pieces):
        spot = pl.multiple_of(jnp.where(core == 0, k, 3 - k) * HALF, 8)
        held[pl.ds(spot, HALF), :] = piece[...]


def chunked(length, compute, outs, bufs, sems):
    copies = []
    for n in range(CAP // CHUNK):
        left = length - n * CHUNK

        @pl.when(left > 0)
        def _():
            def tile(i, carry):
                row = pl.multiple_of(n * CHUNK + i * TILE, TILE)
                used = lax.broadcasted_iota(jnp.int32, (TILE, LANES), 0) < length - row
                for buf, value in zip(bufs, compute(row)):
                    buf[pl.ds(row, TILE), :] = jnp.where(used, value, 0.0)
                return carry

            lax.fori_loop(0, CHUNK // TILE, tile, 0, unroll=2)

        @pl.when(left <= 0)
        def _():
            for buf in bufs:
                buf[n * CHUNK : (n + 1) * CHUNK, :] = jnp.zeros((CHUNK, LANES), jnp.float32)

        for k, (buf, out) in enumerate(zip(bufs, outs)):
            rows = pl.ds(n * CHUNK, CHUNK)
            copy = pltpu.make_async_copy(buf.at[rows], out.at[rows], sems.at[k, n])
            copy.start()
            copies.append(copy)
    for copy in copies:
        copy.wait()


def moments_kernel(offsets, fixes, *refs):
    gradient, first_out, second_out, ratio_out = refs[8:12]
    first_held, second_held, first_buf, second_buf, sems = refs[12:]
    begin, length = window(offsets)
    load_pieces(refs[:4], first_held)
    load_pieces(refs[4:8], second_held)

    def compute(row):
        rows = pl.ds(begin + row, TILE)
        grad = gradient[pl.ds(row, TILE), :].astype(jnp.float32)
        new_first = beta_one * first_held[rows, :] + (1.0 - beta_one) * grad
        new_second = beta_two * second_held[rows, :] + (1.0 - beta_two) * grad * grad
        root = jnp.sqrt(new_second * fixes[1]) + epsilon
        ratio_out[pl.ds(row, TILE), :] = new_first * fixes[0] / root
        return new_first, new_second

    chunked(length, compute, (first_out, second_out), (first_buf, second_buf), sems)


def moments(offsets, fixes, pieces, gradient):
    out = jax.ShapeDtypeStruct((CAP, LANES), jnp.float32)
    return pl.pallas_call(
        moments_kernel,
        out_shape=(out,) * 3,
        in_specs=[SMEM, SMEM] + [VMEM] * 9,
        out_specs=(ANY, ANY, VMEM),
        scratch_shapes=[
            pltpu.VMEM((E_ROWS, LANES), jnp.float32),
            pltpu.VMEM((E_ROWS, LANES), jnp.float32),
            pltpu.VMEM((CAP, LANES), jnp.float32),
            pltpu.VMEM((CAP, LANES), jnp.float32),
            pltpu.SemaphoreType.DMA((2, CAP // CHUNK)),
        ],
        compiler_params=params(),
        cost_estimate=cost(7 * CAP * LANES * 4),
        name="moments",
    )(offsets, fixes, *pieces, gradient)


def weights_kernel(offsets, *refs):
    ratio, weight_out, held, buf, sems = refs[4:]
    begin, length = window(offsets)
    load_pieces(refs[:4], held)

    def compute(row):
        master = held[pl.ds(begin + row, TILE), :]
        return (master - learn_rate * (ratio[pl.ds(row, TILE), :] + weight_decay * master),)

    chunked(length, compute, (weight_out,), (buf,), sems)


def weights(offsets, pieces, ratio):
    return pl.pallas_call(
        weights_kernel,
        out_shape=jax.ShapeDtypeStruct((CAP, LANES), jnp.float32),
        in_specs=[SMEM] + [VMEM] * 5,
        out_specs=ANY,
        scratch_shapes=[
            pltpu.VMEM((E_ROWS, LANES), jnp.float32),
            pltpu.VMEM((CAP, LANES), jnp.float32),
            pltpu.SemaphoreType.DMA((1, CAP // CHUNK)),
        ],
        compiler_params=params(),
        cost_estimate=cost(3 * CAP * LANES * 4),
        name="weights",
    )(offsets, *pieces, ratio)


def routes():
    ranks = range(OLD_RANKS)
    above = [(r + 1) % OLD_RANKS for r in ranks]
    own = [(2 * r, 2 * above[r]) for r in ranks] + [(2 * above[r] + 1, 2 * r + 1) for r in ranks]
    other = [(2 * r + 1, 2 * above[r]) for r in ranks] + [(2 * above[r], 2 * r + 1) for r in ranks]
    swap = [(i, i ^ 1) for i in range(N_DP)]
    return own, other, swap


def shards(
    old_weight,
    old_first,
    old_second,
    gradient,
    old_offsets,
    new_offsets,
    old_heads,
    new_heads,
    step_count,
):
    state = (old_weight[0, 0], old_first[0, 0], old_second[0, 0])
    own_route, other_route, swap_route = routes()
    shift = [[(i, (i + s) % COLUMNS) for i in range(COLUMNS)] for s in range(COLUMNS)]

    f, s, w = ORDER
    swap_part, *near = cut(
        old_offsets,
        state,
        (tuple((m, "swap") for m in ORDER), ((f, "own"),), ((f, "other"),)),
        FIRST_LIMIT,
        "pack",
    )
    swapped = lax.ppermute(swap_part, "dp", swap_route)
    moved = {f: [lax.ppermute(near[0], "dp", own_route), lax.ppermute(near[1], "dp", other_route)]}
    send, recv = tables(old_heads, new_heads, near[0])
    late = cut(
        old_offsets,
        state,
        tuple(((m, kind),) for m in (s, w) for kind in ("own", "other"))
        + tuple(((m, "keep"),) for m in ORDER),
        LIMIT,
        "pack",
    )
    kept = dict(zip(ORDER, late[4:]))
    moved[s] = [lax.ppermute(late[0], "dp", own_route), lax.ppermute(late[1], "dp", other_route)]
    moved[w] = [lax.ppermute(late[2], "dp", own_route), lax.ppermute(late[3], "dp", other_route)]
    pieces = {}
    for turn, m in enumerate(ORDER):
        parts = spread(turn, old_offsets, send, kept[m], moved[m][0], swapped, moved[m][1])
        parts = [parts[0]] + [lax.ppermute(parts[k], "tensor", shift[k]) for k in (1, 2, 3)]
        outer, inner = collect(recv, parts)
        pieces[m] = [
            lax.ppermute(outer, "dp", other_route),
            outer,
            inner,
            lax.ppermute(inner, "dp", swap_route),
        ]
    step_float = step_count.astype(jnp.float32)
    fixes = jnp.stack(
        [
            1.0 / (1.0 - jnp.power(jnp.float32(beta_one), step_float)),
            1.0 / (1.0 - jnp.power(jnp.float32(beta_two), step_float)),
        ]
    )
    first, second, ratio = moments(new_offsets, fixes, pieces[1] + pieces[2], gradient[0, 0])
    weight = weights(new_offsets, pieces[0], ratio)
    return tuple(out[None, None] for out in (weight, first, second))


def solution(mesh):
    spread_out = P("dp", "tensor", None, None)
    return jax.shard_map(
        shards,
        mesh=mesh,
        in_specs=(spread_out,) * 4 + (P(),) * 5,
        out_specs=(spread_out,) * 3,
        check_vma=False,
    )
```

time: 113 us -> 75 us (0.66)
  the two profiles are of different devices: /device:TPU:8 before, /device:TPU:1 now
where the time goes in v2:
time: 75 us; the launch traced here: 74.8 us
  starting transfers between devices  43.6 us (58%)
  Pallas kernels  19 us (25%)
  waiting for transfers between devices  7.6 us (10%)
  local copies, waits for them, and re-layouts  2.71 us (4%)
  between operations  1.77 us (2%)
    ppermute x3, starting transfers between devices, shards(): lax.ppermute(inner, 'dp', swap_route)  12.5 us
    ppermute x9, starting transfers between devices, shards(): lax.ppermute(parts[k], 'tensor', shift[k])  9.07 us
    ppermute x1, starting transfers between devices, shards(): lax.ppermute(near[0], 'dp', own_route)  6.35 us
    ppermute x9, waiting for transfers between devices, shards(): lax.ppermute(parts[k], 'tensor', shift[k])  5.61 us
    ppermute x1, starting transfers between devices, shards(): lax.ppermute(late[2], 'dp', own_route)  5.51 us
    ppermute x3, starting transfers between devices, shards(): lax.ppermute(outer, 'dp', other_route)  5.45 us
    pallas_call x2, Pallas kernels, cut(): pl.pallas_call(functools.partial(cut_kernel, plan), out_shape=tuple((jax....  5.37 us
    ppermute x1, starting transfers between devices, shards(): swapped = lax.ppermute(swap_part, 'dp', swap_route)  3.25 us
  transfers between devices with their start and end apart: 22, of which 3 were waited for; matrix products, arithmetic and copies ran while one was open for 0% of the time, Pallas kernels for 17%

profile of v2, /device:TPU:1, one launch (start us, length us, event | category | flops | bytes accessed | tf_op | source)
XLA Modules:
  0.0 74.8 jit_solution(9298118026212876331)
XLA Ops:
  0.6 0.0 copy-start
  0.6 0.0 copy-start.5
  0.6 3.6 %pack.2 = (f32[2016,128]{1,0:T(8,128)}, f32[672,128]{1,0:T(8,128)}, f32[672,128]{1,0:T(8,128)}) custom-call(s32[8,32]{1,0:T(8,128)} %offsets.11, f32[2688,128]{1,0:T(8,128)} %bitcast.9, f32[2688,128]{1,0:T(8,128)} %bitcast.11, f32[2688,128]{1,0:T(8,128)} %bitcast.13), custom_call_target="tpu_custom_call" | custom-call | bytes 3440640 | tf_op jit(solution)/shard_map/pack/pallas_call | solution.py:98
  4.2 3.3 %collective-permute-start.1 = (f32[2016,128]{1,0:T(8,128)}, f32[2016,128]{1,0:T(8,128)S(1)}, u32[]{:S(2)}, u32[]{:S(2)}) collective-permute-start(f32[2016,128]{1,0:T(8,128)} %get-tuple-element.41), channel_id=1, source_target_pairs={{0,4},{4,0},{8,12},{12,8},{16,20},{20,16},{24,28},{28,24},{32,36},... | collective-permute-start | bytes 3096584 | tf_op jit(solution)/shard_map/ppermute | solution.py:390
  7.5 0.0 collective-permute-start.9
  7.5 6.4 %collective-permute-start.8 = (f32[672,128]{1,0:T(8,128)}, f32[672,128]{1,0:T(8,128)S(1)}, u32[]{:S(2)}, u32[]{:S(2)}) collective-permute-start(f32[672,128]{1,0:T(8,128)} %get-tuple-element.36.after), channel_id=1, source_target_pairs={{0,8},{8,16},{16,24},{24,32},{32,40},{40,48},{48,56},{56,64},{64,7... | collective-permute-start | bytes 1032200 | tf_op jit(solution)/shard_map/ppermute | solution.py:391
  13.9 0.0 copy-done.5
  13.9 1.3 %copy-done.1 = f32[1,1,2688,128]{3,2,1,0:T(8,128)S(1)} copy-done((f32[1,1,2688,128]{3,2,1,0:T(8,128)S(1)}, f32[1,1,2688,128]{3,2,1,0:T(8,128)}, u32[]{:S(2)}) %copy-start.1) | copy-done | bytes 1376280
  15.2 1.3 %copy-done.2 = f32[1,1,2688,128]{3,2,1,0:T(8,128)S(1)} copy-done((f32[1,1,2688,128]{3,2,1,0:T(8,128)S(1)}, f32[1,1,2688,128]{3,2,1,0:T(8,128)}, u32[]{:S(2)}) %copy-start.2) | copy-done | bytes 1376280
  16.5 1.8 %pack.3 = (f32[672,128]{1,0:T(8,128)S(1)}, f32[672,128]{1,0:T(8,128)S(1)}, f32[672,128]{1,0:T(8,128)S(1)}, f32[672,128]{1,0:T(8,128)S(1)}, f32[672,128]{1,0:T(8,...) custom-call(s32[8,32]{1,0:T(8,128)S(1)} %copy-done.5, f32[2688,128]{1,0:T(8,128)S(1)} %bitcast.10, ...), custom_call_target="tpu_custom_call" | custom-call | bytes 4816896 | tf_op jit(solution)/shard_map/pack/pallas_call | solution.py:98
  18.3 1.5 %collective-permute-start.15 = (f32[672,128]{1,0:T(8,128)S(1)}, f32[672,128]{1,0:T(8,128)S(1)}, u32[]{:S(2)}, u32[]{:S(2)}) collective-permute-start(f32[672,128]{1,0:T(8,128)S(1)} %get-tuple-element.58), channel_id=1, source_target_pairs={{0,8},{8,16},{16,24},{24,32},{32,40},{40,48},{48,56},{56,64},{64,7... | collective-permute-start | bytes 1032200 | tf_op jit(solution)/shard_map/ppermute | solution.py:402
  19.8 0.0 collective-permute-start.16
  19.8 0.0 copy-done.4
  19.8 2.3 %tables.1 = (s32[32]{0:T(128)S(1)}, s32[32]{0:T(128)S(1)}) custom-call(s32[112]{0:T(128)S(1)} %copy-done.7, s32[112]{0:T(128)S(1)} %copy-done.8, f32[672,128]{1,0:T(8,128)S(1)} %copy-done.4), custom_call_target="tpu_custom_call" | custom-call | bytes 4000000 | tf_op jit(solution)/shard_map/tables/pallas_call | solution.py:148
  22.1 0.0 collective-permute-done.9.other_halo
  22.1 5.5 %collective-permute-start = (f32[672,128]{1,0:T(8,128)S(1)}, f32[672,128]{1,0:T(8,128)S(1)}, u32[]{:S(2)}, u32[]{:S(2)}) collective-permute-start(f32[672,128]{1,0:T(8,128)S(1)} %get-tuple-element.40), channel_id=1, source_target_pairs={{0,8},{8,16},{16,24},{24,32},{32,40},{40,48},{48,56},{56,64},{64,7... | collective-permute-start | bytes 1032200 | tf_op jit(solution)/shard_map/ppermute | solution.py:403
  27.6 0.0 collective-permute-done.8.halo
  27.6 0.0 collective-permute-start.2
  27.7 0.0 collective-permute-done.1.swapped
  27.7 1.0 %spread.4 = (f32[336,128]{1,0:T(8,128)S(1)}, f32[336,128]{1,0:T(8,128)S(1)}, f32[336,128]{1,0:T(8,128)S(1)}, f32[336,128]{1,0:T(8,128)S(1)}) custom-call(s32[8,32]{1,0:T(8,128)S(1)} %copy-done.5, s32[32]{0:T(128)S(1)} %get-tuple-element.38.send, f32[672,128]{1,0:T(8,128)S(1)} %get-tuple-element.49.keep, f32[672,128]{1,0:T(8,128)S(1)} %collective-permute-done.8.halo, ...), custom_call_target="tpu_custom_call" | custom-call | bytes 2064384 | tf_op jit(solution)/shard_map/spread/pallas_call | solution.py:204
  28.7 1.3 %collective-permute-start.10 = (f32[336,128]{1,0:T(8,128)S(1)}, f32[336,128]{1,0:T(8,128)S(1)}, u32[]{:S(2)}, u32[]{:S(2)}) collective-permute-start(f32[336,128]{1,0:T(8,128)S(1)} %get-tuple-element.52), channel_id=1, source_target_pairs={{0,1},{1,2},{2,3},{3,0},{4,5},{5,6},{6,7},{7,4},{8,9},{9,10},{10,1... | collective-permute-start | bytes 516104 | tf_op jit(solution)/shard_map/ppermute | solution.py:407
  29.9 0.0 collective-permute-done.15.halo
  29.9 2.5 %collective-permute-start.11 = (f32[336,128]{1,0:T(8,128)S(1)}, f32[336,128]{1,0:T(8,128)S(1)}, u32[]{:S(2)}, u32[]{:S(2)}) collective-permute-start(f32[336,128]{1,0:T(8,128)S(1)} %get-tuple-element.53), channel_id=1, source_target_pairs={{0,2},{1,3},{2,0},{3,1},{4,6},{5,7},{6,4},{7,5},{8,10},{9,11},{10,... | collective-permute-start | bytes 516104 | tf_op jit(solution)/shard_map/ppermute | solution.py:407
  32.4 0.0 collective-permute-done.16.other_halo
  32.4 1.2 %collective-permute-start.12 = (f32[336,128]{1,0:T(8,128)S(1)}, f32[336,128]{1,0:T(8,128)S(1)}, u32[]{:S(2)}, u32[]{:S(2)}) collective-permute-start(f32[336,128]{1,0:T(8,128)S(1)} %get-tuple-element.54), channel_id=1, source_target_pairs={{0,3},{1,0},{2,1},{3,2},{4,7},{5,4},{6,5},{7,6},{8,11},{9,8},{10,9... | collective-permute-start | bytes 516104 | tf_op jit(solution)/shard_map/ppermute | solution.py:407
  33.5 1.0 %spread.5 = (f32[336,128]{1,0:T(8,128)S(1)}, f32[336,128]{1,0:T(8,128)S(1)}, f32[336,128]{1,0:T(8,128)S(1)}, f32[336,128]{1,0:T(8,128)S(1)}) custom-call(s32[8,32]{1,0:T(8,128)S(1)} %copy-done.5, s32[32]{0:T(128)S(1)} %get-tuple-element.38.send, f32[672,128]{1,0:T(8,128)S(1)} %get-tuple-element.57.keep, f32[672,128]{1,0:T(8,128)S(1)} %collective-permute-done.15.halo, ...), custom_call_target="tpu_custom_call" | custom-call | bytes 2064384 | tf_op jit(solution)/shard_map/spread/pallas_call | solution.py:204
  34.5 1.0 %collective-permute-done.10.refs_1_ = f32[336,128]{1,0:T(8,128)S(1)} collective-permute-done((f32[336,128]{1,0:T(8,128)S(1)}, f32[336,128]{1,0:T(8,128)S(1)}, u32[]{:S(2)}, u32[]{:S(2)}) %collective-permute-start.10) | collective-permute-done | bytes 172064 | tf_op jit(solution)/shard_map/ppermute | solution.py:407
  35.5 0.0 collective-permute-start.17
  35.5 4.6 %collective-permute-done.11.refs_2_ = f32[336,128]{1,0:T(8,128)S(1)} collective-permute-done((f32[336,128]{1,0:T(8,128)S(1)}, f32[336,128]{1,0:T(8,128)S(1)}, u32[]{:S(2)}, u32[]{:S(2)}) %collective-permute-start.11) | collective-permute-done | bytes 172064 | tf_op jit(solution)/shard_map/ppermute | solution.py:407
  40.1 0.0 collective-permute-start.18
  40.1 0.0 collective-permute-done.12.refs_3_
  40.1 0.6 collect.4
  40.8 4.4 %collective-permute-start.13 = (f32[672,128]{1,0:T(8,128)S(1)}, f32[672,128]{1,0:T(8,128)S(1)}, u32[]{:S(2)}, u32[]{:S(2)}) collective-permute-start(f32[672,128]{1,0:T(8,128)S(1)} %get-tuple-element.55.refs_1_), channel_id=1, source_target_pairs={{4,8},{12,16},{20,24},{28,32},{36,40},{44,48},{52,56},{60,64},{68,... | collective-permute-start | bytes 1032200 | tf_op jit(solution)/shard_map/ppermute | solution.py:410
  45.2 0.0 collective-permute-done.halo
  45.2 0.0 collective-permute-start.19
  45.2 0.0 collective-permute-done.2.other_halo
  45.2 0.0 copy-start.3
  45.2 0.0 copy-start.6
  45.2 1.0 %spread.3 = (f32[336,128]{1,0:T(8,128)S(1)}, f32[336,128]{1,0:T(8,128)S(1)}, f32[336,128]{1,0:T(8,128)S(1)}, f32[336,128]{1,0:T(8,128)S(1)}) custom-call(s32[8,32]{1,0:T(8,128)S(1)} %copy-done.5, s32[32]{0:T(128)S(1)} %get-tuple-element.38.send, f32[672,128]{1,0:T(8,128)S(1)} %get-tuple-element.39.keep, f32[672,128]{1,0:T(8,128)S(1)} %collective-permute-done.halo, ...), custom_call_target="tpu_custom_call" | custom-call | bytes 2064384 | tf_op jit(solution)/shard_map/spread/pallas_call | solution.py:204
  46.2 1.7 %collective-permute-start.3 = (f32[336,128]{1,0:T(8,128)S(1)}, f32[336,128]{1,0:T(8,128)S(1)}, u32[]{:S(2)}, u32[]{:S(2)}) collective-permute-start(f32[336,128]{1,0:T(8,128)S(1)} %get-tuple-element.44), channel_id=1, source_target_pairs={{0,1},{1,2},{2,3},{3,0},{4,5},{5,6},{6,7},{7,4},{8,9},{9,10},{10,1... | collective-permute-start | bytes 516104 | tf_op jit(solution)/shard_map/ppermute | solution.py:407
  47.9 0.0 collective-permute-done.17.refs_1_
  47.9 1.7 %collective-permute-start.4 = (f32[336,128]{1,0:T(8,128)S(1)}, f32[336,128]{1,0:T(8,128)S(1)}, u32[]{:S(2)}, u32[]{:S(2)}) collective-permute-start(f32[336,128]{1,0:T(8,128)S(1)} %get-tuple-element.45), channel_id=1, source_target_pairs={{0,2},{1,3},{2,0},{3,1},{4,6},{5,7},{6,4},{7,5},{8,10},{9,11},{10,... | collective-permute-start | bytes 516104 | tf_op jit(solution)/shard_map/ppermute | solution.py:407
  49.6 0.0 collective-permute-done.18.refs_2_
  49.6 0.8 %collective-permute-start.5 = (f32[336,128]{1,0:T(8,128)S(1)}, f32[336,128]{1,0:T(8,128)S(1)}, u32[]{:S(2)}, u32[]{:S(2)}) collective-permute-start(f32[336,128]{1,0:T(8,128)S(1)} %get-tuple-element.46), channel_id=1, source_target_pairs={{0,3},{1,0},{2,1},{3,2},{4,7},{5,4},{6,5},{7,6},{8,11},{9,8},{10,9... | collective-permute-start | bytes 516104 | tf_op jit(solution)/shard_map/ppermute | solution.py:407
  50.4 0.0 collective-permute-done.19.refs_3_
  50.4 5.4 %collective-permute-start.14 = (f32[672,128]{1,0:T(8,128)S(1)}, f32[672,128]{1,0:T(8,128)S(1)}, u32[]{:S(2)}, u32[]{:S(2)}) collective-permute-start(f32[672,128]{1,0:T(8,128)S(1)} %get-tuple-element.56.refs_2_), channel_id=1, source_target_pairs={{0,4},{4,0},{8,12},{12,8},{16,20},{20,16},{24,28},{28,24},{32,36},... | collective-permute-start | bytes 1032200 | tf_op jit(solution)/shard_map/ppermute | solution.py:413
  55.9 0.6 collect.5
  56.5 0.0 collective-permute-done.3.refs_1_
  56.5 1.1 %collective-permute-start.20 = (f32[672,128]{1,0:T(8,128)S(1)}, f32[672,128]{1,0:T(8,128)S(1)}, u32[]{:S(2)}, u32[]{:S(2)}) collective-permute-start(f32[672,128]{1,0:T(8,128)S(1)} %get-tuple-element.64.refs_5_), channel_id=1, source_target_pairs={{4,8},{12,16},{20,24},{28,32},{36,40},{44,48},{52,56},{60,64},{68,... | collective-permute-start | bytes 1032200 | tf_op jit(solution)/shard_map/ppermute | solution.py:410
  57.5 0.0 collective-permute-done.4.refs_2_
  57.5 5.6 %collective-permute-start.21 = (f32[672,128]{1,0:T(8,128)S(1)}, f32[672,128]{1,0:T(8,128)S(1)}, u32[]{:S(2)}, u32[]{:S(2)}) collective-permute-start(f32[672,128]{1,0:T(8,128)S(1)} %get-tuple-element.65.refs_6_), channel_id=1, source_target_pairs={{0,4},{4,0},{8,12},{12,8},{16,20},{20,16},{24,28},{28,24},{32,36},... | collective-permute-start | bytes 1032200 | tf_op jit(solution)/shard_map/ppermute | solution.py:413
  63.2 0.0 collective-permute-done.5.refs_3_
  63.2 1.5 %collect.3 = (f32[672,128]{1,0:T(8,128)}, f32[672,128]{1,0:T(8,128)}) custom-call(s32[32]{0:T(128)S(1)} %get-tuple-element.37.recv, f32[336,128]{1,0:T(8,128)S(1)} %get-tuple-element.43.refs_0_, f32[336,128]{1,0:T(8,128)S(1)} %collective-permute-done.3.refs_1_, f32[336,128]{1,0:T(8,128)S(1)} %collective-permute-done.4.refs_2_, ...), custom_call_target="tpu_custom_call" | custom-call | bytes 1376256 | tf_op jit(solution)/shard_map/collect/pallas_call | solution.py:233
  64.7 0.0 collective-permute-start.6
  64.7 0.0 collective-permute-done.13.refs_0_
  64.7 1.4 %collective-permute-start.7 = (f32[672,128]{1,0:T(8,128)}, f32[672,128]{1,0:T(8,128)}, u32[]{:S(2)}, u32[]{:S(2)}) collective-permute-start(f32[672,128]{1,0:T(8,128)} %get-tuple-element.48.refs_2_), channel_id=1, source_target_pairs={{0,4},{4,0},{8,12},{12,8},{16,20},{20,16},{24,28},{28,24},{32,36},... | collective-permute-start | bytes 1032200 | tf_op jit(solution)/shard_map/ppermute | solution.py:413
  66.9 0.1 pad_maximum_fusion.fixes
  66.9 0.0 collective-permute-done.14.refs_3_
  66.9 0.0 collective-permute-done.20.refs_4_
  66.9 0.0 collective-permute-done.21.refs_7_
  67.0 3.0 %moments.1 = (f32[2688,128]{1,0:T(8,128)}, f32[2688,128]{1,0:T(8,128)}, f32[2688,128]{1,0:T(8,128)S(1)}) custom-call(s32[4,64]{1,0:T(4,128)S(1)} %copy-done.6, f32[2]{0:T(128)S(1)} %pad_maximum_fusion.fixes, f32[672,128]{1,0:T(8,128)S(1)} %collective-permute-done.13.refs_0_, f32[672,128]{1,0:T(8,128)S(1)} %get-tuple-element.55.refs_1_, ...), custom_call_target="tpu_custom_call" | custom-call | bytes 9633792 | tf_op jit(solution)/shard_map/moments/pallas_call | solution.py:311
  70.0 2.0 %collective-permute-done.6.refs_0_ = f32[672,128]{1,0:T(8,128)} collective-permute-done((f32[672,128]{1,0:T(8,128)}, f32[672,128]{1,0:T(8,128)}, u32[]{:S(2)}, u32[]{:S(2)}) %collective-permute-start.6) | collective-permute-done | bytes 344096 | tf_op jit(solution)/shard_map/ppermute | solution.py:410
  71.9 0.0 collective-permute-done.7.refs_3_
  71.9 2.7 %weights.1 = f32[2688,128]{1,0:T(8,128)} custom-call(s32[4,64]{1,0:T(4,128)S(1)} %copy-done.6, f32[672,128]{1,0:T(8,128)} %collective-permute-done.6.refs_0_, f32[672,128]{1,0:T(8,128)} %get-tuple-element.47.refs_1_, f32[672,128]{1,0:T(8,128)} %get-tuple-element.48.refs_2_, f32[672,128]{1,0:T(8,128)} %collective-permute-done.7.refs_3_, ...), custom_call_target="tpu_custom_call" | custom-call | bytes 4128768 | tf_op jit(solution)/shard_map/weights/pallas_call | solution.py:342
  (10 shorter events, 0.0 us)
Async XLA Ops:
  0.6 13.2 %copy-start = (f32[1,1,2688,128]{3,2,1,0:T(8,128)S(1)}, f32[1,1,2688,128]{3,2,1,0:T(8,128)}, u32[]{:S(2)}) copy-start(f32[1,1,2688,128]{3,2,1,0:T(8,128)} %param.9) | copy-start | bytes 4128772
  0.6 13.2 %copy-start.5 = (s32[8,32]{1,0:T(8,128)S(1)}, s32[8,32]{1,0:T(8,128)}, u32[]{:S(2)}) copy-start(s32[8,32]{1,0:T(8,128)} %offsets.11) | copy-start | bytes 3076
  4.2 23.4 %collective-permute-start.1 = (f32[2016,128]{1,0:T(8,128)}, f32[2016,128]{1,0:T(8,128)S(1)}, u32[]{:S(2)}, u32[]{:S(2)}) collective-permute-start(f32[2016,128]{1,0:T(8,128)} %get-tuple-element.41), channel_id=1, source_target_pairs={{0,4},{4,0},{8,12},{12,8},{16,20},{20,16},{24,28},{28,24},{32,36},... | collective-permute-start | bytes 3096584 | tf_op jit(solution)/shard_map/ppermute | solution.py:390
  7.5 14.6 %collective-permute-start.9 = (f32[672,128]{1,0:T(8,128)}, f32[672,128]{1,0:T(8,128)S(1)}, u32[]{:S(2)}, u32[]{:S(2)}) collective-permute-start(f32[672,128]{1,0:T(8,128)} %get-tuple-element.50), channel_id=1, source_target_pairs={{4,8},{12,16},{20,24},{28,32},{36,40},{44,48},{52,56},{60,64},{68,... | collective-permute-start | bytes 1032200 | tf_op jit(solution)/shard_map/ppermute | solution.py:391
  7.5 20.1 %collective-permute-start.8 = (f32[672,128]{1,0:T(8,128)}, f32[672,128]{1,0:T(8,128)S(1)}, u32[]{:S(2)}, u32[]{:S(2)}) collective-permute-start(f32[672,128]{1,0:T(8,128)} %get-tuple-element.36.after), channel_id=1, source_target_pairs={{0,8},{8,16},{16,24},{24,32},{32,40},{40,48},{48,56},{56,64},{64,7... | collective-permute-start | bytes 1032200 | tf_op jit(solution)/shard_map/ppermute | solution.py:391
  13.9 1.3 %copy-start.1 = (f32[1,1,2688,128]{3,2,1,0:T(8,128)S(1)}, f32[1,1,2688,128]{3,2,1,0:T(8,128)}, u32[]{:S(2)}) copy-start(f32[1,1,2688,128]{3,2,1,0:T(8,128)} %param.10) | copy-start | bytes 4128772
  15.2 1.3 %copy-start.2 = (f32[1,1,2688,128]{3,2,1,0:T(8,128)S(1)}, f32[1,1,2688,128]{3,2,1,0:T(8,128)}, u32[]{:S(2)}) copy-start(f32[1,1,2688,128]{3,2,1,0:T(8,128)} %param.11) | copy-start | bytes 4128772
  16.5 3.3 %copy-start.4 = (f32[672,128]{1,0:T(8,128)S(1)}, f32[672,128]{1,0:T(8,128)}, u32[]{:S(2)}) copy-start(f32[672,128]{1,0:T(8,128)} %get-tuple-element.36.after) | copy-start | bytes 1032196
  16.5 3.3 %copy-start.7 = (s32[112]{0:T(128)S(1)}, s32[112]{0:T(128)}, u32[]{:S(2)}) copy-start(s32[112]{0:T(128)} %old_heads.1) | copy-start | bytes 1348
  16.5 3.3 %copy-start.8 = (s32[112]{0:T(128)S(1)}, s32[112]{0:T(128)}, u32[]{:S(2)}) copy-start(s32[112]{0:T(128)} %new_heads.1) | copy-start | bytes 1348
  18.3 11.6 %collective-permute-start.15 = (f32[672,128]{1,0:T(8,128)S(1)}, f32[672,128]{1,0:T(8,128)S(1)}, u32[]{:S(2)}, u32[]{:S(2)}) collective-permute-start(f32[672,128]{1,0:T(8,128)S(1)} %get-tuple-element.58), channel_id=1, source_target_pairs={{0,8},{8,16},{16,24},{24,32},{32,40},{40,48},{48,56},{56,64},{64,7... | collective-permute-start | bytes 1032200 | tf_op jit(solution)/shard_map/ppermute | solution.py:402
  19.8 12.6 %collective-permute-start.16 = (f32[672,128]{1,0:T(8,128)S(1)}, f32[672,128]{1,0:T(8,128)S(1)}, u32[]{:S(2)}, u32[]{:S(2)}) collective-permute-start(f32[672,128]{1,0:T(8,128)S(1)} %get-tuple-element.59), channel_id=1, source_target_pairs={{4,8},{12,16},{20,24},{28,32},{36,40},{44,48},{52,56},{60,64},{68,... | collective-permute-start | bytes 1032200 | tf_op jit(solution)/shard_map/ppermute | solution.py:402
  22.1 23.0 %collective-permute-start = (f32[672,128]{1,0:T(8,128)S(1)}, f32[672,128]{1,0:T(8,128)S(1)}, u32[]{:S(2)}, u32[]{:S(2)}) collective-permute-start(f32[672,128]{1,0:T(8,128)S(1)} %get-tuple-element.40), channel_id=1, source_target_pairs={{0,8},{8,16},{16,24},{24,32},{32,40},{40,48},{48,56},{56,64},{64,7... | collective-permute-start | bytes 1032200 | tf_op jit(solution)/shard_map/ppermute | solution.py:403
  27.6 17.5 %collective-permute-start.2 = (f32[672,128]{1,0:T(8,128)S(1)}, f32[672,128]{1,0:T(8,128)S(1)}, u32[]{:S(2)}, u32[]{:S(2)}) collective-permute-start(f32[672,128]{1,0:T(8,128)S(1)} %get-tuple-element.42), channel_id=1, source_target_pairs={{4,8},{12,16},{20,24},{28,32},{36,40},{44,48},{52,56},{60,64},{68,... | collective-permute-start | bytes 1032200 | tf_op jit(solution)/shard_map/ppermute | solution.py:403
  28.7 6.8 %collective-permute-start.10 = (f32[336,128]{1,0:T(8,128)S(1)}, f32[336,128]{1,0:T(8,128)S(1)}, u32[]{:S(2)}, u32[]{:S(2)}) collective-permute-start(f32[336,128]{1,0:T(8,128)S(1)} %get-tuple-element.52), channel_id=1, source_target_pairs={{0,1},{1,2},{2,3},{3,0},{4,5},{5,6},{6,7},{7,4},{8,9},{9,10},{10,1... | collective-permute-start | bytes 516104 | tf_op jit(solution)/shard_map/ppermute | solution.py:407
  29.9 10.2 %collective-permute-start.11 = (f32[336,128]{1,0:T(8,128)S(1)}, f32[336,128]{1,0:T(8,128)S(1)}, u32[]{:S(2)}, u32[]{:S(2)}) collective-permute-start(f32[336,128]{1,0:T(8,128)S(1)} %get-tuple-element.53), channel_id=1, source_target_pairs={{0,2},{1,3},{2,0},{3,1},{4,6},{5,7},{6,4},{7,5},{8,10},{9,11},{10,... | collective-permute-start | bytes 516104 | tf_op jit(solution)/shard_map/ppermute | solution.py:407
  32.4 7.8 %collective-permute-start.12 = (f32[336,128]{1,0:T(8,128)S(1)}, f32[336,128]{1,0:T(8,128)S(1)}, u32[]{:S(2)}, u32[]{:S(2)}) collective-permute-start(f32[336,128]{1,0:T(8,128)S(1)} %get-tuple-element.54), channel_id=1, source_target_pairs={{0,3},{1,0},{2,1},{3,2},{4,7},{5,4},{6,5},{7,6},{8,11},{9,8},{10,9... | collective-permute-start | bytes 516104 | tf_op jit(solution)/shard_map/ppermute | solution.py:407
  35.5 12.4 %collective-permute-start.17 = (f32[336,128]{1,0:T(8,128)S(1)}, f32[336,128]{1,0:T(8,128)S(1)}, u32[]{:S(2)}, u32[]{:S(2)}) collective-permute-start(f32[336,128]{1,0:T(8,128)S(1)} %get-tuple-element.61), channel_id=1, source_target_pairs={{0,1},{1,2},{2,3},{3,0},{4,5},{5,6},{6,7},{7,4},{8,9},{9,10},{10,1... | collective-permute-start | bytes 516104 | tf_op jit(solution)/shard_map/ppermute | solution.py:407
  40.1 9.4 %collective-permute-start.18 = (f32[336,128]{1,0:T(8,128)S(1)}, f32[336,128]{1,0:T(8,128)S(1)}, u32[]{:S(2)}, u32[]{:S(2)}) collective-permute-start(f32[336,128]{1,0:T(8,128)S(1)} %get-tuple-element.62), channel_id=1, source_target_pairs={{0,2},{1,3},{2,0},{3,1},{4,6},{5,7},{6,4},{7,5},{8,10},{9,11},{10,... | collective-permute-start | bytes 516104 | tf_op jit(solution)/shard_map/ppermute | solution.py:407
  40.8 23.9 %collective-permute-start.13 = (f32[672,128]{1,0:T(8,128)S(1)}, f32[672,128]{1,0:T(8,128)S(1)}, u32[]{:S(2)}, u32[]{:S(2)}) collective-permute-start(f32[672,128]{1,0:T(8,128)S(1)} %get-tuple-element.55.refs_1_), channel_id=1, source_target_pairs={{4,8},{12,16},{20,24},{28,32},{36,40},{44,48},{52,56},{60,64},{68,... | collective-permute-start | bytes 1032200 | tf_op jit(solution)/shard_map/ppermute | solution.py:410
  45.2 5.3 %collective-permute-start.19 = (f32[336,128]{1,0:T(8,128)S(1)}, f32[336,128]{1,0:T(8,128)S(1)}, u32[]{:S(2)}, u32[]{:S(2)}) collective-permute-start(f32[336,128]{1,0:T(8,128)S(1)} %get-tuple-element.63), channel_id=1, source_target_pairs={{0,3},{1,0},{2,1},{3,2},{4,7},{5,4},{6,5},{7,6},{8,11},{9,8},{10,9... | collective-permute-start | bytes 516104 | tf_op jit(solution)/shard_map/ppermute | solution.py:407
  45.2 21.8 %copy-start.3 = (bf16[1,1,2688,128]{3,2,1,0:T(8,128)(2,1)S(1)}, bf16[1,1,2688,128]{3,2,1,0:T(8,128)(2,1)}, u32[]{:S(2)}) copy-start(bf16[1,1,2688,128]{3,2,1,0:T(8,128)(2,1)} %param.12) | copy-start | bytes 2064388
  45.2 21.8 %copy-start.6 = (s32[4,64]{1,0:T(4,128)S(1)}, s32[4,64]{1,0:T(4,128)}, u32[]{:S(2)}) copy-start(s32[4,64]{1,0:T(4,128)} %offsets.13) | copy-start | bytes 3076
  46.2 10.3 %collective-permute-start.3 = (f32[336,128]{1,0:T(8,128)S(1)}, f32[336,128]{1,0:T(8,128)S(1)}, u32[]{:S(2)}, u32[]{:S(2)}) collective-permute-start(f32[336,128]{1,0:T(8,128)S(1)} %get-tuple-element.44), channel_id=1, source_target_pairs={{0,1},{1,2},{2,3},{3,0},{4,5},{5,6},{6,7},{7,4},{8,9},{9,10},{10,1... | collective-permute-start | bytes 516104 | tf_op jit(solution)/shard_map/ppermute | solution.py:407
  47.9 9.6 %collective-permute-start.4 = (f32[336,128]{1,0:T(8,128)S(1)}, f32[336,128]{1,0:T(8,128)S(1)}, u32[]{:S(2)}, u32[]{:S(2)}) collective-permute-start(f32[336,128]{1,0:T(8,128)S(1)} %get-tuple-element.45), channel_id=1, source_target_pairs={{0,2},{1,3},{2,0},{3,1},{4,6},{5,7},{6,4},{7,5},{8,10},{9,11},{10,... | collective-permute-start | bytes 516104 | tf_op jit(solution)/shard_map/ppermute | solution.py:407
  49.6 13.6 %collective-permute-start.5 = (f32[336,128]{1,0:T(8,128)S(1)}, f32[336,128]{1,0:T(8,128)S(1)}, u32[]{:S(2)}, u32[]{:S(2)}) collective-permute-start(f32[336,128]{1,0:T(8,128)S(1)} %get-tuple-element.46), channel_id=1, source_target_pairs={{0,3},{1,0},{2,1},{3,2},{4,7},{5,4},{6,5},{7,6},{8,11},{9,8},{10,9... | collective-permute-start | bytes 516104 | tf_op jit(solution)/shard_map/ppermute | solution.py:407
  50.4 16.5 %collective-permute-start.14 = (f32[672,128]{1,0:T(8,128)S(1)}, f32[672,128]{1,0:T(8,128)S(1)}, u32[]{:S(2)}, u32[]{:S(2)}) collective-permute-start(f32[672,128]{1,0:T(8,128)S(1)} %get-tuple-element.56.refs_2_), channel_id=1, source_target_pairs={{0,4},{4,0},{8,12},{12,8},{16,20},{20,16},{24,28},{28,24},{32,36},... | collective-permute-start | bytes 1032200 | tf_op jit(solution)/shard_map/ppermute | solution.py:413
  56.5 10.5 %collective-permute-start.20 = (f32[672,128]{1,0:T(8,128)S(1)}, f32[672,128]{1,0:T(8,128)S(1)}, u32[]{:S(2)}, u32[]{:S(2)}) collective-permute-start(f32[672,128]{1,0:T(8,128)S(1)} %get-tuple-element.64.refs_5_), channel_id=1, source_target_pairs={{4,8},{12,16},{20,24},{28,32},{36,40},{44,48},{52,56},{60,64},{68,... | collective-permute-start | bytes 1032200 | tf_op jit(solution)/shard_map/ppermute | solution.py:410
  57.5 9.4 %collective-permute-start.21 = (f32[672,128]{1,0:T(8,128)S(1)}, f32[672,128]{1,0:T(8,128)S(1)}, u32[]{:S(2)}, u32[]{:S(2)}) collective-permute-start(f32[672,128]{1,0:T(8,128)S(1)} %get-tuple-element.65.refs_6_), channel_id=1, source_target_pairs={{0,4},{4,0},{8,12},{12,8},{16,20},{20,16},{24,28},{28,24},{32,36},... | collective-permute-start | bytes 1032200 | tf_op jit(solution)/shard_map/ppermute | solution.py:413
  64.7 7.3 %collective-permute-start.6 = (f32[672,128]{1,0:T(8,128)}, f32[672,128]{1,0:T(8,128)}, u32[]{:S(2)}, u32[]{:S(2)}) collective-permute-start(f32[672,128]{1,0:T(8,128)} %get-tuple-element.47.refs_1_), channel_id=1, source_target_pairs={{4,8},{12,16},{20,24},{28,32},{36,40},{44,48},{52,56},{60,64},{68,... | collective-permute-start | bytes 1032200 | tf_op jit(solution)/shard_map/ppermute | solution.py:410
  64.7 7.3 %collective-permute-start.7 = (f32[672,128]{1,0:T(8,128)}, f32[672,128]{1,0:T(8,128)}, u32[]{:S(2)}, u32[]{:S(2)}) collective-permute-start(f32[672,128]{1,0:T(8,128)} %get-tuple-element.48.refs_2_), channel_id=1, source_target_pairs={{0,4},{4,0},{8,12},{12,8},{16,20},{20,16},{24,28},{28,24},{32,36},... | collective-permute-start | bytes 1032200 | tf_op jit(solution)/shard_map/ppermute | solution.py:413

commit v3 on v2

--- a/solution.py
+++ b/solution.py
@@ -27,12 +27,15 @@
 PEER = GROUP // COLUMNS
 PART = 16 * PEER * 3
 LANES = 128
-ORDER = (1, 2, 0)
+GROUPS = ((1,), (2,), (0,))
+ORDER = sum(GROUPS, ())
+SWAP_FIRST = True
+COST_SCALE = 1000
 E_ROWS = CAP + BLOCK
 CHUNK = 672
 TILE = 48
 LIMIT = 12 * 1024 * 1024
-FIRST_LIMIT = 62 * 1024 * 1024
+FIRST_LIMIT = LIMIT
 
 HBM = pl.BlockSpec(memory_space=pltpu.HBM)
 ANY = pl.BlockSpec(memory_space=pl.ANY)
@@ -45,7 +48,7 @@
 
 
 def cost(moved):
-    return pl.CostEstimate(flops=0, bytes_accessed=moved, transcendentals=0)
+    return pl.CostEstimate(flops=0, bytes_accessed=moved // COST_SCALE, transcendentals=0)
 
 
 def place():
@@ -98,7 +101,7 @@
     return pl.pallas_call(
         functools.partial(cut_kernel, plan),
         out_shape=tuple(
-            jax.ShapeDtypeStruct((len(pieces) * HALF, LANES), jnp.float32) for pieces in plan
+            pltpu.VMEM((len(pieces) * HALF, LANES), jnp.float32) for pieces in plan
         ),
         in_specs=[SMEM] + [HBM] * 3,
         out_specs=(VMEM,) * len(plan),
@@ -112,7 +115,7 @@
     )(offsets, *state)
 
 
-def tables_kernel(old_heads, new_heads, after, send, recv, where, used):
+def tables_kernel(old_heads, new_heads, send, recv, where, used):
     column = lax.axis_index("tensor")
 
     def invert(i, carry):
@@ -143,12 +146,12 @@
     lax.fori_loop(0, GROUP, slot, 0, unroll=4)
 
 
-def tables(old_heads, new_heads, after):
+def tables(old_heads, new_heads):
     out = jax.ShapeDtypeStruct((8 * COLUMNS,), jnp.int32)
     return pl.pallas_call(
         tables_kernel,
         out_shape=(out, out),
-        in_specs=[SMEM, SMEM, ANY],
+        in_specs=[SMEM, SMEM],
         out_specs=(SMEM, SMEM),
         scratch_shapes=[
             pltpu.SMEM((HEADS,), jnp.int32),
@@ -157,10 +160,10 @@
         compiler_params=params(),
         cost_estimate=cost(4_000_000),
         name="tables",
-    )(old_heads, new_heads, after)
-
-
-def spread_kernel(turn, offsets, send, keep, halo, swapped, other_halo, *outs):
+    )(old_heads, new_heads)
+
+
+def spread_kernel(turn, count, offsets, send, keep, halo, swapped, other_halo, *outs):
     rank, core, column = place()
     shard = 2 * column + core
 
@@ -184,59 +187,63 @@
             side = head // OLD_HEADS
             mine = side == core
             unit = 3 * (head - side * OLD_HEADS)
-            for c in range(3):
-                for half in range(2):
-                    begin = unit + (half * 8 * 42 + c)
-                    where = pl.ds(begin, 8, stride=42)
-                    rows = steps + begin
-                    a = choose(keep[where, :], halo[where, :], rows, mine_cut)
-                    there = pl.ds(begin + turn * HALF, 8, stride=42)
-                    b = choose(swapped[there, :], other_halo[where, :], rows, other_cut)
-                    row = pl.multiple_of(q * 48 + c * 16 + half * 8, 8)
-                    outs[s][pl.ds(row, 8), :] = jnp.where(mine, a, b)
+            for j in range(count):
+                for c in range(3):
+                    for half in range(2):
+                        begin = unit + (half * 8 * 42 + c)
+                        here = pl.ds(begin + j * HALF, 8, stride=42)
+                        there = pl.ds(begin + (turn + j) * HALF, 8, stride=42)
+                        rows = steps + begin
+                        a = choose(keep[here, :], halo[here, :], rows, mine_cut)
+                        b = choose(swapped[there, :], other_halo[here, :], rows, other_cut)
+                        row = pl.multiple_of(j * PART + q * 48 + c * 16 + half * 8, 8)
+                        outs[s][pl.ds(row, 8), :] = jnp.where(mine, a, b)
             return carry
 
         lax.fori_loop(0, PEER, one, 0, unroll=True)
 
 
 def spread(turn, offsets, send, keep, halo, swapped, other_halo):
-    out = jax.ShapeDtypeStruct((PART, LANES), jnp.float32)
-    return pl.pallas_call(
-        functools.partial(spread_kernel, turn),
+    count = keep.shape[0] // HALF
+    out = pltpu.VMEM((count * PART, LANES), jnp.float32)
+    return pl.pallas_call(
+        functools.partial(spread_kernel, turn, count),
         out_shape=(out,) * 4,
         in_specs=[SMEM, SMEM] + [VMEM] * 4,
         out_specs=(VMEM,) * 4,
         compiler_params=params(),
-        cost_estimate=cost(6 * HALF * LANES * 4),
+        cost_estimate=cost(count * 6 * HALF * LANES * 4),
         name="spread",
     )(offsets, send, keep, halo, swapped, other_halo)
 
 
-def collect_kernel(recv, *refs):
+def collect_kernel(count, recv, *refs):
     parts = refs[:4]
     outer, inner = refs[4:]
     lower = lax.axis_index("dp") % 2 == 0
     for s in range(COLUMNS):
         for q in range(PEER):
             b = recv[s * 8 + q]
-            for c in range(3):
-                row = q * 48 + c * 16
-                to = pl.ds(3 * b + c, 8, stride=84)
-                low = parts[s][row : row + 8, :]
-                high = parts[s][row + 8 : row + 16, :]
-                outer[to, :] = jnp.where(lower, low, high)
-                inner[to, :] = jnp.where(lower, high, low)
+            for j in range(count):
+                for c in range(3):
+                    row = j * PART + q * 48 + c * 16
+                    to = pl.ds(j * HALF + 3 * b + c, 8, stride=84)
+                    low = parts[s][row : row + 8, :]
+                    high = parts[s][row + 8 : row + 16, :]
+                    outer[to, :] = jnp.where(lower, low, high)
+                    inner[to, :] = jnp.where(lower, high, low)
 
 
 def collect(recv, parts):
-    out = jax.ShapeDtypeStruct((HALF, LANES), jnp.float32)
-    return pl.pallas_call(
-        collect_kernel,
+    count = parts[0].shape[0] // PART
+    out = pltpu.VMEM((count * HALF, LANES), jnp.float32)
+    return pl.pallas_call(
+        functools.partial(collect_kernel, count),
         out_shape=(out, out),
         in_specs=[SMEM] + [VMEM] * 4,
         out_specs=(VMEM, VMEM),
         compiler_params=params(),
-        cost_estimate=cost(4 * HALF * LANES * 4),
+        cost_estimate=cost(count * 4 * HALF * LANES * 4),
         name="collect",
     )(recv, *parts)
 
@@ -250,11 +257,11 @@
     return start - (dp * BLOCK - HALF), end - start
 
 
-def load_pieces(pieces, held):
+def load_pieces(pieces, turn, held):
     core = lax.axis_index("dp") % 2
     for k, piece in enumerate(pieces):
         spot = pl.multiple_of(jnp.where(core == 0, k, 3 - k) * HALF, 8)
-        held[pl.ds(spot, HALF), :] = piece[...]
+        held[pl.ds(spot, HALF), :] = piece[turn * HALF : (turn + 1) * HALF, :]
 
 
 def chunked(length, compute, outs, bufs, sems):
@@ -287,12 +294,12 @@
         copy.wait()
 
 
-def moments_kernel(offsets, fixes, *refs):
+def moments_kernel(turns, offsets, fixes, *refs):
     gradient, first_out, second_out, ratio_out = refs[8:12]
     first_held, second_held, first_buf, second_buf, sems = refs[12:]
     begin, length = window(offsets)
-    load_pieces(refs[:4], first_held)
-    load_pieces(refs[4:8], second_held)
+    load_pieces(refs[:4], turns[0], first_held)
+    load_pieces(refs[4:8], turns[1], second_held)
 
     def compute(row):
         rows = pl.ds(begin + row, TILE)
@@ -306,10 +313,10 @@
     chunked(length, compute, (first_out, second_out), (first_buf, second_buf), sems)
 
 
-def moments(offsets, fixes, pieces, gradient):
+def moments(turns, offsets, fixes, pieces, gradient):
     out = jax.ShapeDtypeStruct((CAP, LANES), jnp.float32)
     return pl.pallas_call(
-        moments_kernel,
+        functools.partial(moments_kernel, turns),
         out_shape=(out,) * 3,
         in_specs=[SMEM, SMEM] + [VMEM] * 9,
         out_specs=(ANY, ANY, VMEM),
@@ -326,10 +333,10 @@
     )(offsets, fixes, *pieces, gradient)
 
 
-def weights_kernel(offsets, *refs):
+def weights_kernel(turn, offsets, *refs):
     ratio, weight_out, held, buf, sems = refs[4:]
     begin, length = window(offsets)
-    load_pieces(refs[:4], held)
+    load_pieces(refs[:4], turn, held)
 
     def compute(row):
         master = held[pl.ds(begin + row, TILE), :]
@@ -338,9 +345,9 @@
     chunked(length, compute, (weight_out,), (buf,), sems)
 
 
-def weights(offsets, pieces, ratio):
-    return pl.pallas_call(
-        weights_kernel,
+def weights(turn, offsets, pieces, ratio):
+    return pl.pallas_call(
+        functools.partial(weights_kernel, turn),
         out_shape=jax.ShapeDtypeStruct((CAP, LANES), jnp.float32),
         in_specs=[SMEM] + [VMEM] * 5,
         out_specs=ANY,
@@ -375,43 +382,48 @@
     new_heads,
     step_count,
 ):
-    state = (old_weight[0, 0], old_first[0, 0], old_second[0, 0])
+    state = tuple(
+        pltpu.with_memory_space_constraint(member[0, 0], pltpu.HBM)
+        for member in (old_weight, old_first, old_second)
+    )
     own_route, other_route, swap_route = routes()
     shift = [[(i, (i + s) % COLUMNS) for i in range(COLUMNS)] for s in range(COLUMNS)]
 
-    f, s, w = ORDER
-    swap_part, *near = cut(
-        old_offsets,
-        state,
-        (tuple((m, "swap") for m in ORDER), ((f, "own"),), ((f, "other"),)),
-        FIRST_LIMIT,
-        "pack",
-    )
-    swapped = lax.ppermute(swap_part, "dp", swap_route)
-    moved = {f: [lax.ppermute(near[0], "dp", own_route), lax.ppermute(near[1], "dp", other_route)]}
-    send, recv = tables(old_heads, new_heads, near[0])
-    late = cut(
-        old_offsets,
-        state,
-        tuple(((m, kind),) for m in (s, w) for kind in ("own", "other"))
-        + tuple(((m, "keep"),) for m in ORDER),
-        LIMIT,
-        "pack",
-    )
-    kept = dict(zip(ORDER, late[4:]))
-    moved[s] = [lax.ppermute(late[0], "dp", own_route), lax.ppermute(late[1], "dp", other_route)]
-    moved[w] = [lax.ppermute(late[2], "dp", own_route), lax.ppermute(late[3], "dp", other_route)]
-    pieces = {}
-    for turn, m in enumerate(ORDER):
-        parts = spread(turn, old_offsets, send, kept[m], moved[m][0], swapped, moved[m][1])
+    def halos(groups):
+        return [tuple((m, kind) for m in g) for g in groups for kind in ("own", "other")]
+
+    swap_plan = [tuple((m, "swap") for m in ORDER)]
+    plan = (swap_plan if SWAP_FIRST else []) + halos(GROUPS[:1])
+    rest = ([] if SWAP_FIRST else swap_plan) + halos(GROUPS[1:])
+    rest += [tuple((m, "keep") for m in g) for g in GROUPS]
+    near = list(cut(old_offsets, state, plan, FIRST_LIMIT, "pack"))
+    near[0], later_offsets, old_heads = lax.optimization_barrier((near[0], old_offsets, old_heads))
+    send, recv = tables(old_heads, new_heads)
+    far = list(cut(later_offsets, state, rest, LIMIT, "pack"))
+    swapped = lax.ppermute((near if SWAP_FIRST else far).pop(0), "dp", swap_route)
+    halves = near + far
+    moved = [
+        (
+            lax.ppermute(halves[2 * g], "dp", own_route),
+            lax.ppermute(halves[2 * g + 1], "dp", other_route),
+        )
+        for g in range(len(GROUPS))
+    ]
+    kept = halves[2 * len(GROUPS) :]
+    pieces, turns = {}, {}
+    for g, members in enumerate(GROUPS):
+        turn = ORDER.index(members[0])
+        parts = spread(turn, old_offsets, send, kept[g], moved[g][0], swapped, moved[g][1])
         parts = [parts[0]] + [lax.ppermute(parts[k], "tensor", shift[k]) for k in (1, 2, 3)]
         outer, inner = collect(recv, parts)
-        pieces[m] = [
+        arrived = [
             lax.ppermute(outer, "dp", other_route),
             outer,
             inner,
             lax.ppermute(inner, "dp", swap_route),
         ]
+        for turn, m in enumerate(members):
+            pieces[m], turns[m] = arrived, turn
     step_float = step_count.astype(jnp.float32)
     fixes = jnp.stack(
         [
@@ -419,8 +431,10 @@
             1.0 / (1.0 - jnp.power(jnp.float32(beta_two), step_float)),
         ]
     )
-    first, second, ratio = moments(new_offsets, fixes, pieces[1] + pieces[2], gradient[0, 0])
-    weight = weights(new_offsets, pieces[0], ratio)
+    first, second, ratio = moments(
+        (turns[1], turns[2]), new_offsets, fixes, pieces[1] + pieces[2], gradient[0, 0]
+    )
+    weight = weights(turns[0], new_offsets, pieces[0], ratio)
     return tuple(out[None, None] for out in (weight, first, second))
 
 

time: 75 us -> 71.1 us (0.948)
  waiting for transfers between devices: 7.6 us -> 2.07 us
  starting transfers between devices: 43.6 us -> 48 us
  local copies, waits for them, and re-layouts: 2.71 us -> 0.7 us
  Pallas kernels: 19 us -> 18 us
    ppermute x9, starting transfers between devices: 9.07 us -> 13.2 us  [shards(): lax.ppermute(parts[k], 'tensor', shift[k])]
    ppermute x9, waiting for transfers between devices: 5.61 us -> 1.78 us  [shards(): lax.ppermute(parts[k], 'tensor', shift[k])]
    unnamed x18 -> x12, local copies, waits for them, and re-layouts: 2.71 us -> 0.7 us
    ppermute x3, waiting for transfers between devices: 1.97 us -> 0.22 us  [shards(): lax.ppermute(outer, 'dp', other_route)]
    pallas_call x11, Pallas kernels: 19 us -> 18 us  [the longest x2 4.5 us: cut(): pl.pallas_call(functools.partial(cut_kernel, plan), out_shape=tuple((pltp...]
    ppermute x3, starting transfers between devices: 5.45 us -> 6.43 us  [shards(): lax.ppermute(outer, 'dp', other_route)]
    ppermute x3, starting transfers between devices: 12.5 us -> 11.6 us  [shards(): lax.ppermute(inner, 'dp', swap_route)]
  transfers between devices with their start and end apart: 22 -> 22, of which waited for: 3 -> 2; matrix products, arithmetic and copies ran while one was open for 0% -> 0% of each run, Pallas kernels for 17% -> 19%
where the time goes in v3:
time: 71.1 us; the launch traced here: 70.6 us
  starting transfers between devices  48 us (68%)
  Pallas kernels  18 us (25%)
  waiting for transfers between devices  2.07 us (3%)
  between operations  1.76 us (2%)
    ppermute x9, starting transfers between devices, shards(): lax.ppermute(parts[k], 'tensor', shift[k])  13.2 us
    ppermute x3, starting transfers between devices, shards(): lax.ppermute(halves[2 * g], 'dp', own_route)  12.3 us
    ppermute x3, starting transfers between devices, shards(): lax.ppermute(inner, 'dp', swap_route)  11.6 us
    ppermute x3, starting transfers between devices, shards(): lax.ppermute(outer, 'dp', other_route)  6.43 us
    pallas_call x2, Pallas kernels, cut(): pl.pallas_call(functools.partial(cut_kernel, plan), out_shape=tuple((pltp...  4.5 us
    ppermute x1, starting transfers between devices, shards(): lax.ppermute((near if SWAP_FIRST else far).pop(0), 'dp', swap_route)  3.25 us
    pallas_call x3, Pallas kernels, spread(): pl.pallas_call(functools.partial(spread_kernel, turn, count), out_shape=(...  3.04 us
    pallas_call x1, Pallas kernels, moments(): pl.pallas_call(functools.partial(moments_kernel, turns), out_shape=(out,)...  2.87 us
  transfers between devices with their start and end apart: 22, of which 2 were waited for; matrix products, arithmetic and copies ran while one was open for 0% of the time, Pallas kernels for 19%

profile of v3, /device:TPU:1, one launch (start us, length us, event | category | flops | bytes accessed | tf_op | source)
XLA Modules:
  0.0 70.6 jit_solution(12516050667826045164)
XLA Ops:
  0.6 0.0 copy-start.1
  0.6 0.7 copy-done.1
  1.3 2.2 %pack.2 = (f32[2016,128]{1,0:T(8,128)S(1)}, f32[672,128]{1,0:T(8,128)S(1)}, f32[672,128]{1,0:T(8,128)S(1)}) custom-call(s32[8,32]{1,0:T(8,128)S(1)} %copy-done.1, f32[2688,128]{1,0:T(8,128)} %bitcast.10, f32[2688,128]{1,0:T(8,128)} %bitcast.12, f32[2688,128]{1,0:T(8,128)} %bitcast.14), custom_call_target="tpu_custom_call" | custom-call | bytes 3440 | tf_op jit(solution)/shard_map/pack/pallas_call | solution.py:101
  3.5 3.3 %collective-permute-start.1 = (f32[2016,128]{1,0:T(8,128)S(1)}, f32[2016,128]{1,0:T(8,128)S(1)}, u32[]{:S(2)}, u32[]{:S(2)}) collective-permute-start(f32[2016,128]{1,0:T(8,128)S(1)} %get-tuple-element.46), channel_id=1, source_target_pairs={{0,4},{4,0},{8,12},{12,8},{16,20},{20,16},{24,28},{28,24},{32,36},... | collective-permute-start | bytes 3096584 | tf_op jit(solution)/shard_map/ppermute | solution.py:403
  6.8 6.3 %collective-permute-start.8 = (f32[672,128]{1,0:T(8,128)S(1)}, f32[672,128]{1,0:T(8,128)S(1)}, u32[]{:S(2)}, u32[]{:S(2)}) collective-permute-start(f32[672,128]{1,0:T(8,128)S(1)} %get-tuple-element.55), channel_id=1, source_target_pairs={{0,8},{8,16},{16,24},{24,32},{32,40},{40,48},{48,56},{56,64},{64,7... | collective-permute-start | bytes 1032200 | tf_op jit(solution)/shard_map/ppermute | solution.py:407
  13.1 0.0 copy-start.5
  13.1 0.0 collective-permute-start.9
  13.1 2.3 %pack.3 = (f32[672,128]{1,0:T(8,128)S(1)}, f32[672,128]{1,0:T(8,128)S(1)}, f32[672,128]{1,0:T(8,128)S(1)}, f32[672,128]{1,0:T(8,128)S(1)}, f32[672,128]{1,0:T(8,...) custom-call(s32[8,32]{1,0:T(8,128)S(1)} %copy-done.1, f32[2688,128]{1,0:T(8,128)} %bitcast.11, ...), custom_call_target="tpu_custom_call" | custom-call | bytes 4816 | tf_op jit(solution)/shard_map/pack/pallas_call | solution.py:101
  15.5 0.7 %collective-permute-start.15 = (f32[672,128]{1,0:T(8,128)S(1)}, f32[672,128]{1,0:T(8,128)S(1)}, u32[]{:S(2)}, u32[]{:S(2)}) collective-permute-start(f32[672,128]{1,0:T(8,128)S(1)} %get-tuple-element.64), channel_id=1, source_target_pairs={{0,8},{8,16},{16,24},{24,32},{32,40},{40,48},{48,56},{56,64},{64,7... | collective-permute-start | bytes 1032200 | tf_op jit(solution)/shard_map/ppermute | solution.py:407
  16.2 1.2 %collective-permute-start.16 = (f32[672,128]{1,0:T(8,128)S(1)}, f32[672,128]{1,0:T(8,128)S(1)}, u32[]{:S(2)}, u32[]{:S(2)}) collective-permute-start(f32[672,128]{1,0:T(8,128)S(1)} %get-tuple-element.65), channel_id=1, source_target_pairs={{4,8},{12,16},{20,24},{28,32},{36,40},{44,48},{52,56},{60,64},{68,... | collective-permute-start | bytes 1032200 | tf_op jit(solution)/shard_map/ppermute | solution.py:408
  17.4 0.0 copy-done.4
  17.4 0.0 copy-done.5
  17.4 2.3 %tables.1 = (s32[32]{0:T(128)S(1)}, s32[32]{0:T(128)S(1)}) custom-call(s32[112]{0:T(128)S(1)} %copy-done.4, s32[112]{0:T(128)S(1)} %copy-done.5), custom_call_target="tpu_custom_call" | custom-call | bytes 4000 | tf_op jit(solution)/shard_map/tables/pallas_call | solution.py:151
  19.6 0.0 collective-permute-done.8.halo
  19.7 5.2 %collective-permute-start = (f32[672,128]{1,0:T(8,128)S(1)}, f32[672,128]{1,0:T(8,128)S(1)}, u32[]{:S(2)}, u32[]{:S(2)}) collective-permute-start(f32[672,128]{1,0:T(8,128)S(1)} %get-tuple-element.45), channel_id=1, source_target_pairs={{0,8},{8,16},{16,24},{24,32},{32,40},{40,48},{48,56},{56,64},{64,7... | collective-permute-start | bytes 1032200 | tf_op jit(solution)/shard_map/ppermute | solution.py:407
  24.9 0.0 collective-permute-done.9.other_halo
  24.9 0.0 collective-permute-start.2
  24.9 0.0 collective-permute-done.1.swapped
  24.9 0.0 copy-done.2
  24.9 1.0 %spread.4 = (f32[336,128]{1,0:T(8,128)S(1)}, f32[336,128]{1,0:T(8,128)S(1)}, f32[336,128]{1,0:T(8,128)S(1)}, f32[336,128]{1,0:T(8,128)S(1)}) custom-call(s32[8,32]{1,0:T(8,128)S(1)} %copy-done.2, s32[32]{0:T(128)S(1)} %get-tuple-element.42.send, f32[672,128]{1,0:T(8,128)S(1)} %get-tuple-element.54.keep, f32[672,128]{1,0:T(8,128)S(1)} %collective-permute-done.8.halo, ...), custom_call_target="tpu_custom_call" | custom-call | bytes 2064 | tf_op jit(solution)/shard_map/spread/pallas_call | solution.py:209
  26.0 1.2 %collective-permute-start.10 = (f32[336,128]{1,0:T(8,128)S(1)}, f32[336,128]{1,0:T(8,128)S(1)}, u32[]{:S(2)}, u32[]{:S(2)}) collective-permute-start(f32[336,128]{1,0:T(8,128)S(1)} %get-tuple-element.58), channel_id=1, source_target_pairs={{0,1},{1,2},{2,3},{3,0},{4,5},{5,6},{6,7},{7,4},{8,9},{9,10},{10,1... | collective-permute-start | bytes 516104 | tf_op jit(solution)/shard_map/ppermute | solution.py:417
  27.1 0.0 collective-permute-done.15.halo
  27.1 2.6 %collective-permute-start.11 = (f32[336,128]{1,0:T(8,128)S(1)}, f32[336,128]{1,0:T(8,128)S(1)}, u32[]{:S(2)}, u32[]{:S(2)}) collective-permute-start(f32[336,128]{1,0:T(8,128)S(1)} %get-tuple-element.59), channel_id=1, source_target_pairs={{0,2},{1,3},{2,0},{3,1},{4,6},{5,7},{6,4},{7,5},{8,10},{9,11},{10,... | collective-permute-start | bytes 516104 | tf_op jit(solution)/shard_map/ppermute | solution.py:417
  29.7 0.0 collective-permute-done.16.other_halo
  29.7 1.9 %collective-permute-start.12 = (f32[336,128]{1,0:T(8,128)S(1)}, f32[336,128]{1,0:T(8,128)S(1)}, u32[]{:S(2)}, u32[]{:S(2)}) collective-permute-start(f32[336,128]{1,0:T(8,128)S(1)} %get-tuple-element.60), channel_id=1, source_target_pairs={{0,3},{1,0},{2,1},{3,2},{4,7},{5,4},{6,5},{7,6},{8,11},{9,8},{10,9... | collective-permute-start | bytes 516104 | tf_op jit(solution)/shard_map/ppermute | solution.py:417
  31.6 1.0 %spread.5 = (f32[336,128]{1,0:T(8,128)S(1)}, f32[336,128]{1,0:T(8,128)S(1)}, f32[336,128]{1,0:T(8,128)S(1)}, f32[336,128]{1,0:T(8,128)S(1)}) custom-call(s32[8,32]{1,0:T(8,128)S(1)} %copy-done.2, s32[32]{0:T(128)S(1)} %get-tuple-element.42.send, f32[672,128]{1,0:T(8,128)S(1)} %get-tuple-element.63.keep, f32[672,128]{1,0:T(8,128)S(1)} %collective-permute-done.15.halo, ...), custom_call_target="tpu_custom_call" | custom-call | bytes 2064 | tf_op jit(solution)/shard_map/spread/pallas_call | solution.py:209
  32.7 0.0 collective-permute-done.10.refs_1_
  32.7 0.1 collective-permute-start.17
  32.8 1.8 %collective-permute-done.11.refs_2_ = f32[336,128]{1,0:T(8,128)S(1)} collective-permute-done((f32[336,128]{1,0:T(8,128)S(1)}, f32[336,128]{1,0:T(8,128)S(1)}, u32[]{:S(2)}, u32[]{:S(2)}) %collective-permute-start.11) | collective-permute-done | bytes 172064 | tf_op jit(solution)/shard_map/ppermute | solution.py:417
  34.5 2.1 %collective-permute-start.18 = (f32[336,128]{1,0:T(8,128)S(1)}, f32[336,128]{1,0:T(8,128)S(1)}, u32[]{:S(2)}, u32[]{:S(2)}) collective-permute-start(f32[336,128]{1,0:T(8,128)S(1)} %get-tuple-element.68), channel_id=1, source_target_pairs={{0,2},{1,3},{2,0},{3,1},{4,6},{5,7},{6,4},{7,5},{8,10},{9,11},{10,... | collective-permute-start | bytes 516104 | tf_op jit(solution)/shard_map/ppermute | solution.py:417
  36.6 0.0 collective-permute-done.12.refs_3_
  36.6 0.6 collect.4
  37.2 4.4 %collective-permute-start.13 = (f32[672,128]{1,0:T(8,128)S(1)}, f32[672,128]{1,0:T(8,128)S(1)}, u32[]{:S(2)}, u32[]{:S(2)}) collective-permute-start(f32[672,128]{1,0:T(8,128)S(1)} %get-tuple-element.61.refs_1_), channel_id=1, source_target_pairs={{4,8},{12,16},{20,24},{28,32},{36,40},{44,48},{52,56},{60,64},{68,... | collective-permute-start | bytes 1032200 | tf_op jit(solution)/shard_map/ppermute | solution.py:420
  41.6 0.0 collective-permute-done.halo
  41.6 0.4 collective-permute-start.19
  42.1 0.0 collective-permute-done.2.other_halo
  42.1 1.0 %spread.3 = (f32[336,128]{1,0:T(8,128)S(1)}, f32[336,128]{1,0:T(8,128)S(1)}, f32[336,128]{1,0:T(8,128)S(1)}, f32[336,128]{1,0:T(8,128)S(1)}) custom-call(s32[8,32]{1,0:T(8,128)S(1)} %copy-done.2, s32[32]{0:T(128)S(1)} %get-tuple-element.42.send, f32[672,128]{1,0:T(8,128)S(1)} %get-tuple-element.44.keep, f32[672,128]{1,0:T(8,128)S(1)} %collective-permute-done.halo, ...), custom_call_target="tpu_custom_call" | custom-call | bytes 2064 | tf_op jit(solution)/shard_map/spread/pallas_call | solution.py:209
  43.1 1.1 %collective-permute-start.3 = (f32[336,128]{1,0:T(8,128)S(1)}, f32[336,128]{1,0:T(8,128)S(1)}, u32[]{:S(2)}, u32[]{:S(2)}) collective-permute-start(f32[336,128]{1,0:T(8,128)S(1)} %get-tuple-element.49), channel_id=1, source_target_pairs={{0,1},{1,2},{2,3},{3,0},{4,5},{5,6},{6,7},{7,4},{8,9},{9,10},{10,1... | collective-permute-start | bytes 516104 | tf_op jit(solution)/shard_map/ppermute | solution.py:417
  44.2 0.0 collective-permute-done.17.refs_1_
  44.2 3.1 %collective-permute-start.4 = (f32[336,128]{1,0:T(8,128)S(1)}, f32[336,128]{1,0:T(8,128)S(1)}, u32[]{:S(2)}, u32[]{:S(2)}) collective-permute-start(f32[336,128]{1,0:T(8,128)S(1)} %get-tuple-element.50), channel_id=1, source_target_pairs={{0,2},{1,3},{2,0},{3,1},{4,6},{5,7},{6,4},{7,5},{8,10},{9,11},{10,... | collective-permute-start | bytes 516104 | tf_op jit(solution)/shard_map/ppermute | solution.py:417
  47.3 0.0 collective-permute-done.18.refs_2_
  47.3 0.6 collective-permute-start.5
  47.9 0.0 collective-permute-done.19.refs_3_
  47.9 5.2 %collective-permute-start.14 = (f32[672,128]{1,0:T(8,128)S(1)}, f32[672,128]{1,0:T(8,128)S(1)}, u32[]{:S(2)}, u32[]{:S(2)}) collective-permute-start(f32[672,128]{1,0:T(8,128)S(1)} %get-tuple-element.62.refs_2_), channel_id=1, source_target_pairs={{0,4},{4,0},{8,12},{12,8},{16,20},{20,16},{24,28},{28,24},{32,36},... | collective-permute-start | bytes 1032200 | tf_op jit(solution)/shard_map/ppermute | solution.py:423
  53.1 0.6 collect.5
  53.7 0.0 collective-permute-done.3.refs_1_
  53.7 2.0 %collective-permute-start.20 = (f32[672,128]{1,0:T(8,128)S(1)}, f32[672,128]{1,0:T(8,128)S(1)}, u32[]{:S(2)}, u32[]{:S(2)}) collective-permute-start(f32[672,128]{1,0:T(8,128)S(1)} %get-tuple-element.70.refs_5_), channel_id=1, source_target_pairs={{4,8},{12,16},{20,24},{28,32},{36,40},{44,48},{52,56},{60,64},{68,... | collective-permute-start | bytes 1032200 | tf_op jit(solution)/shard_map/ppermute | solution.py:420
  55.8 0.0 collective-permute-done.4.refs_2_
  55.8 3.2 %collective-permute-start.21 = (f32[672,128]{1,0:T(8,128)S(1)}, f32[672,128]{1,0:T(8,128)S(1)}, u32[]{:S(2)}, u32[]{:S(2)}) collective-permute-start(f32[672,128]{1,0:T(8,128)S(1)} %get-tuple-element.71.refs_6_), channel_id=1, source_target_pairs={{0,4},{4,0},{8,12},{12,8},{16,20},{20,16},{24,28},{28,24},{32,36},... | collective-permute-start | bytes 1032200 | tf_op jit(solution)/shard_map/ppermute | solution.py:423
  59.0 0.0 collective-permute-done.5.refs_3_
  59.0 1.5 %collect.3 = (f32[672,128]{1,0:T(8,128)}, f32[672,128]{1,0:T(8,128)}) custom-call(s32[32]{0:T(128)S(1)} %get-tuple-element.41.recv, f32[336,128]{1,0:T(8,128)S(1)} %get-tuple-element.48.refs_0_, f32[336,128]{1,0:T(8,128)S(1)} %collective-permute-done.3.refs_1_, f32[336,128]{1,0:T(8,128)S(1)} %collective-permute-done.4.refs_2_, ...), custom_call_target="tpu_custom_call" | custom-call | bytes 1376 | tf_op jit(solution)/shard_map/collect/pallas_call | solution.py:240
  60.5 0.0 collective-permute-start.6
  60.5 0.0 collective-permute-done.13.refs_0_
  60.5 3.3 %collective-permute-start.7 = (f32[672,128]{1,0:T(8,128)}, f32[672,128]{1,0:T(8,128)}, u32[]{:S(2)}, u32[]{:S(2)}) collective-permute-start(f32[672,128]{1,0:T(8,128)} %get-tuple-element.53.refs_2_), channel_id=1, source_target_pairs={{0,4},{4,0},{8,12},{12,8},{16,20},{20,16},{24,28},{28,24},{32,36},... | collective-permute-start | bytes 1032200 | tf_op jit(solution)/shard_map/ppermute | solution.py:423
  64.6 0.1 pad_maximum_fusion.fixes
  64.6 0.0 collective-permute-done.14.refs_3_
  64.6 0.0 collective-permute-done.20.refs_4_
  64.6 0.0 collective-permute-done.21.refs_7_
  64.6 0.0 copy-done
  64.7 0.0 copy-done.3
  64.7 2.9 %moments.1 = (f32[2688,128]{1,0:T(8,128)}, f32[2688,128]{1,0:T(8,128)}, f32[2688,128]{1,0:T(8,128)S(1)}) custom-call(s32[4,64]{1,0:T(4,128)S(1)} %copy-done.3, f32[2]{0:T(128)S(1)} %pad_maximum_fusion.fixes, f32[672,128]{1,0:T(8,128)S(1)} %collective-permute-done.13.refs_0_, f32[672,128]{1,0:T(8,128)S(1)} %get-tuple-element.61.refs_1_, ...), custom_call_target="tpu_custom_call" | custom-call | bytes 9633 | tf_op jit(solution)/shard_map/moments/pallas_call | solution.py:318
  67.5 0.2 collective-permute-done.6.refs_0_
  67.8 0.0 collective-permute-done.7.refs_3_
  67.8 2.6 %weights.1 = f32[2688,128]{1,0:T(8,128)} custom-call(s32[4,64]{1,0:T(4,128)S(1)} %copy-done.3, f32[672,128]{1,0:T(8,128)} %collective-permute-done.6.refs_0_, f32[672,128]{1,0:T(8,128)} %get-tuple-element.52.refs_1_, f32[672,128]{1,0:T(8,128)} %get-tuple-element.53.refs_2_, f32[672,128]{1,0:T(8,128)} %collective-permute-done.7.refs_3_, ...), custom_call_target="tpu_custom_call" | custom-call | bytes 4128 | tf_op jit(solution)/shard_map/weights/pallas_call | solution.py:349
  (4 shorter events, 0.0 us)
Async XLA Ops:
  0.6 0.7 copy-start.1
  3.5 21.4 %collective-permute-start.1 = (f32[2016,128]{1,0:T(8,128)S(1)}, f32[2016,128]{1,0:T(8,128)S(1)}, u32[]{:S(2)}, u32[]{:S(2)}) collective-permute-start(f32[2016,128]{1,0:T(8,128)S(1)} %get-tuple-element.46), channel_id=1, source_target_pairs={{0,4},{4,0},{8,12},{12,8},{16,20},{20,16},{24,28},{28,24},{32,36},... | collective-permute-start | bytes 3096584 | tf_op jit(solution)/shard_map/ppermute | solution.py:403
  6.8 12.9 %collective-permute-start.8 = (f32[672,128]{1,0:T(8,128)S(1)}, f32[672,128]{1,0:T(8,128)S(1)}, u32[]{:S(2)}, u32[]{:S(2)}) collective-permute-start(f32[672,128]{1,0:T(8,128)S(1)} %get-tuple-element.55), channel_id=1, source_target_pairs={{0,8},{8,16},{16,24},{24,32},{32,40},{40,48},{48,56},{56,64},{64,7... | collective-permute-start | bytes 1032200 | tf_op jit(solution)/shard_map/ppermute | solution.py:407
  13.1 4.3 %copy-start.4 = (s32[112]{0:T(128)S(1)}, s32[112]{0:T(128)}, u32[]{:S(2)}) copy-start(s32[112]{0:T(128)} %old_heads) | copy-start | bytes 1348
  13.1 4.3 %copy-start.5 = (s32[112]{0:T(128)S(1)}, s32[112]{0:T(128)}, u32[]{:S(2)}) copy-start(s32[112]{0:T(128)} %new_heads.1) | copy-start | bytes 1348
  13.1 11.8 %copy-start.2 = (s32[8,32]{1,0:T(8,128)S(1)}, s32[8,32]{1,0:T(8,128)}, u32[]{:S(2)}) copy-start(s32[8,32]{1,0:T(8,128)} %offsets.10) | copy-start | bytes 3076
  13.1 11.8 %collective-permute-start.9 = (f32[672,128]{1,0:T(8,128)S(1)}, f32[672,128]{1,0:T(8,128)S(1)}, u32[]{:S(2)}, u32[]{:S(2)}) collective-permute-start(f32[672,128]{1,0:T(8,128)S(1)} %get-tuple-element.56), channel_id=1, source_target_pairs={{4,8},{12,16},{20,24},{28,32},{36,40},{44,48},{52,56},{60,64},{68,... | collective-permute-start | bytes 1032200 | tf_op jit(solution)/shard_map/ppermute | solution.py:408
  15.5 11.7 %collective-permute-start.15 = (f32[672,128]{1,0:T(8,128)S(1)}, f32[672,128]{1,0:T(8,128)S(1)}, u32[]{:S(2)}, u32[]{:S(2)}) collective-permute-start(f32[672,128]{1,0:T(8,128)S(1)} %get-tuple-element.64), channel_id=1, source_target_pairs={{0,8},{8,16},{16,24},{24,32},{32,40},{40,48},{48,56},{56,64},{64,7... | collective-permute-start | bytes 1032200 | tf_op jit(solution)/shard_map/ppermute | solution.py:407
  16.2 13.5 %collective-permute-start.16 = (f32[672,128]{1,0:T(8,128)S(1)}, f32[672,128]{1,0:T(8,128)S(1)}, u32[]{:S(2)}, u32[]{:S(2)}) collective-permute-start(f32[672,128]{1,0:T(8,128)S(1)} %get-tuple-element.65), channel_id=1, source_target_pairs={{4,8},{12,16},{20,24},{28,32},{36,40},{44,48},{52,56},{60,64},{68,... | collective-permute-start | bytes 1032200 | tf_op jit(solution)/shard_map/ppermute | solution.py:408
  19.7 21.9 %collective-permute-start = (f32[672,128]{1,0:T(8,128)S(1)}, f32[672,128]{1,0:T(8,128)S(1)}, u32[]{:S(2)}, u32[]{:S(2)}) collective-permute-start(f32[672,128]{1,0:T(8,128)S(1)} %get-tuple-element.45), channel_id=1, source_target_pairs={{0,8},{8,16},{16,24},{24,32},{32,40},{40,48},{48,56},{56,64},{64,7... | collective-permute-start | bytes 1032200 | tf_op jit(solution)/shard_map/ppermute | solution.py:407
  24.9 17.1 %collective-permute-start.2 = (f32[672,128]{1,0:T(8,128)S(1)}, f32[672,128]{1,0:T(8,128)S(1)}, u32[]{:S(2)}, u32[]{:S(2)}) collective-permute-start(f32[672,128]{1,0:T(8,128)S(1)} %get-tuple-element.47), channel_id=1, source_target_pairs={{4,8},{12,16},{20,24},{28,32},{36,40},{44,48},{52,56},{60,64},{68,... | collective-permute-start | bytes 1032200 | tf_op jit(solution)/shard_map/ppermute | solution.py:408
  26.0 6.7 %collective-permute-start.10 = (f32[336,128]{1,0:T(8,128)S(1)}, f32[336,128]{1,0:T(8,128)S(1)}, u32[]{:S(2)}, u32[]{:S(2)}) collective-permute-start(f32[336,128]{1,0:T(8,128)S(1)} %get-tuple-element.58), channel_id=1, source_target_pairs={{0,1},{1,2},{2,3},{3,0},{4,5},{5,6},{6,7},{7,4},{8,9},{9,10},{10,1... | collective-permute-start | bytes 516104 | tf_op jit(solution)/shard_map/ppermute | solution.py:417
  27.1 7.4 %collective-permute-start.11 = (f32[336,128]{1,0:T(8,128)S(1)}, f32[336,128]{1,0:T(8,128)S(1)}, u32[]{:S(2)}, u32[]{:S(2)}) collective-permute-start(f32[336,128]{1,0:T(8,128)S(1)} %get-tuple-element.59), channel_id=1, source_target_pairs={{0,2},{1,3},{2,0},{3,1},{4,6},{5,7},{6,4},{7,5},{8,10},{9,11},{10,... | collective-permute-start | bytes 516104 | tf_op jit(solution)/shard_map/ppermute | solution.py:417
  29.7 6.9 %collective-permute-start.12 = (f32[336,128]{1,0:T(8,128)S(1)}, f32[336,128]{1,0:T(8,128)S(1)}, u32[]{:S(2)}, u32[]{:S(2)}) collective-permute-start(f32[336,128]{1,0:T(8,128)S(1)} %get-tuple-element.60), channel_id=1, source_target_pairs={{0,3},{1,0},{2,1},{3,2},{4,7},{5,4},{6,5},{7,6},{8,11},{9,8},{10,9... | collective-permute-start | bytes 516104 | tf_op jit(solution)/shard_map/ppermute | solution.py:417
  32.7 11.5 %collective-permute-start.17 = (f32[336,128]{1,0:T(8,128)S(1)}, f32[336,128]{1,0:T(8,128)S(1)}, u32[]{:S(2)}, u32[]{:S(2)}) collective-permute-start(f32[336,128]{1,0:T(8,128)S(1)} %get-tuple-element.67), channel_id=1, source_target_pairs={{0,1},{1,2},{2,3},{3,0},{4,5},{5,6},{6,7},{7,4},{8,9},{9,10},{10,1... | collective-permute-start | bytes 516104 | tf_op jit(solution)/shard_map/ppermute | solution.py:417
  34.5 12.8 %collective-permute-start.18 = (f32[336,128]{1,0:T(8,128)S(1)}, f32[336,128]{1,0:T(8,128)S(1)}, u32[]{:S(2)}, u32[]{:S(2)}) collective-permute-start(f32[336,128]{1,0:T(8,128)S(1)} %get-tuple-element.68), channel_id=1, source_target_pairs={{0,2},{1,3},{2,0},{3,1},{4,6},{5,7},{6,4},{7,5},{8,10},{9,11},{10,... | collective-permute-start | bytes 516104 | tf_op jit(solution)/shard_map/ppermute | solution.py:417
  37.2 23.2 %collective-permute-start.13 = (f32[672,128]{1,0:T(8,128)S(1)}, f32[672,128]{1,0:T(8,128)S(1)}, u32[]{:S(2)}, u32[]{:S(2)}) collective-permute-start(f32[672,128]{1,0:T(8,128)S(1)} %get-tuple-element.61.refs_1_), channel_id=1, source_target_pairs={{4,8},{12,16},{20,24},{28,32},{36,40},{44,48},{52,56},{60,64},{68,... | collective-permute-start | bytes 1032200 | tf_op jit(solution)/shard_map/ppermute | solution.py:420
  41.6 6.3 %collective-permute-start.19 = (f32[336,128]{1,0:T(8,128)S(1)}, f32[336,128]{1,0:T(8,128)S(1)}, u32[]{:S(2)}, u32[]{:S(2)}) collective-permute-start(f32[336,128]{1,0:T(8,128)S(1)} %get-tuple-element.69), channel_id=1, source_target_pairs={{0,3},{1,0},{2,1},{3,2},{4,7},{5,4},{6,5},{7,6},{8,11},{9,8},{10,9... | collective-permute-start | bytes 516104 | tf_op jit(solution)/shard_map/ppermute | solution.py:417
  42.1 22.6 %copy-start = (bf16[1,1,2688,128]{3,2,1,0:T(8,128)(2,1)S(1)}, bf16[1,1,2688,128]{3,2,1,0:T(8,128)(2,1)}, u32[]{:S(2)}) copy-start(bf16[1,1,2688,128]{3,2,1,0:T(8,128)(2,1)} %param.12) | copy-start | bytes 2064388
  42.1 22.6 %copy-start.3 = (s32[4,64]{1,0:T(4,128)S(1)}, s32[4,64]{1,0:T(4,128)}, u32[]{:S(2)}) copy-start(s32[4,64]{1,0:T(4,128)} %offsets.12) | copy-start | bytes 3076
  43.1 10.7 %collective-permute-start.3 = (f32[336,128]{1,0:T(8,128)S(1)}, f32[336,128]{1,0:T(8,128)S(1)}, u32[]{:S(2)}, u32[]{:S(2)}) collective-permute-start(f32[336,128]{1,0:T(8,128)S(1)} %get-tuple-element.49), channel_id=1, source_target_pairs={{0,1},{1,2},{2,3},{3,0},{4,5},{5,6},{6,7},{7,4},{8,9},{9,10},{10,1... | collective-permute-start | bytes 516104 | tf_op jit(solution)/shard_map/ppermute | solution.py:417
  44.2 11.6 %collective-permute-start.4 = (f32[336,128]{1,0:T(8,128)S(1)}, f32[336,128]{1,0:T(8,128)S(1)}, u32[]{:S(2)}, u32[]{:S(2)}) collective-permute-start(f32[336,128]{1,0:T(8,128)S(1)} %get-tuple-element.50), channel_id=1, source_target_pairs={{0,2},{1,3},{2,0},{3,1},{4,6},{5,7},{6,4},{7,5},{8,10},{9,11},{10,... | collective-permute-start | bytes 516104 | tf_op jit(solution)/shard_map/ppermute | solution.py:417
  47.3 11.7 %collective-permute-start.5 = (f32[336,128]{1,0:T(8,128)S(1)}, f32[336,128]{1,0:T(8,128)S(1)}, u32[]{:S(2)}, u32[]{:S(2)}) collective-permute-start(f32[336,128]{1,0:T(8,128)S(1)} %get-tuple-element.51), channel_id=1, source_target_pairs={{0,3},{1,0},{2,1},{3,2},{4,7},{5,4},{6,5},{7,6},{8,11},{9,8},{10,9... | collective-permute-start | bytes 516104 | tf_op jit(solution)/shard_map/ppermute | solution.py:417
  47.9 16.7 %collective-permute-start.14 = (f32[672,128]{1,0:T(8,128)S(1)}, f32[672,128]{1,0:T(8,128)S(1)}, u32[]{:S(2)}, u32[]{:S(2)}) collective-permute-start(f32[672,128]{1,0:T(8,128)S(1)} %get-tuple-element.62.refs_2_), channel_id=1, source_target_pairs={{0,4},{4,0},{8,12},{12,8},{16,20},{20,16},{24,28},{28,24},{32,36},... | collective-permute-start | bytes 1032200 | tf_op jit(solution)/shard_map/ppermute | solution.py:423
  53.7 10.9 %collective-permute-start.20 = (f32[672,128]{1,0:T(8,128)S(1)}, f32[672,128]{1,0:T(8,128)S(1)}, u32[]{:S(2)}, u32[]{:S(2)}) collective-permute-start(f32[672,128]{1,0:T(8,128)S(1)} %get-tuple-element.70.refs_5_), channel_id=1, source_target_pairs={{4,8},{12,16},{20,24},{28,32},{36,40},{44,48},{52,56},{60,64},{68,... | collective-permute-start | bytes 1032200 | tf_op jit(solution)/shard_map/ppermute | solution.py:420
  55.8 8.8 %collective-permute-start.21 = (f32[672,128]{1,0:T(8,128)S(1)}, f32[672,128]{1,0:T(8,128)S(1)}, u32[]{:S(2)}, u32[]{:S(2)}) collective-permute-start(f32[672,128]{1,0:T(8,128)S(1)} %get-tuple-element.71.refs_6_), channel_id=1, source_target_pairs={{0,4},{4,0},{8,12},{12,8},{16,20},{20,16},{24,28},{28,24},{32,36},... | collective-permute-start | bytes 1032200 | tf_op jit(solution)/shard_map/ppermute | solution.py:423
  60.5 7.3 %collective-permute-start.6 = (f32[672,128]{1,0:T(8,128)}, f32[672,128]{1,0:T(8,128)}, u32[]{:S(2)}, u32[]{:S(2)}) collective-permute-start(f32[672,128]{1,0:T(8,128)} %get-tuple-element.52.refs_1_), channel_id=1, source_target_pairs={{4,8},{12,16},{20,24},{28,32},{36,40},{44,48},{52,56},{60,64},{68,... | collective-permute-start | bytes 1032200 | tf_op jit(solution)/shard_map/ppermute | solution.py:420
  60.5 7.3 %collective-permute-start.7 = (f32[672,128]{1,0:T(8,128)}, f32[672,128]{1,0:T(8,128)}, u32[]{:S(2)}, u32[]{:S(2)}) collective-permute-start(f32[672,128]{1,0:T(8,128)} %get-tuple-element.53.refs_2_), channel_id=1, source_target_pairs={{0,4},{4,0},{8,12},{12,8},{16,20},{20,16},{24,28},{28,24},{32,36},... | collective-permute-start | bytes 1032200 | tf_op jit(solution)/shard_map/ppermute | solution.py:423

commit v4 on v3

--- a/solution.py
+++ b/solution.py
@@ -51,6 +51,10 @@
     return pl.CostEstimate(flops=0, bytes_accessed=moved // COST_SCALE, transcendentals=0)
 
 
+def pinned(arrays):
+    return [pltpu.with_memory_space_constraint(x, pltpu.VMEM) for x in arrays]
+
+
 def place():
     dp = lax.axis_index("dp")
     return dp // 2, dp % 2, lax.axis_index("tensor")
@@ -74,7 +78,22 @@
     }
 
 
-def cut_kernel(plan, offsets, *refs):
+def correction(beta, steps):
+    power = lax.fori_loop(0, steps[0], lambda _, value: value * beta, jnp.float32(1.0))
+    return 1.0 / (1.0 - jnp.full((8, LANES), power, jnp.float32))
+
+
+def first_cut_kernel(plan, offsets, steps, *refs):
+    fixes = refs[3 + len(plan)]
+
+    def meanwhile():
+        fixes[0:8, :] = correction(beta_one, steps)
+        fixes[8:16, :] = correction(beta_two, steps)
+
+    cut_kernel(plan, offsets, *refs[: 3 + len(plan)], *refs[4 + len(plan) :], meanwhile=meanwhile)
+
+
+def cut_kernel(plan, offsets, *refs, meanwhile=None):
     outs = refs[3 : 3 + len(plan)]
     wide, sems = refs[3 + len(plan) :]
     firsts = first_slots_of(offsets)
@@ -91,59 +110,56 @@
             )
             copy.start()
             copies.append((copy, out, spot * HALF, HALF + firsts[kind] - begin))
+    if meanwhile is not None:
+        meanwhile()
     for n, (copy, out, to, rest) in enumerate(copies):
         copy.wait()
         out[to : to + HALF, :] = wide[n, pl.ds(rest, HALF), :]
 
 
-def cut(offsets, state, plan, limit, name):
+def cut(offsets, state, plan, limit, steps=None):
     total = sum(len(pieces) for pieces in plan)
-    return pl.pallas_call(
-        functools.partial(cut_kernel, plan),
-        out_shape=tuple(
-            pltpu.VMEM((len(pieces) * HALF, LANES), jnp.float32) for pieces in plan
-        ),
-        in_specs=[SMEM] + [HBM] * 3,
-        out_specs=(VMEM,) * len(plan),
+    scalars = [offsets] if steps is None else [offsets, steps]
+    rows = [len(pieces) * HALF for pieces in plan] + [16] * (len(scalars) - 1)
+    return pl.pallas_call(
+        functools.partial(cut_kernel if steps is None else first_cut_kernel, plan),
+        out_shape=tuple(pltpu.VMEM((count, LANES), jnp.float32) for count in rows),
+        in_specs=[SMEM] * len(scalars) + [HBM] * 3,
+        out_specs=(VMEM,) * len(rows),
         scratch_shapes=[
             pltpu.VMEM((total, HALF + WIDE, LANES), jnp.float32),
             pltpu.SemaphoreType.DMA((total,)),
         ],
         compiler_params=pltpu.CompilerParams(vmem_limit_bytes=limit),
         cost_estimate=cost(total * 2 * HALF * LANES * 4),
-        name=name,
-    )(offsets, *state)
-
-
-def tables_kernel(old_heads, new_heads, send, recv, where, used):
+        name="pack",
+    )(*scalars, *state)
+
+
+def tables_kernel(old_heads, new_heads, send, recv, where):
     column = lax.axis_index("tensor")
-
-    def invert(i, carry):
-        where[old_heads[i]] = i
-        return carry
-
-    lax.fori_loop(0, HEADS, invert, 0, unroll=8)
+    for i in range(0, HEADS, GROUP):
+        heads = [old_heads[i + b] for b in range(GROUP)]
+        for b in range(GROUP):
+            where[heads[b]] = i + b
+
+    def spots(target):
+        heads = [new_heads[target * GROUP + b] for b in range(GROUP)]
+        return [where[head] for head in heads]
+
     for s in range(COLUMNS):
-        target = (column + s) % COLUMNS
-
-        def one(b, found):
-            position = where[new_heads[target * GROUP + b]] - column * GROUP
-            mine = (position >= 0) & (position < GROUP)
-            send[s * 8 + found] = position
-            return found + jnp.where(mine, 1, 0)
-
-        lax.fori_loop(0, GROUP, one, jnp.int32(0), unroll=4)
-        used[s] = 0
-
-    def slot(b, carry):
-        source = where[new_heads[column * GROUP + b]] // GROUP
-        shift = (column - source + COLUMNS) % COLUMNS
-        found = used[shift]
-        recv[shift * 8 + found] = b
-        used[shift] = found + 1
-        return carry
-
-    lax.fori_loop(0, GROUP, slot, 0, unroll=4)
+        found = jnp.int32(s * 8)
+        for spot in spots((column + s) % COLUMNS):
+            position = spot - column * GROUP
+            send[found] = position
+            found += jnp.where((position >= 0) & (position < GROUP), 1, 0)
+    mine = spots(column)
+    for s in range(COLUMNS):
+        begin = (column + COLUMNS - s) % COLUMNS * GROUP
+        found = jnp.int32(s * 8)
+        for b in range(GROUP):
+            recv[found] = b
+            found += jnp.where((mine[b] >= begin) & (mine[b] < begin + GROUP), 1, 0)
 
 
 def tables(old_heads, new_heads):
@@ -153,10 +169,7 @@
         out_shape=(out, out),
         in_specs=[SMEM, SMEM],
         out_specs=(SMEM, SMEM),
-        scratch_shapes=[
-            pltpu.SMEM((HEADS,), jnp.int32),
-            pltpu.SMEM((COLUMNS,), jnp.int32),
-        ],
+        scratch_shapes=[pltpu.SMEM((HEADS,), jnp.int32)],
         compiler_params=params(),
         cost_estimate=cost(4_000_000),
         name="tables",
@@ -214,7 +227,7 @@
         compiler_params=params(),
         cost_estimate=cost(count * 6 * HALF * LANES * 4),
         name="spread",
-    )(offsets, send, keep, halo, swapped, other_halo)
+    )(offsets, send, *pinned([keep, halo, swapped, other_halo]))
 
 
 def collect_kernel(count, recv, *refs):
@@ -245,7 +258,7 @@
         compiler_params=params(),
         cost_estimate=cost(count * 4 * HALF * LANES * 4),
         name="collect",
-    )(recv, *parts)
+    )(recv, *pinned(parts))
 
 
 def window(offsets):
@@ -294,20 +307,22 @@
         copy.wait()
 
 
-def moments_kernel(turns, offsets, fixes, *refs):
-    gradient, first_out, second_out, ratio_out = refs[8:12]
-    first_held, second_held, first_buf, second_buf, sems = refs[12:]
+def moments_kernel(turns, offsets, *refs):
+    fixes, gradient, first_out, second_out, ratio_out = refs[8:13]
+    first_held, second_held, first_buf, second_buf, sems = refs[13:]
     begin, length = window(offsets)
     load_pieces(refs[:4], turns[0], first_held)
     load_pieces(refs[4:8], turns[1], second_held)
+
+    fix_one, fix_two = fixes[0:1, :], fixes[8:9, :]
 
     def compute(row):
         rows = pl.ds(begin + row, TILE)
         grad = gradient[pl.ds(row, TILE), :].astype(jnp.float32)
         new_first = beta_one * first_held[rows, :] + (1.0 - beta_one) * grad
         new_second = beta_two * second_held[rows, :] + (1.0 - beta_two) * grad * grad
-        root = jnp.sqrt(new_second * fixes[1]) + epsilon
-        ratio_out[pl.ds(row, TILE), :] = new_first * fixes[0] / root
+        root = jnp.sqrt(new_second * fix_two) + epsilon
+        ratio_out[pl.ds(row, TILE), :] = new_first * fix_one / root
         return new_first, new_second
 
     chunked(length, compute, (first_out, second_out), (first_buf, second_buf), sems)
@@ -318,7 +333,7 @@
     return pl.pallas_call(
         functools.partial(moments_kernel, turns),
         out_shape=(out,) * 3,
-        in_specs=[SMEM, SMEM] + [VMEM] * 9,
+        in_specs=[SMEM] + [VMEM] * 10,
         out_specs=(ANY, ANY, VMEM),
         scratch_shapes=[
             pltpu.VMEM((E_ROWS, LANES), jnp.float32),
@@ -330,7 +345,7 @@
         compiler_params=params(),
         cost_estimate=cost(7 * CAP * LANES * 4),
         name="moments",
-    )(offsets, fixes, *pieces, gradient)
+    )(offsets, *pinned(pieces + [fixes]), gradient)
 
 
 def weights_kernel(turn, offsets, *refs):
@@ -359,7 +374,7 @@
         compiler_params=params(),
         cost_estimate=cost(3 * CAP * LANES * 4),
         name="weights",
-    )(offsets, *pieces, ratio)
+    )(offsets, *pinned(pieces + [ratio]))
 
 
 def routes():
@@ -396,10 +411,11 @@
     plan = (swap_plan if SWAP_FIRST else []) + halos(GROUPS[:1])
     rest = ([] if SWAP_FIRST else swap_plan) + halos(GROUPS[1:])
     rest += [tuple((m, "keep") for m in g) for g in GROUPS]
-    near = list(cut(old_offsets, state, plan, FIRST_LIMIT, "pack"))
+    far_offsets = pltpu.with_memory_space_constraint(old_offsets, pltpu.HBM)
+    *near, fixes = cut(far_offsets, state, plan, FIRST_LIMIT, step_count.reshape(1))
     near[0], later_offsets, old_heads = lax.optimization_barrier((near[0], old_offsets, old_heads))
     send, recv = tables(old_heads, new_heads)
-    far = list(cut(later_offsets, state, rest, LIMIT, "pack"))
+    far = list(cut(later_offsets, state, rest, LIMIT))
     swapped = lax.ppermute((near if SWAP_FIRST else far).pop(0), "dp", swap_route)
     halves = near + far
     moved = [
@@ -424,13 +440,6 @@
         ]
         for turn, m in enumerate(members):
             pieces[m], turns[m] = arrived, turn
-    step_float = step_count.astype(jnp.float32)
-    fixes = jnp.stack(
-        [
-            1.0 / (1.0 - jnp.power(jnp.float32(beta_one), step_float)),
-            1.0 / (1.0 - jnp.power(jnp.float32(beta_two), step_float)),
-        ]
-    )
     first, second, ratio = moments(
         (turns[1], turns[2]), new_offsets, fixes, pieces[1] + pieces[2], gradient[0, 0]
     )

time: 71.1 us -> 70.1 us (0.986)
  Pallas kernels: 18 us -> 16.3 us
  waiting for transfers between devices: 2.07 us -> 3.06 us
    ppermute x3, waiting for transfers between devices: 0.22 us -> 1.23 us  [shards(): lax.ppermute(outer, 'dp', other_route)]
    ppermute x3, starting transfers between devices: 11.6 us -> 10.7 us  [shards(): lax.ppermute(inner, 'dp', swap_route)]
    pallas_call x3, Pallas kernels: 2.67 us -> 1.81 us  [collect(): pl.pallas_call(functools.partial(collect_kernel, count), out_shape=(out,...]
    ppermute x3, starting transfers between devices: 6.43 us -> 7.21 us  [shards(): lax.ppermute(outer, 'dp', other_route)]
    pallas_call x1, Pallas kernels: 2.63 us -> 1.91 us  [weights(): pl.pallas_call(functools.partial(weights_kernel, turn), out_shape=jax.Sha...]
  transfers between devices with their start and end apart: 22 -> 22, of which waited for: 2 -> 3; matrix products, arithmetic and copies ran while one was open for 0% -> 0% of each run, Pallas kernels for 19% -> 17%
where the time goes in v4:
time: 70.1 us; the launch traced here: 69.2 us
  starting transfers between devices  48.2 us (69%)
  Pallas kernels  16.3 us (23%)
  waiting for transfers between devices  3.06 us (4%)
  between operations  1.6 us (2%)
    ppermute x9, starting transfers between devices, shards(): lax.ppermute(parts[k], 'tensor', shift[k])  13.6 us
    ppermute x3, starting transfers between devices, shards(): lax.ppermute(halves[2 * g], 'dp', own_route)  12.4 us
    ppermute x3, starting transfers between devices, shards(): lax.ppermute(inner, 'dp', swap_route)  10.7 us
    ppermute x3, starting transfers between devices, shards(): lax.ppermute(outer, 'dp', other_route)  7.21 us
    pallas_call x2, Pallas kernels, cut(): pl.pallas_call(functools.partial(cut_kernel if steps is None else first_c...  4.76 us
    ppermute x1, starting transfers between devices, shards(): lax.ppermute((near if SWAP_FIRST else far).pop(0), 'dp', swap_route)  3.25 us
    pallas_call x3, Pallas kernels, spread(): pl.pallas_call(functools.partial(spread_kernel, turn, count), out_shape=(...  3.03 us
    pallas_call x1, Pallas kernels, moments(): pl.pallas_call(functools.partial(moments_kernel, turns), out_shape=(out,)...  2.73 us
  transfers between devices with their start and end apart: 22, of which 3 were waited for; matrix products, arithmetic and copies ran while one was open for 0% of the time, Pallas kernels for 17%

profile of v4, /device:TPU:1, one launch (start us, length us, event | category | flops | bytes accessed | tf_op | source)
XLA Modules:
  0.0 69.2 jit_solution(11359508552870142114)
XLA Ops:
  1.3 0.0 copy-start.1
  1.3 2.4 %pack.2 = (f32[2016,128]{1,0:T(8,128)S(1)}, f32[672,128]{1,0:T(8,128)S(1)}, f32[672,128]{1,0:T(8,128)S(1)}, f32[16,128]{1,0:T(8,128)S(1)}) custom-call(s32[8,32]{1,0:T(8,128)} %offsets.10, s32[1]{0:T(128)} %bitcast.8.steps, f32[2688,128]{1,0:T(8,128)} %bitcast.10, f32[2688,128]{1,0:T(8,128)} %bitcast.12, f32[2688,128]{1,0:T(8,128)} %bitcast.14), custom_call_target="tpu_custom_call" | custom-call | bytes 3440 | tf_op jit(solution)/shard_map/pack/pallas_call | solution.py:124
  3.7 3.3 %collective-permute-start.1 = (f32[2016,128]{1,0:T(8,128)S(1)}, f32[2016,128]{1,0:T(8,128)S(1)}, u32[]{:S(2)}, u32[]{:S(2)}) collective-permute-start(f32[2016,128]{1,0:T(8,128)S(1)} %get-tuple-element.47), channel_id=1, source_target_pairs={{0,4},{4,0},{8,12},{12,8},{16,20},{20,16},{24,28},{28,24},{32,36},... | collective-permute-start | bytes 3096584 | tf_op jit(solution)/shard_map/ppermute | solution.py:419
  7.0 6.3 %collective-permute-start.8 = (f32[672,128]{1,0:T(8,128)S(1)}, f32[672,128]{1,0:T(8,128)S(1)}, u32[]{:S(2)}, u32[]{:S(2)}) collective-permute-start(f32[672,128]{1,0:T(8,128)S(1)} %get-tuple-element.56), channel_id=1, source_target_pairs={{0,8},{8,16},{16,24},{24,32},{32,40},{40,48},{48,56},{56,64},{64,7... | collective-permute-start | bytes 1032200 | tf_op jit(solution)/shard_map/ppermute | solution.py:423
  13.3 0.0 copy-start.3
  13.3 0.0 copy-start.4
  13.3 0.0 collective-permute-start.9
  13.3 0.0 copy-done.1
  13.3 2.3 %pack.3 = (f32[672,128]{1,0:T(8,128)S(1)}, f32[672,128]{1,0:T(8,128)S(1)}, f32[672,128]{1,0:T(8,128)S(1)}, f32[672,128]{1,0:T(8,128)S(1)}, f32[672,128]{1,0:T(8,...) custom-call(s32[8,32]{1,0:T(8,128)S(1)} %copy-done.1, f32[2688,128]{1,0:T(8,128)} %bitcast.11, ...), custom_call_target="tpu_custom_call" | custom-call | bytes 4816 | tf_op jit(solution)/shard_map/pack/pallas_call | solution.py:124
  15.6 0.9 %collective-permute-start.15 = (f32[672,128]{1,0:T(8,128)S(1)}, f32[672,128]{1,0:T(8,128)S(1)}, u32[]{:S(2)}, u32[]{:S(2)}) collective-permute-start(f32[672,128]{1,0:T(8,128)S(1)} %get-tuple-element.65), channel_id=1, source_target_pairs={{0,8},{8,16},{16,24},{24,32},{32,40},{40,48},{48,56},{56,64},{64,7... | collective-permute-start | bytes 1032200 | tf_op jit(solution)/shard_map/ppermute | solution.py:423
  16.5 1.0 %collective-permute-start.16 = (f32[672,128]{1,0:T(8,128)S(1)}, f32[672,128]{1,0:T(8,128)S(1)}, u32[]{:S(2)}, u32[]{:S(2)}) collective-permute-start(f32[672,128]{1,0:T(8,128)S(1)} %get-tuple-element.66), channel_id=1, source_target_pairs={{4,8},{12,16},{20,24},{28,32},{36,40},{44,48},{52,56},{60,64},{68,... | collective-permute-start | bytes 1032200 | tf_op jit(solution)/shard_map/ppermute | solution.py:424
  17.5 0.0 copy-done.3
  17.5 0.0 copy-done.4
  17.5 2.1 %tables.1 = (s32[32]{0:T(128)S(1)}, s32[32]{0:T(128)S(1)}) custom-call(s32[112]{0:T(128)S(1)} %copy-done.3, s32[112]{0:T(128)S(1)} %copy-done.4), custom_call_target="tpu_custom_call" | custom-call | bytes 4000 | tf_op jit(solution)/shard_map/tables/pallas_call | solution.py:167
  19.6 0.1 collective-permute-done.8.halo
  19.7 5.2 %collective-permute-start = (f32[672,128]{1,0:T(8,128)S(1)}, f32[672,128]{1,0:T(8,128)S(1)}, u32[]{:S(2)}, u32[]{:S(2)}) collective-permute-start(f32[672,128]{1,0:T(8,128)S(1)} %get-tuple-element.46), channel_id=1, source_target_pairs={{0,8},{8,16},{16,24},{24,32},{32,40},{40,48},{48,56},{56,64},{64,7... | collective-permute-start | bytes 1032200 | tf_op jit(solution)/shard_map/ppermute | solution.py:423
  25.0 0.0 collective-permute-done.9.other_halo
  25.0 0.0 collective-permute-start.2
  25.0 0.0 collective-permute-done.1.swapped
  25.0 1.0 %spread.4 = (f32[336,128]{1,0:T(8,128)S(1)}, f32[336,128]{1,0:T(8,128)S(1)}, f32[336,128]{1,0:T(8,128)S(1)}, f32[336,128]{1,0:T(8,128)S(1)}) custom-call(s32[8,32]{1,0:T(8,128)S(1)} %copy-done.1, s32[32]{0:T(128)S(1)} %get-tuple-element.43.send, f32[672,128]{1,0:T(8,128)S(1)} %get-tuple-element.55.keep, f32[672,128]{1,0:T(8,128)S(1)} %collective-permute-done.8.halo, ...), custom_call_target="tpu_custom_call" | custom-call | bytes 2064 | tf_op jit(solution)/shard_map/spread/pallas_call | solution.py:222
  26.0 1.4 %collective-permute-start.10 = (f32[336,128]{1,0:T(8,128)S(1)}, f32[336,128]{1,0:T(8,128)S(1)}, u32[]{:S(2)}, u32[]{:S(2)}) collective-permute-start(f32[336,128]{1,0:T(8,128)S(1)} %get-tuple-element.59), channel_id=1, source_target_pairs={{0,1},{1,2},{2,3},{3,0},{4,5},{5,6},{6,7},{7,4},{8,9},{9,10},{10,1... | collective-permute-start | bytes 516104 | tf_op jit(solution)/shard_map/ppermute | solution.py:433
  27.3 0.0 collective-permute-done.15.halo
  27.3 2.6 %collective-permute-start.11 = (f32[336,128]{1,0:T(8,128)S(1)}, f32[336,128]{1,0:T(8,128)S(1)}, u32[]{:S(2)}, u32[]{:S(2)}) collective-permute-start(f32[336,128]{1,0:T(8,128)S(1)} %get-tuple-element.60), channel_id=1, source_target_pairs={{0,2},{1,3},{2,0},{3,1},{4,6},{5,7},{6,4},{7,5},{8,10},{9,11},{10,... | collective-permute-start | bytes 516104 | tf_op jit(solution)/shard_map/ppermute | solution.py:433
  29.9 0.0 collective-permute-done.16.other_halo
  29.9 2.0 %collective-permute-start.12 = (f32[336,128]{1,0:T(8,128)S(1)}, f32[336,128]{1,0:T(8,128)S(1)}, u32[]{:S(2)}, u32[]{:S(2)}) collective-permute-start(f32[336,128]{1,0:T(8,128)S(1)} %get-tuple-element.61), channel_id=1, source_target_pairs={{0,3},{1,0},{2,1},{3,2},{4,7},{5,4},{6,5},{7,6},{8,11},{9,8},{10,9... | collective-permute-start | bytes 516104 | tf_op jit(solution)/shard_map/ppermute | solution.py:433
  31.9 1.0 %spread.5 = (f32[336,128]{1,0:T(8,128)S(1)}, f32[336,128]{1,0:T(8,128)S(1)}, f32[336,128]{1,0:T(8,128)S(1)}, f32[336,128]{1,0:T(8,128)S(1)}) custom-call(s32[8,32]{1,0:T(8,128)S(1)} %copy-done.1, s32[32]{0:T(128)S(1)} %get-tuple-element.43.send, f32[672,128]{1,0:T(8,128)S(1)} %get-tuple-element.64.keep, f32[672,128]{1,0:T(8,128)S(1)} %collective-permute-done.15.halo, ...), custom_call_target="tpu_custom_call" | custom-call | bytes 2064 | tf_op jit(solution)/shard_map/spread/pallas_call | solution.py:222
  32.9 0.0 collective-permute-done.10.refs_1_
  32.9 0.1 collective-permute-start.17
  33.0 1.7 %collective-permute-done.11.refs_2_ = f32[336,128]{1,0:T(8,128)S(1)} collective-permute-done((f32[336,128]{1,0:T(8,128)S(1)}, f32[336,128]{1,0:T(8,128)S(1)}, u32[]{:S(2)}, u32[]{:S(2)}) %collective-permute-start.11) | collective-permute-done | bytes 172064 | tf_op jit(solution)/shard_map/ppermute | solution.py:433
  34.6 2.2 %collective-permute-start.18 = (f32[336,128]{1,0:T(8,128)S(1)}, f32[336,128]{1,0:T(8,128)S(1)}, u32[]{:S(2)}, u32[]{:S(2)}) collective-permute-start(f32[336,128]{1,0:T(8,128)S(1)} %get-tuple-element.69), channel_id=1, source_target_pairs={{0,2},{1,3},{2,0},{3,1},{4,6},{5,7},{6,4},{7,5},{8,10},{9,11},{10,... | collective-permute-start | bytes 516104 | tf_op jit(solution)/shard_map/ppermute | solution.py:433
  36.8 0.0 collective-permute-done.12.refs_3_
  36.8 0.6 collect.4
  37.4 4.2 %collective-permute-start.13 = (f32[672,128]{1,0:T(8,128)S(1)}, f32[672,128]{1,0:T(8,128)S(1)}, u32[]{:S(2)}, u32[]{:S(2)}) collective-permute-start(f32[672,128]{1,0:T(8,128)S(1)} %get-tuple-element.62.refs_1_), channel_id=1, source_target_pairs={{4,8},{12,16},{20,24},{28,32},{36,40},{44,48},{52,56},{60,64},{68,... | collective-permute-start | bytes 1032200 | tf_op jit(solution)/shard_map/ppermute | solution.py:436
  41.6 0.0 collective-permute-done.halo
  41.7 0.6 collective-permute-start.19
  42.3 0.0 collective-permute-done.2.other_halo
  42.3 0.0 copy-start
  42.3 1.0 %spread.3 = (f32[336,128]{1,0:T(8,128)S(1)}, f32[336,128]{1,0:T(8,128)S(1)}, f32[336,128]{1,0:T(8,128)S(1)}, f32[336,128]{1,0:T(8,128)S(1)}) custom-call(s32[8,32]{1,0:T(8,128)S(1)} %copy-done.1, s32[32]{0:T(128)S(1)} %get-tuple-element.43.send, f32[672,128]{1,0:T(8,128)S(1)} %get-tuple-element.45.keep, f32[672,128]{1,0:T(8,128)S(1)} %collective-permute-done.halo, ...), custom_call_target="tpu_custom_call" | custom-call | bytes 2064 | tf_op jit(solution)/shard_map/spread/pallas_call | solution.py:222
  43.3 1.1 %collective-permute-start.3 = (f32[336,128]{1,0:T(8,128)S(1)}, f32[336,128]{1,0:T(8,128)S(1)}, u32[]{:S(2)}, u32[]{:S(2)}) collective-permute-start(f32[336,128]{1,0:T(8,128)S(1)} %get-tuple-element.50), channel_id=1, source_target_pairs={{0,1},{1,2},{2,3},{3,0},{4,5},{5,6},{6,7},{7,4},{8,9},{9,10},{10,1... | collective-permute-start | bytes 516104 | tf_op jit(solution)/shard_map/ppermute | solution.py:433
  44.4 0.0 collective-permute-done.17.refs_1_
  44.4 3.1 %collective-permute-start.4 = (f32[336,128]{1,0:T(8,128)S(1)}, f32[336,128]{1,0:T(8,128)S(1)}, u32[]{:S(2)}, u32[]{:S(2)}) collective-permute-start(f32[336,128]{1,0:T(8,128)S(1)} %get-tuple-element.51), channel_id=1, source_target_pairs={{0,2},{1,3},{2,0},{3,1},{4,6},{5,7},{6,4},{7,5},{8,10},{9,11},{10,... | collective-permute-start | bytes 516104 | tf_op jit(solution)/shard_map/ppermute | solution.py:433
  47.5 0.0 collective-permute-done.18.refs_2_
  47.5 0.6 collective-permute-start.5
  48.2 0.0 collective-permute-done.19.refs_3_
  48.2 4.2 %collective-permute-start.14 = (f32[672,128]{1,0:T(8,128)S(1)}, f32[672,128]{1,0:T(8,128)S(1)}, u32[]{:S(2)}, u32[]{:S(2)}) collective-permute-start(f32[672,128]{1,0:T(8,128)S(1)} %get-tuple-element.63.refs_2_), channel_id=1, source_target_pairs={{0,4},{4,0},{8,12},{12,8},{16,20},{20,16},{24,28},{28,24},{32,36},... | collective-permute-start | bytes 1032200 | tf_op jit(solution)/shard_map/ppermute | solution.py:439
  52.3 0.6 collect.5
  52.9 0.0 collective-permute-done.3.refs_1_
  52.9 2.9 %collective-permute-start.20 = (f32[672,128]{1,0:T(8,128)S(1)}, f32[672,128]{1,0:T(8,128)S(1)}, u32[]{:S(2)}, u32[]{:S(2)}) collective-permute-start(f32[672,128]{1,0:T(8,128)S(1)} %get-tuple-element.71.refs_5_), channel_id=1, source_target_pairs={{4,8},{12,16},{20,24},{28,32},{36,40},{44,48},{52,56},{60,64},{68,... | collective-permute-start | bytes 1032200 | tf_op jit(solution)/shard_map/ppermute | solution.py:436
  55.8 0.0 collective-permute-done.4.refs_2_
  55.9 3.6 %collective-permute-start.21 = (f32[672,128]{1,0:T(8,128)S(1)}, f32[672,128]{1,0:T(8,128)S(1)}, u32[]{:S(2)}, u32[]{:S(2)}) collective-permute-start(f32[672,128]{1,0:T(8,128)S(1)} %get-tuple-element.72.refs_6_), channel_id=1, source_target_pairs={{0,4},{4,0},{8,12},{12,8},{16,20},{20,16},{24,28},{28,24},{32,36},... | collective-permute-start | bytes 1032200 | tf_op jit(solution)/shard_map/ppermute | solution.py:439
  59.5 0.0 collective-permute-done.5.refs_3_
  59.5 0.6 collect.3
  60.1 0.1 collective-permute-start.6
  60.2 0.0 collective-permute-done.13.refs_0_
  60.2 3.0 %collective-permute-start.7 = (f32[672,128]{1,0:T(8,128)S(1)}, f32[672,128]{1,0:T(8,128)S(1)}, u32[]{:S(2)}, u32[]{:S(2)}) collective-permute-start(f32[672,128]{1,0:T(8,128)S(1)} %get-tuple-element.54.refs_2_), channel_id=1, source_target_pairs={{0,4},{4,0},{8,12},{12,8},{16,20},{20,16},{24,28},{28,24},{32,36},... | collective-permute-start | bytes 1032200 | tf_op jit(solution)/shard_map/ppermute | solution.py:439
  63.2 0.0 collective-permute-done.14.refs_3_
  63.2 0.0 collective-permute-done.20.refs_4_
  63.2 0.0 collective-permute-done.21.refs_7_
  63.2 0.0 copy-done
  63.2 0.0 copy-done.2
  63.2 2.7 %moments.1 = (f32[2688,128]{1,0:T(8,128)}, f32[2688,128]{1,0:T(8,128)}, f32[2688,128]{1,0:T(8,128)S(1)}) custom-call(s32[4,64]{1,0:T(4,128)S(1)} %copy-done.2, f32[672,128]{1,0:T(8,128)S(1)} %collective-permute-done.13.refs_0_, f32[672,128]{1,0:T(8,128)S(1)} %get-tuple-element.62.refs_1_, f32[672,128]{1,0:T(8,128)S(1)} %get-tuple-element.63.refs_2_, ...), custom_call_target="tpu_custom_call" | custom-call | bytes 9633 | tf_op jit(solution)/shard_map/moments/pallas_call | solution.py:333
  65.9 1.2 %collective-permute-done.6.refs_0_ = f32[672,128]{1,0:T(8,128)S(1)} collective-permute-done((f32[672,128]{1,0:T(8,128)S(1)}, f32[672,128]{1,0:T(8,128)S(1)}, u32[]{:S(2)}, u32[]{:S(2)}) %collective-permute-start.6) | collective-permute-done | bytes 344096 | tf_op jit(solution)/shard_map/ppermute | solution.py:436
  67.2 0.0 collective-permute-done.7.refs_3_
  67.2 1.9 %weights.1 = f32[2688,128]{1,0:T(8,128)} custom-call(s32[4,64]{1,0:T(4,128)S(1)} %copy-done.2, f32[672,128]{1,0:T(8,128)S(1)} %collective-permute-done.6.refs_0_, f32[672,128]{1,0:T(8,128)S(1)} %get-tuple-element.53.refs_1_, f32[672,128]{1,0:T(8,128)S(1)} %get-tuple-element.54.refs_2_, f32[672,128]{1,0:T(8,128)S(1)} %collective-permute-done.7.refs_3_, ...), custom_call_target="tpu_custom_call" | custom-call | bytes 4128 | tf_op jit(solution)/shard_map/weights/pallas_call | solution.py:364
  (1 shorter events, 0.0 us)
Async XLA Ops:
  1.3 12.0 %copy-start.1 = (s32[8,32]{1,0:T(8,128)S(1)}, s32[8,32]{1,0:T(8,128)}, u32[]{:S(2)}) copy-start(s32[8,32]{1,0:T(8,128)} %offsets.10) | copy-start | bytes 3076
  3.7 21.2 %collective-permute-start.1 = (f32[2016,128]{1,0:T(8,128)S(1)}, f32[2016,128]{1,0:T(8,128)S(1)}, u32[]{:S(2)}, u32[]{:S(2)}) collective-permute-start(f32[2016,128]{1,0:T(8,128)S(1)} %get-tuple-element.47), channel_id=1, source_target_pairs={{0,4},{4,0},{8,12},{12,8},{16,20},{20,16},{24,28},{28,24},{32,36},... | collective-permute-start | bytes 3096584 | tf_op jit(solution)/shard_map/ppermute | solution.py:419
  7.0 12.8 %collective-permute-start.8 = (f32[672,128]{1,0:T(8,128)S(1)}, f32[672,128]{1,0:T(8,128)S(1)}, u32[]{:S(2)}, u32[]{:S(2)}) collective-permute-start(f32[672,128]{1,0:T(8,128)S(1)} %get-tuple-element.56), channel_id=1, source_target_pairs={{0,8},{8,16},{16,24},{24,32},{32,40},{40,48},{48,56},{56,64},{64,7... | collective-permute-start | bytes 1032200 | tf_op jit(solution)/shard_map/ppermute | solution.py:423
  13.3 4.3 %copy-start.3 = (s32[112]{0:T(128)S(1)}, s32[112]{0:T(128)}, u32[]{:S(2)}) copy-start(s32[112]{0:T(128)} %old_heads) | copy-start | bytes 1348
  13.3 4.3 %copy-start.4 = (s32[112]{0:T(128)S(1)}, s32[112]{0:T(128)}, u32[]{:S(2)}) copy-start(s32[112]{0:T(128)} %new_heads.1) | copy-start | bytes 1348
  13.3 11.7 %collective-permute-start.9 = (f32[672,128]{1,0:T(8,128)S(1)}, f32[672,128]{1,0:T(8,128)S(1)}, u32[]{:S(2)}, u32[]{:S(2)}) collective-permute-start(f32[672,128]{1,0:T(8,128)S(1)} %get-tuple-element.57), channel_id=1, source_target_pairs={{4,8},{12,16},{20,24},{28,32},{36,40},{44,48},{52,56},{60,64},{68,... | collective-permute-start | bytes 1032200 | tf_op jit(solution)/shard_map/ppermute | solution.py:424
  15.6 11.7 %collective-permute-start.15 = (f32[672,128]{1,0:T(8,128)S(1)}, f32[672,128]{1,0:T(8,128)S(1)}, u32[]{:S(2)}, u32[]{:S(2)}) collective-permute-start(f32[672,128]{1,0:T(8,128)S(1)} %get-tuple-element.65), channel_id=1, source_target_pairs={{0,8},{8,16},{16,24},{24,32},{32,40},{40,48},{48,56},{56,64},{64,7... | collective-permute-start | bytes 1032200 | tf_op jit(solution)/shard_map/ppermute | solution.py:423
  16.5 13.4 %collective-permute-start.16 = (f32[672,128]{1,0:T(8,128)S(1)}, f32[672,128]{1,0:T(8,128)S(1)}, u32[]{:S(2)}, u32[]{:S(2)}) collective-permute-start(f32[672,128]{1,0:T(8,128)S(1)} %get-tuple-element.66), channel_id=1, source_target_pairs={{4,8},{12,16},{20,24},{28,32},{36,40},{44,48},{52,56},{60,64},{68,... | collective-permute-start | bytes 1032200 | tf_op jit(solution)/shard_map/ppermute | solution.py:424
  19.7 21.9 %collective-permute-start = (f32[672,128]{1,0:T(8,128)S(1)}, f32[672,128]{1,0:T(8,128)S(1)}, u32[]{:S(2)}, u32[]{:S(2)}) collective-permute-start(f32[672,128]{1,0:T(8,128)S(1)} %get-tuple-element.46), channel_id=1, source_target_pairs={{0,8},{8,16},{16,24},{24,32},{32,40},{40,48},{48,56},{56,64},{64,7... | collective-permute-start | bytes 1032200 | tf_op jit(solution)/shard_map/ppermute | solution.py:423
  25.0 17.3 %collective-permute-start.2 = (f32[672,128]{1,0:T(8,128)S(1)}, f32[672,128]{1,0:T(8,128)S(1)}, u32[]{:S(2)}, u32[]{:S(2)}) collective-permute-start(f32[672,128]{1,0:T(8,128)S(1)} %get-tuple-element.48), channel_id=1, source_target_pairs={{4,8},{12,16},{20,24},{28,32},{36,40},{44,48},{52,56},{60,64},{68,... | collective-permute-start | bytes 1032200 | tf_op jit(solution)/shard_map/ppermute | solution.py:424
  26.0 6.9 %collective-permute-start.10 = (f32[336,128]{1,0:T(8,128)S(1)}, f32[336,128]{1,0:T(8,128)S(1)}, u32[]{:S(2)}, u32[]{:S(2)}) collective-permute-start(f32[336,128]{1,0:T(8,128)S(1)} %get-tuple-element.59), channel_id=1, source_target_pairs={{0,1},{1,2},{2,3},{3,0},{4,5},{5,6},{6,7},{7,4},{8,9},{9,10},{10,1... | collective-permute-start | bytes 516104 | tf_op jit(solution)/shard_map/ppermute | solution.py:433
  27.3 7.3 %collective-permute-start.11 = (f32[336,128]{1,0:T(8,128)S(1)}, f32[336,128]{1,0:T(8,128)S(1)}, u32[]{:S(2)}, u32[]{:S(2)}) collective-permute-start(f32[336,128]{1,0:T(8,128)S(1)} %get-tuple-element.60), channel_id=1, source_target_pairs={{0,2},{1,3},{2,0},{3,1},{4,6},{5,7},{6,4},{7,5},{8,10},{9,11},{10,... | collective-permute-start | bytes 516104 | tf_op jit(solution)/shard_map/ppermute | solution.py:433
  29.9 6.9 %collective-permute-start.12 = (f32[336,128]{1,0:T(8,128)S(1)}, f32[336,128]{1,0:T(8,128)S(1)}, u32[]{:S(2)}, u32[]{:S(2)}) collective-permute-start(f32[336,128]{1,0:T(8,128)S(1)} %get-tuple-element.61), channel_id=1, source_target_pairs={{0,3},{1,0},{2,1},{3,2},{4,7},{5,4},{6,5},{7,6},{8,11},{9,8},{10,9... | collective-permute-start | bytes 516104 | tf_op jit(solution)/shard_map/ppermute | solution.py:433
  32.9 11.5 %collective-permute-start.17 = (f32[336,128]{1,0:T(8,128)S(1)}, f32[336,128]{1,0:T(8,128)S(1)}, u32[]{:S(2)}, u32[]{:S(2)}) collective-permute-start(f32[336,128]{1,0:T(8,128)S(1)} %get-tuple-element.68), channel_id=1, source_target_pairs={{0,1},{1,2},{2,3},{3,0},{4,5},{5,6},{6,7},{7,4},{8,9},{9,10},{10,1... | collective-permute-start | bytes 516104 | tf_op jit(solution)/shard_map/ppermute | solution.py:433
  34.6 12.9 %collective-permute-start.18 = (f32[336,128]{1,0:T(8,128)S(1)}, f32[336,128]{1,0:T(8,128)S(1)}, u32[]{:S(2)}, u32[]{:S(2)}) collective-permute-start(f32[336,128]{1,0:T(8,128)S(1)} %get-tuple-element.69), channel_id=1, source_target_pairs={{0,2},{1,3},{2,0},{3,1},{4,6},{5,7},{6,4},{7,5},{8,10},{9,11},{10,... | collective-permute-start | bytes 516104 | tf_op jit(solution)/shard_map/ppermute | solution.py:433
  37.4 22.8 %collective-permute-start.13 = (f32[672,128]{1,0:T(8,128)S(1)}, f32[672,128]{1,0:T(8,128)S(1)}, u32[]{:S(2)}, u32[]{:S(2)}) collective-permute-start(f32[672,128]{1,0:T(8,128)S(1)} %get-tuple-element.62.refs_1_), channel_id=1, source_target_pairs={{4,8},{12,16},{20,24},{28,32},{36,40},{44,48},{52,56},{60,64},{68,... | collective-permute-start | bytes 1032200 | tf_op jit(solution)/shard_map/ppermute | solution.py:436
  41.7 6.5 %collective-permute-start.19 = (f32[336,128]{1,0:T(8,128)S(1)}, f32[336,128]{1,0:T(8,128)S(1)}, u32[]{:S(2)}, u32[]{:S(2)}) collective-permute-start(f32[336,128]{1,0:T(8,128)S(1)} %get-tuple-element.70), channel_id=1, source_target_pairs={{0,3},{1,0},{2,1},{3,2},{4,7},{5,4},{6,5},{7,6},{8,11},{9,8},{10,9... | collective-permute-start | bytes 516104 | tf_op jit(solution)/shard_map/ppermute | solution.py:433
  42.3 20.9 %copy-start = (bf16[1,1,2688,128]{3,2,1,0:T(8,128)(2,1)S(1)}, bf16[1,1,2688,128]{3,2,1,0:T(8,128)(2,1)}, u32[]{:S(2)}) copy-start(bf16[1,1,2688,128]{3,2,1,0:T(8,128)(2,1)} %param.12) | copy-start | bytes 2064388
  42.3 20.9 %copy-start.2 = (s32[4,64]{1,0:T(4,128)S(1)}, s32[4,64]{1,0:T(4,128)}, u32[]{:S(2)}) copy-start(s32[4,64]{1,0:T(4,128)} %offsets.12) | copy-start | bytes 3076
  43.3 9.6 %collective-permute-start.3 = (f32[336,128]{1,0:T(8,128)S(1)}, f32[336,128]{1,0:T(8,128)S(1)}, u32[]{:S(2)}, u32[]{:S(2)}) collective-permute-start(f32[336,128]{1,0:T(8,128)S(1)} %get-tuple-element.50), channel_id=1, source_target_pairs={{0,1},{1,2},{2,3},{3,0},{4,5},{5,6},{6,7},{7,4},{8,9},{9,10},{10,1... | collective-permute-start | bytes 516104 | tf_op jit(solution)/shard_map/ppermute | solution.py:433
  44.4 11.4 %collective-permute-start.4 = (f32[336,128]{1,0:T(8,128)S(1)}, f32[336,128]{1,0:T(8,128)S(1)}, u32[]{:S(2)}, u32[]{:S(2)}) collective-permute-start(f32[336,128]{1,0:T(8,128)S(1)} %get-tuple-element.51), channel_id=1, source_target_pairs={{0,2},{1,3},{2,0},{3,1},{4,6},{5,7},{6,4},{7,5},{8,10},{9,11},{10,... | collective-permute-start | bytes 516104 | tf_op jit(solution)/shard_map/ppermute | solution.py:433
  47.5 11.9 %collective-permute-start.5 = (f32[336,128]{1,0:T(8,128)S(1)}, f32[336,128]{1,0:T(8,128)S(1)}, u32[]{:S(2)}, u32[]{:S(2)}) collective-permute-start(f32[336,128]{1,0:T(8,128)S(1)} %get-tuple-element.52), channel_id=1, source_target_pairs={{0,3},{1,0},{2,1},{3,2},{4,7},{5,4},{6,5},{7,6},{8,11},{9,8},{10,9... | collective-permute-start | bytes 516104 | tf_op jit(solution)/shard_map/ppermute | solution.py:433
  48.2 15.0 %collective-permute-start.14 = (f32[672,128]{1,0:T(8,128)S(1)}, f32[672,128]{1,0:T(8,128)S(1)}, u32[]{:S(2)}, u32[]{:S(2)}) collective-permute-start(f32[672,128]{1,0:T(8,128)S(1)} %get-tuple-element.63.refs_2_), channel_id=1, source_target_pairs={{0,4},{4,0},{8,12},{12,8},{16,20},{20,16},{24,28},{28,24},{32,36},... | collective-permute-start | bytes 1032200 | tf_op jit(solution)/shard_map/ppermute | solution.py:439
  52.9 10.2 %collective-permute-start.20 = (f32[672,128]{1,0:T(8,128)S(1)}, f32[672,128]{1,0:T(8,128)S(1)}, u32[]{:S(2)}, u32[]{:S(2)}) collective-permute-start(f32[672,128]{1,0:T(8,128)S(1)} %get-tuple-element.71.refs_5_), channel_id=1, source_target_pairs={{4,8},{12,16},{20,24},{28,32},{36,40},{44,48},{52,56},{60,64},{68,... | collective-permute-start | bytes 1032200 | tf_op jit(solution)/shard_map/ppermute | solution.py:436
  55.9 7.3 %collective-permute-start.21 = (f32[672,128]{1,0:T(8,128)S(1)}, f32[672,128]{1,0:T(8,128)S(1)}, u32[]{:S(2)}, u32[]{:S(2)}) collective-permute-start(f32[672,128]{1,0:T(8,128)S(1)} %get-tuple-element.72.refs_6_), channel_id=1, source_target_pairs={{0,4},{4,0},{8,12},{12,8},{16,20},{20,16},{24,28},{28,24},{32,36},... | collective-permute-start | bytes 1032200 | tf_op jit(solution)/shard_map/ppermute | solution.py:439
  60.1 7.1 %collective-permute-start.6 = (f32[672,128]{1,0:T(8,128)S(1)}, f32[672,128]{1,0:T(8,128)S(1)}, u32[]{:S(2)}, u32[]{:S(2)}) collective-permute-start(f32[672,128]{1,0:T(8,128)S(1)} %get-tuple-element.53.refs_1_), channel_id=1, source_target_pairs={{4,8},{12,16},{20,24},{28,32},{36,40},{44,48},{52,56},{60,64},{68,... | collective-permute-start | bytes 1032200 | tf_op jit(solution)/shard_map/ppermute | solution.py:436
  60.2 6.9 %collective-permute-start.7 = (f32[672,128]{1,0:T(8,128)S(1)}, f32[672,128]{1,0:T(8,128)S(1)}, u32[]{:S(2)}, u32[]{:S(2)}) collective-permute-start(f32[672,128]{1,0:T(8,128)S(1)} %get-tuple-element.54.refs_2_), channel_id=1, source_target_pairs={{0,4},{4,0},{8,12},{12,8},{16,20},{20,16},{24,28},{28,24},{32,36},... | collective-permute-start | bytes 1032200 | tf_op jit(solution)/shard_map/ppermute | solution.py:439
